TPU v7x, 32 devices: a whole 2x2x4 slice. The times are simulated.
32 devices in a mesh: groups: 2 (over x), ctx: 8 (over z, y), exp: 2 (over core).
Axes of the slice: x: 2, y: 2, z: 4, core: 2. Of those that a mesh axis runs over, the one named last changes fastest.
Arguments:
- tokens: bfloat16 [4096, 2048], P(('groups', 'ctx', 'exp')), parts along dimension 0, may hold values from -6 to 152
- norm_gain: float32 [2048], replicated, may hold values from 0.1 to 1.9
- router_weight: float32 [2048, 8], replicated, may hold values from -0.125 to 5.1
- routes: int32 [4096, 2], P(('groups', 'ctx', 'exp')), parts along dimension 0, may hold values from 0 to 7, all different within a row; in each aligned block of 128 rows (0 to 127, 128 to 255, ...) at most 40 rows name the same one
- key_weight: bfloat16 [2048, 1024], replicated, may hold values from -0.125 to 0.125
- value_weight: bfloat16 [2048, 1024], replicated, may hold values from -0.125 to 0.125
- query_weight: bfloat16 [8, 2048, 1024], P('ctx'), may hold values from -0.125 to 0.125
- output_weight: bfloat16 [8, 1024, 2048], P('ctx'), may hold values from -3 to 3
Outputs:
- attention_out: bfloat16 [4096, 2048], P(('groups', 'ctx', 'exp')), parts along dimension 0
There are 2 independent parts, one for each index of `groups`. A program takes and returns all parts, laid end to end along the dimension named above; an argument that names none is the same for every part. Nothing has to cross between parts.
Inputs may be any that keep to these rules, and one draw needn't show every extreme that they name: `routes`: each row names 2 different experts; among the 128 rows of one device no expert is named more than 40 times, a bound that some block reaches.
All inputs are finite; a program needn't handle non-finite values.
Results may differ from a plain program's by a relative error of at most 0.006.
The roundings to bfloat16 on the way count: a program that leaves them out, or rounds other values in their place, can miss the bound.
Values may be sent and summed in bfloat16 or wider, within the bound.
No kernel may reach another device: no remote copies, remote signals or barrier semaphores. Data moves between devices by JAX's collectives and lax.ppermute only.
A program may use at most 128 MiB of HBM per device.

v0:
```python
import functools
import math

import jax
import jax.numpy as jnp
from jax import lax
from jax.experimental import pallas as pl
from jax.experimental.pallas import tpu as pltpu
from jax.sharding import PartitionSpec as P

HS = 128
EXPERTS = 8
MOST = 40
SLOTS = 48
MASKED = -1e30
LANES = 128
CODES = 16
TERMS = 2
MIB = 1 << 20
WHOLE = pl.BlockSpec(memory_space=pltpu.VMEM)


def ring_rank(place, count):
    place = lax.rem(place + 2 * count, count)
    return jnp.where(place < count // 2, 2 * place, 2 * (count - 1 - place) + 1)


def ring_place(rank, count):
    return jnp.where(rank % 2 == 0, rank // 2, count - 1 - rank // 2)


def ring_owner(offset):
    count = lax.axis_size("ctx")
    return ring_rank(ring_place(lax.axis_index("ctx"), count) + offset, count)


def norm_kernel(*refs):
    sources, top_ref, bottom_ref, *held, arrivals = refs[:3], *refs[3:]
    copies = [
        pltpu.make_async_copy(source, target, arrivals.at[i])
        for i, (source, target) in enumerate(zip(sources, held))
    ]
    for copy in copies:
        copy.start()
    for copy in copies:
        copy.wait()
    tokens_ref, gain_ref, routes_ref = held
    floats = tokens_ref[...].astype(jnp.float32)
    count, width = floats.shape
    factor = lax.rsqrt(jnp.mean(floats * floats, axis=1, keepdims=True) + 1e-06)
    normed = (floats * factor * gain_ref[...]).astype(jnp.bfloat16)
    expert = lax.broadcasted_iota(jnp.int32, (CODES, count), 0)
    named = (expert == routes_ref[0:1, :]) | (expert == routes_ref[1:2, :])
    before = lax.broadcasted_iota(jnp.int32, (count, count), 0) < lax.broadcasted_iota(
        jnp.int32, (count, count), 1
    )
    rank = jnp.dot(
        named.astype(jnp.bfloat16),
        before.astype(jnp.bfloat16),
        preferred_element_type=jnp.float32,
    )
    codes = jnp.where(named, rank, -1.0).astype(jnp.bfloat16)
    half = count // 2
    for ref, first in ((top_ref, 0), (bottom_ref, half)):
        for c in range(width // LANES):
            ref[pl.ds(c * half, half), :] = normed[
                first : first + half, c * LANES : (c + 1) * LANES
            ]
        ref[pl.ds(width // LANES * half, CODES), :] = codes


def message_rows(ref, half):
    tiles = (ref.shape[0] - CODES) // half
    return jnp.concatenate([ref[pl.ds(c * half, half), :] for c in range(tiles)], axis=1)


def message_codes(ref):
    return ref[pl.ds(ref.shape[0] - CODES, CODES), :].astype(jnp.float32)


def norm_rows(tokens, norm_gain, routes):
    count, width = tokens.shape
    half = jax.ShapeDtypeStruct((width // LANES * (count // 2) + CODES, LANES), jnp.bfloat16)
    operands = (tokens, norm_gain.reshape(1, -1), routes.T)
    return pl.pallas_call(
        norm_kernel,
        in_specs=[pl.BlockSpec(memory_space=pltpu.HBM)] * 3,
        out_specs=[WHOLE] * 2,
        out_shape=[half, half],
        scratch_shapes=[pltpu.VMEM(x.shape, x.dtype) for x in operands]
        + [pltpu.SemaphoreType.DMA((3,))],
        compiler_params=pltpu.CompilerParams(vmem_limit_bytes=60 * MIB),
        name="norm_rows",
    )(*operands)


def column_parts(ref):
    step = min(ref.shape[1], 256)
    return [pl.ds(start, step) for start in range(0, ref.shape[1], step)]


def keys_kernel(half, count, *refs):
    blocks = refs[:count]
    weight_ref, panel_ref, mark_ref = refs[count:]
    rows = jnp.concatenate([message_rows(block, half) for block in blocks], axis=0)
    for cols in column_parts(weight_ref):
        product = jnp.dot(rows, weight_ref[:, cols], preferred_element_type=jnp.float32)
        panel_ref[:, cols] = product.astype(jnp.bfloat16)
    mark_ref[...] = product[:8, :LANES]


def project_keys(half, blocks, key_weight):
    row_count = half * len(blocks)
    width = key_weight.shape[1]
    return pl.pallas_call(
        functools.partial(keys_kernel, half, len(blocks)),
        in_specs=[WHOLE] * (len(blocks) + 1),
        out_specs=[WHOLE] * 2,
        out_shape=[
            jax.ShapeDtypeStruct((row_count, width), jnp.bfloat16),
            jax.ShapeDtypeStruct((8, LANES), jnp.float32),
        ],
        compiler_params=pltpu.CompilerParams(vmem_limit_bytes=12 * MIB),
        name="project_keys",
    )(*blocks, key_weight)


def values_kernel(half, offsets, count, experts, mark_ref, keys_ref, *refs):
    blocks = refs[:count]
    value_ref, panel_ref, picked_ref, pos_ref = refs[count:]
    rows = jnp.concatenate([message_rows(block, half) for block in blocks], axis=0)
    tok_count = 2 * half
    expert = lax.axis_index("ctx") // (lax.axis_size("ctx") // experts)
    number = lax.broadcasted_iota(jnp.int32, (tok_count, LANES), 0).astype(jnp.bfloat16)
    for g, offset in enumerate(offsets):
        part = slice(g * tok_count, (g + 1) * tok_count)
        codes = message_codes(blocks[2 * g])
        mine = lax.broadcasted_iota(jnp.int32, codes.shape, 0) == expert
        slot = jnp.sum(jnp.where(mine, codes, 0.0), axis=0, keepdims=True)
        order = lax.broadcasted_iota(jnp.int32, (SLOTS, tok_count), 0).astype(jnp.float32)
        chosen = (order == slot).astype(jnp.bfloat16)
        picked_ref[g] = jnp.dot(
            chosen, rows[part], preferred_element_type=jnp.float32
        ).astype(jnp.bfloat16)
        start = (ring_owner(offset) * lax.axis_size("exp") + lax.axis_index("exp")) * tok_count
        pos_ref[g] = jnp.dot(
            chosen, number, preferred_element_type=jnp.float32
        ) + start.astype(jnp.float32)
    panel_ref[0] = keys_ref[...]
    for cols in column_parts(value_ref):
        panel_ref[1, :, cols] = jnp.dot(
            rows, value_ref[:, cols], preferred_element_type=jnp.float32
        ).astype(jnp.bfloat16)


def project_values(half, blocks, offsets, mark, keys, value_weight):
    row_count = half * len(blocks)
    model_width, width = value_weight.shape
    owners = len(offsets)
    return pl.pallas_call(
        functools.partial(values_kernel, half, offsets, len(blocks), EXPERTS),
        in_specs=[WHOLE] * (len(blocks) + 3),
        out_specs=[WHOLE] * 3,
        out_shape=[
            jax.ShapeDtypeStruct((2, row_count, width), jnp.bfloat16),
            jax.ShapeDtypeStruct((owners, SLOTS, model_width), jnp.bfloat16),
            jax.ShapeDtypeStruct((owners, SLOTS, LANES), jnp.float32),
        ],
        compiler_params=pltpu.CompilerParams(vmem_limit_bytes=12 * MIB),
        name="project_values",
    )(mark, keys, *blocks, value_weight)


def queries_kernel(*refs):
    count = len(refs) // 2 - 1
    picked, weight_ref, outs = refs[:count], refs[count], refs[count + 2 :]
    rows = jnp.concatenate([ref[g] for ref in picked for g in range(ref.shape[0])], axis=0)
    places = [(ref, g) for ref in outs for g in range(ref.shape[0])]
    for cols in column_parts(weight_ref):
        product = jnp.dot(rows, weight_ref[:, cols], preferred_element_type=jnp.float32)
        for i, (ref, g) in enumerate(places):
            ref[g, :, cols] = product[i * SLOTS : (i + 1) * SLOTS].astype(jnp.bfloat16)


def project_queries(picked, query_slab, next_slab):
    model_width, width = query_slab.shape
    owners = sum(rows.shape[0] for rows in picked)
    held = 4 * model_width * width + owners * SLOTS * (4 * model_width + 4 * width)
    return pl.pallas_call(
        queries_kernel,
        in_specs=[WHOLE] * (len(picked) + 2),
        out_specs=[WHOLE] * len(picked),
        out_shape=[
            jax.ShapeDtypeStruct((rows.shape[0], SLOTS, width), jnp.bfloat16) for rows in picked
        ],
        compiler_params=pltpu.CompilerParams(vmem_limit_bytes=held + 6 * MIB),
        name="project_queries",
    )(*picked, query_slab, next_slab)


def arrange_kernel(plan, *refs):
    count = len(plan)
    own_refs, other_refs, query_refs, pos_refs = (refs[k * count : (k + 1) * count] for k in range(4))
    panel_ref, queries_ref, places_ref = refs[4 * count :]
    exp_count = 2
    side = lax.axis_index("exp")
    tok_count = panel_ref.shape[2]
    for offsets, own_ref, other_ref, query_ref, pos_ref in zip(
        plan, own_refs, other_refs, query_refs, pos_refs
    ):
        for g, offset in enumerate(offsets):
            owner = ring_owner(offset)
            part = pl.ds(g * tok_count, tok_count)
            for which in range(2):
                panel_ref[which, owner * exp_count + side] = own_ref[which, part]
                panel_ref[which, owner * exp_count + 1 - side] = other_ref[which, part]
            queries_ref[owner] = query_ref[g].astype(jnp.float32)[:MOST]
            places_ref[owner] = pos_ref[g, :MOST]


def arrange(owners, plan, own, other, queries, positions):
    width = own[0].shape[2]
    tok_count = own[0].shape[1] // len(plan[0])
    shapes = [
        jax.ShapeDtypeStruct((2, 2 * owners, tok_count, width), jnp.bfloat16),
        jax.ShapeDtypeStruct((owners, MOST, width), jnp.float32),
        jax.ShapeDtypeStruct((owners, MOST, LANES), jnp.float32),
    ]
    operands = (*own, *other, *queries, *positions)
    return pl.pallas_call(
        functools.partial(arrange_kernel, plan),
        in_specs=[WHOLE] * len(operands),
        out_specs=[WHOLE] * 3,
        out_shape=shapes,
        compiler_params=pltpu.CompilerParams(
            vmem_limit_bytes=8 * MIB
        ),
        name="arrange",
    )(*operands)


def attend_kernel(lots, heads, panel_ref, queries_ref, places_ref, weight_ref, *refs):
    outs, (attended, scores, weights) = refs[:-3], refs[-3:]
    first, count = lots
    blocks, tok_count, width = panel_ref.shape[1:]
    rate = math.log2(math.e) / math.sqrt(HS)
    rank = lax.axis_index("ctx")
    tiles = blocks // 4
    tile = 2 * MOST
    parts = 4
    span = blocks * tok_count // parts
    per_span = blocks // parts
    passes = width // (heads * HS)

    def serve(part_id, number, lot, lanes):
        reach = (part_id + 1) * span
        pair = pl.ds(2 * number, 2)
        spots = places_ref[pair].reshape(tile, LANES)
        for h in range(heads):
            held = queries_ref[pair, :, lanes[h]].reshape(tile, HS).astype(jnp.bfloat16)
            for j in range(part_id + 1):
                key_part = panel_ref[0, per_span * j : per_span * (j + 1), :, lanes[h]]
                scores[h, :, pl.ds(j * span, span)] = lax.dot_general(
                    held,
                    key_part.reshape(span, HS),
                    (((1,), (1,)), ((), ())),
                    preferred_element_type=jnp.float32,
                )
        for h in range(heads):
            for sub in range(0, tile, 16):
                rows = pl.ds(sub, 16)
                part = scores[h, rows, pl.ds(0, reach)]
                last = part[:, reach - span :]
                key_index = lax.broadcasted_iota(jnp.int32, last.shape, 1) + (reach - span)
                spot = spots[sub : sub + 16, 0:1]
                last = jnp.where(key_index.astype(jnp.float32) <= spot, last, MASKED)
                if part_id > 0:
                    part = jnp.concatenate([part[:, : reach - span], last], axis=1)
                else:
                    part = last
                peak = jnp.max(part, axis=1, keepdims=True)
                raised = jnp.exp2((part - peak) * rate)
                total = jnp.sum(raised, axis=1, keepdims=True)
                weights[h, rows, pl.ds(0, reach)] = (raised * (1.0 / total)).astype(jnp.bfloat16)
        for h in range(heads):
            total = None
            for j in range(part_id + 1):
                value_part = panel_ref[1, per_span * j : per_span * (j + 1), :, lanes[h]]
                product = jnp.dot(
                    weights[h, :, pl.ds(j * span, span)],
                    value_part.reshape(span, HS),
                    preferred_element_type=jnp.float32,
                )
                total = product if total is None else total + product
            spare = jnp.zeros((SLOTS - MOST, HS), jnp.float32)
            for side in range(2):
                rows = jnp.concatenate([total[side * MOST : (side + 1) * MOST], spare], axis=0)
                attended[2 * lot + (side ^ (rank % 2)), :, lanes[h]] = rows.astype(jnp.bfloat16)

    def one(at, carry):
        lot, now = at // passes, at % passes
        number = (rank // 2) ^ (first + lot)
        lanes = [pl.ds(pl.multiple_of((now * heads + h) * HS, HS), HS) for h in range(heads)]
        for part_id in range(parts):
            pl.when(number // (tiles // parts) == part_id)(
                functools.partial(serve, part_id, number, lot, lanes)
            )
        return carry

    lax.fori_loop(0, count * passes, one, 0)
    rows = attended[...].reshape(2 * count * SLOTS, width)
    for cols in column_parts(weight_ref):
        product = jnp.dot(rows, weight_ref[:, cols], preferred_element_type=jnp.float32)
        for k, out_ref in enumerate(outs):
            out_ref[:, cols] = product[k * SLOTS : k * SLOTS + MOST].astype(jnp.bfloat16)


def attend(lots, panel, queries, places, output_slab):
    first, count = lots
    _, blocks, tok_count, width = panel.shape
    length = blocks * tok_count
    heads = min(8 if first == blocks // 8 else 4, width // HS) if blocks <= 16 else 1
    model_width = output_slab.shape[1]
    held = heads * 2 * SLOTS * length * 6 + 2 * length * width * 2 + width * model_width * 2
    held += 2 * count * SLOTS * (model_width * 8 + width * 2)
    return pl.pallas_call(
        functools.partial(attend_kernel, lots, heads),
        in_specs=[WHOLE] * 4,
        out_specs=[WHOLE] * (2 * count),
        out_shape=[jax.ShapeDtypeStruct((MOST, model_width), jnp.bfloat16)] * (2 * count),
        scratch_shapes=[
            pltpu.VMEM((2 * count, SLOTS, width), jnp.bfloat16),
            pltpu.VMEM((heads, 2 * MOST, length), jnp.float32),
            pltpu.VMEM((heads, 2 * MOST, length), jnp.bfloat16),
        ],
        compiler_params=pltpu.CompilerParams(vmem_limit_bytes=held * 9 // 8 + 4 * MIB),
        cost_estimate=pl.CostEstimate(
            flops=count * 2 * SLOTS * width * (4 * length + 2 * model_width),
            bytes_accessed=4 * length * width,
            transcendentals=count * 2 * SLOTS * length * width // HS,
        ),
        name="attend",
    )(panel, queries, places, output_slab)


def piece_groups(count):
    return [0, *range(count // 2, count)], list(range(count // 2 - 1, 0, -1))


def mix_kernel(quarter_count, top_ref, bottom_ref, router_ref, *refs):
    *mix_refs, slots_ref, gates_ref = refs
    half = LANES // 2
    rows = jnp.concatenate([message_rows(ref, half) for ref in (top_ref, bottom_ref)], axis=0)
    rest, terms = router_ref[...], []
    for _ in range(3):
        terms.append(rest.astype(jnp.bfloat16).astype(jnp.float32))
        rest = rest - terms[-1]
    experts = rest.shape[0]
    router = jnp.concatenate([*terms, jnp.zeros_like(rest)], axis=0).astype(jnp.bfloat16)
    products = lax.dot_general(
        router, rows, (((1,), (1,)), ((), ())), preferred_element_type=jnp.float32
    )
    logits = products[:experts] + (
        products[experts : 2 * experts] + products[2 * experts : 3 * experts]
    )
    slots = message_codes(top_ref)[:experts]
    logits = jnp.where(slots >= 0, logits, -jnp.inf)
    raised = jnp.exp(logits - jnp.max(logits, axis=0, keepdims=True))
    slots_ref[...] = slots
    gates_ref[...] = raised / jnp.sum(raised, axis=0, keepdims=True)
    tok_count = slots.shape[1]
    order = lax.broadcasted_iota(jnp.int32, (SLOTS, tok_count), 0).astype(jnp.float32)
    for mix_ref, group in zip(mix_refs, piece_groups(sum(r.shape[1] for r in mix_refs) // SLOTS)):
        parts = []
        for k in group:
            expert = pl.ds((lax.axis_index("ctx") ^ k) // quarter_count, 1)
            parts.append(jnp.where(order == slots_ref[expert, :], gates_ref[expert, :], 0.0))
        total = jnp.concatenate(parts, axis=0).T
        for part in range(TERMS):
            term = total.astype(jnp.bfloat16)
            mix_ref[pl.ds(part * tok_count, tok_count), :] = term
            total = total - term.astype(jnp.float32)


def gate_mix(quarter_count, halves, router, count):
    tok_count = LANES
    held = pltpu.VMEM((router.shape[0], tok_count), jnp.float32)
    return pl.pallas_call(
        functools.partial(mix_kernel, quarter_count),
        in_specs=[WHOLE] * 3,
        out_specs=[WHOLE] * 2,
        out_shape=[
            jax.ShapeDtypeStruct((TERMS * tok_count, len(group) * SLOTS), jnp.bfloat16)
            for group in piece_groups(count)
        ],
        scratch_shapes=[held, held],
        compiler_params=pltpu.CompilerParams(vmem_limit_bytes=16 * MIB),
        name="gate_mix",
    )(*halves, router)


def combine_kernel(ahead_count, mix_ref, *refs):
    *refs, out_ref, held, sent = refs
    ahead, pieces = refs[:ahead_count], refs[ahead_count:]
    tok_count, model_width = out_ref.shape
    copies = []
    step = min(model_width, 512)
    spare = jnp.zeros((SLOTS - MOST, step), jnp.float32)
    for start in range(0, model_width, step):
        cols = pl.ds(start, step)
        rows = []
        for piece in pieces:
            rows += [piece[:, cols].astype(jnp.float32), spare]
        rows = jnp.concatenate(rows, axis=0).astype(jnp.bfloat16)
        product = jnp.dot(mix_ref[...], rows, preferred_element_type=jnp.float32)
        total = product[-tok_count:]
        for part in range(TERMS - 2, -1, -1):
            total = product[part * tok_count : (part + 1) * tok_count] + total
        for ref in ahead:
            total = total + ref[:, cols]
        held[:, cols] = total.astype(held.dtype)
        copies.append(
            pltpu.make_async_copy(held.at[:, cols], out_ref.at[:, cols], sent.at[len(copies)])
        )
        copies[-1].start()
    for copy in copies:
        copy.wait()


def combine(mix, pieces, ahead, dtype):
    tok_count = mix.shape[0] // TERMS
    model_width = pieces[0].shape[1]
    return pl.pallas_call(
        functools.partial(combine_kernel, len(ahead)),
        in_specs=[WHOLE] * (1 + len(ahead) + len(pieces)),
        out_specs=pl.BlockSpec(memory_space=pl.ANY),
        out_shape=jax.ShapeDtypeStruct((tok_count, model_width), dtype),
        scratch_shapes=[
            pltpu.VMEM((tok_count, model_width), dtype),
            pltpu.SemaphoreType.DMA((-(-model_width // 512),)),
        ],
        compiler_params=pltpu.CompilerParams(vmem_limit_bytes=24 * MIB),
        name="combine",
    )(mix, *ahead, *pieces)


def per_device(
    tokens, norm_gain, router_weight, routes, key_weight, value_weight, query_weight, output_weight
):
    tok_count, model_width = tokens.shape
    ctx_count = lax.axis_size("ctx")
    exp_count = lax.axis_size("exp")
    quarter_count = ctx_count // EXPERTS
    head_width = query_weight.shape[2]
    ranks = list(range(0, ctx_count, 2)) + list(range(1, ctx_count, 2))[::-1]
    forward = [(ranks[p], ranks[(p + 1) % ctx_count]) for p in range(ctx_count)]
    backward = [(b, a) for a, b in forward]
    sibling = [(e, 1 - e) for e in range(exp_count)]
    query_slab = query_weight[0]
    output_slab = output_weight[0]
    if quarter_count > 1:
        first = (lax.axis_index("ctx") % quarter_count) * head_width
        key_weight = lax.dynamic_slice_in_dim(key_weight, first, head_width, axis=1)
        value_weight = lax.dynamic_slice_in_dim(value_weight, first, head_width, axis=1)

    halves = norm_rows(tokens, norm_gain, routes)
    token_half = tok_count // 2
    steps = ctx_count // 2
    plan = [[0]] + [[-step, step] for step in range(1, steps)] + [[steps]]
    own, other, picked, queries, positions = [], [], [], [], []

    def send(parts):
        return [lax.ppermute(parts[0], "ctx", forward), lax.ppermute(parts[1], "ctx", backward)]

    def hand_over(panel):
        return lax.ppermute(panel, "exp", sibling)

    def tie(*arrays):
        return lax.optimization_barrier(arrays)

    blocks = halves
    lead = send([halves[0], halves[1]])
    rest = send([halves[1], halves[0]])
    for step in range(steps):
        keys, mark = project_keys(token_half, blocks, key_weight)
        following = [lead[0], rest[0], rest[1], lead[1]]
        if step == steps - 2:
            queries = project_queries(picked, query_slab, output_slab)
            picked = []
        if step < steps - 1:
            mark, *lead_next = tie(mark, *lead, *queries)
            queries = lead_next[2:]
            lead = send(lead_next[:2])
        panel, rows, position = project_values(token_half, blocks, plan[step], mark, keys, value_weight)
        if step < steps - 2:
            position, *rest_next = tie(position, *rest)
            rest = send(rest_next)
        own.append(panel)
        picked.append(rows)
        positions.append(position)
        if step < steps - 1:
            other.append(hand_over(panel))
        blocks = following
    queries = [*queries, *project_queries(picked, query_slab, output_slab)]
    own[-1], queries[-1], other[0], *blocks = tie(own[-1], queries[-1], other[0], *lead)
    other.append(hand_over(own[-1]))
    keys, mark = project_keys(token_half, blocks, key_weight)
    panel, rows, position = project_values(token_half, blocks, plan[-1], mark, keys, value_weight)
    own.append(panel)
    other.append(hand_over(panel))
    positions.append(position)
    queries = [*queries, *project_queries([rows], query_slab, output_slab)]
    held = arrange(ctx_count, plan, own, other, queries, positions)

    def swap(piece, k):
        return lax.ppermute(piece, "ctx", [(c, c ^ k) for c in range(ctx_count)])

    half, quarter = ctx_count // 2, ctx_count // 4
    far, mine = [], []
    for start, count in ((half, quarter), (half + quarter, quarter), (0, half)):
        pieces = attend((start // 2, count // 2), *held, output_slab)
        if start > 0:
            places, *pieces = tie(held[2], *pieces)
            held = [*held[:2], places]
            far.append([swap(piece, start + r) for r, piece in enumerate(pieces)])
        else:
            near = pieces
    *near, far[0][0] = tie(*near, far[0][0])
    near = [near[0]] + [swap(near[r], r) for r in range(1, half)]

    pieces = [*near, *far[0], *far[1]]
    early, late = piece_groups(ctx_count)
    early_mix, late_mix = gate_mix(quarter_count, halves, router_weight.T, ctx_count)
    ahead = combine(early_mix, [pieces[k] for k in early], [], jnp.float32)
    return combine(late_mix, [pieces[k] for k in late], [ahead], jnp.bfloat16)


def solution(mesh):
    in_specs = (
        P(("groups", "ctx", "exp"), None),
        P(),
        P(),
        P(("groups", "ctx", "exp"), None),
        P(),
        P(),
        P("ctx", None, None),
        P("ctx", None, None),
    )
    out_specs = P(("groups", "ctx", "exp"), None)
    return jax.shard_map(
        per_device, mesh=mesh, in_specs=in_specs, out_specs=out_specs, check_vma=False
    )
```

profile of v0, /device:TPU:0, one launch (start us, length us, event | category | flops | bytes accessed | tf_op | source)
XLA Modules:
  0.0 89.0 jit_solution(7363060139261211080)
XLA Ops:
  0.0 2.0 %norm_rows.1 = (bf16[1040,128]{1,0:T(8,128)(2,1)}, bf16[1040,128]{1,0:T(8,128)(2,1)}) custom-call(bf16[128,2048]{1,0:T(8,128)(2,1)} %refs_0_.1, f32[1,2048]{1,0:T(1,128)} %bitcast.15, s32[2,128]{1,0:T(2,128)} %bitcast.16), custom_call_target="tpu_custom_call" | custom-call | tf_op jit(solution)/shard_map/norm_rows/pallas_call | solution.py:85
  2.0 3.1 %collective-permute-start = (bf16[1040,128]{1,0:T(8,128)(2,1)}, bf16[1040,128]{1,0:T(8,128)(2,1)S(1)}, u32[]{:S(2)}, u32[]{:S(2)}) collective-permute-start(bf16[1040,128]{1,0:T(8,128)(2,1)} %get-tuple-element.82.top_ref.refs_0_), channel_id=1, source_target_pairs={{0,4},{4,8},{8,12},{12,14},{14,10},{10,6},{6,2},{2,0},{1,5},{5,9},... | collective-permute-start | bytes 798728 | tf_op jit(solution)/shard_map/ppermute | solution.py:473
  5.1 0.0 collective-permute-start.1
  5.1 2.0 %collective-permute-start.3 = (bf16[1040,128]{1,0:T(8,128)(2,1)}, bf16[1040,128]{1,0:T(8,128)(2,1)S(1)}, u32[]{:S(2)}, u32[]{:S(2)}) collective-permute-start(bf16[1040,128]{1,0:T(8,128)(2,1)} %get-tuple-element.82.top_ref.refs_0_), channel_id=1, source_target_pairs={{4,0},{8,4},{12,8},{14,12},{10,14},{6,10},{2,6},{0,2},{5,1},{9,5},... | collective-permute-start | bytes 798728 | tf_op jit(solution)/shard_map/ppermute | solution.py:473
  7.1 0.1 collective-permute-start.2
  7.2 2.2 %copy-done.1 = bf16[2048,1024]{1,0:T(8,128)(2,1)S(1)} copy-done((bf16[2048,1024]{1,0:T(8,128)(2,1)S(1)}, bf16[2048,1024]{1,0:T(8,128)(2,1)}, u32[]{:S(2)}) %copy-start.1) | copy-done | bytes 4194328
  9.4 0.9 %copy-done.6 = bf16[1040,128]{1,0:T(8,128)(2,1)S(1)} copy-done((bf16[1040,128]{1,0:T(8,128)(2,1)S(1)}, bf16[1040,128]{1,0:T(8,128)(2,1)}, u32[]{:S(2)}) %copy-start.6) | copy-done | bytes 266264
  10.3 0.9 %copy-done.8 = bf16[1040,128]{1,0:T(8,128)(2,1)S(1)} copy-done((bf16[1040,128]{1,0:T(8,128)(2,1)S(1)}, bf16[1040,128]{1,0:T(8,128)(2,1)}, u32[]{:S(2)}) %copy-start.8) | copy-done | bytes 266264
  11.3 0.7 project_keys.5
  12.0 0.5 collective-permute-done.refs_0_
  12.5 2.2 %collective-permute-done.1.refs_3_ = bf16[1040,128]{1,0:T(8,128)(2,1)S(1)} collective-permute-done((bf16[1040,128]{1,0:T(8,128)(2,1)}, bf16[1040,128]{1,0:T(8,128)(2,1)S(1)}, u32[]{:S(2)}, u32[]{:S(2)}) %collective-permute-start.1) | collective-permute-done | bytes 266272 | tf_op jit(solution)/shard_map/ppermute | solution.py:473
  14.6 1.6 %collective-permute-start.4 = (bf16[1040,128]{1,0:T(8,128)(2,1)S(1)}, bf16[1040,128]{1,0:T(8,128)(2,1)S(1)}, u32[]{:S(2)}, u32[]{:S(2)}) collective-permute-start(bf16[1040,128]{1,0:T(8,128)(2,1)S(1)} %collective-permute-done.refs_0_), channel_id=1, source_target_pairs={{0,4},{4,8},{8,12},{12,14},{14,10},{10,6},{6,2},{2,0},{1,5},{5,9},... | collective-permute-start | bytes 798728 | tf_op jit(solution)/shard_map/ppermute | solution.py:473
  16.2 0.4 collective-permute-start.5
  16.7 2.2 %copy-done.3 = bf16[2048,1024]{1,0:T(8,128)(2,1)S(1)} copy-done((bf16[2048,1024]{1,0:T(8,128)(2,1)S(1)}, bf16[2048,1024]{1,0:T(8,128)(2,1)}, u32[]{:S(2)}) %copy-start.3) | copy-done | bytes 4194328
  18.9 0.8 project_values.5
  19.7 0.6 collective-permute-done.3.refs_2_
  20.4 1.6 %collective-permute-start.6 = (bf16[1040,128]{1,0:T(8,128)(2,1)S(1)}, bf16[1040,128]{1,0:T(8,128)(2,1)S(1)}, u32[]{:S(2)}, u32[]{:S(2)}) collective-permute-start(bf16[1040,128]{1,0:T(8,128)(2,1)S(1)} %collective-permute-done.2.refs_1_), channel_id=1, source_target_pairs={{0,4},{4,8},{8,12},{12,14},{14,10},{10,6},{6,2},{2,0},{1,5},{5,9},... | collective-permute-start | bytes 798728 | tf_op jit(solution)/shard_map/ppermute | solution.py:473
  21.9 0.4 collective-permute-start.7
  22.4 1.3 %project_keys.6 = (bf16[256,1024]{1,0:T(8,128)(2,1)S(1)}, f32[8,128]{1,0:T(8,128)S(1)}) custom-call(bf16[1040,128]{1,0:T(8,128)(2,1)S(1)} %collective-permute-done.refs_0_, bf16[1040,128]{1,0:T(8,128)(2,1)S(1)} %collective-permute-done.2.refs_1_, bf16[1040,128]{1,0:T(8,128)(2,1)S(1)} %collective-permute-done.3.refs_2_, ...), custom_call_target="tpu_custom_call" | custom-call | tf_op jit(solution)/shard_map/project_keys/pallas_call | solution.py:115
  23.7 0.3 collective-permute-done.4.refs_0_
  24.0 2.1 %collective-permute-done.5.refs_3_ = bf16[1040,128]{1,0:T(8,128)(2,1)S(1)} collective-permute-done((bf16[1040,128]{1,0:T(8,128)(2,1)S(1)}, bf16[1040,128]{1,0:T(8,128)(2,1)S(1)}, u32[]{:S(2)}, u32[]{:S(2)}) %collective-permute-start.5) | collective-permute-done | bytes 266272 | tf_op jit(solution)/shard_map/ppermute | solution.py:473
  26.1 1.6 %collective-permute-start.8 = (bf16[1040,128]{1,0:T(8,128)(2,1)S(1)}, bf16[1040,128]{1,0:T(8,128)(2,1)S(1)}, u32[]{:S(2)}, u32[]{:S(2)}) collective-permute-start(bf16[1040,128]{1,0:T(8,128)(2,1)S(1)} %collective-permute-done.4.refs_0_), channel_id=1, source_target_pairs={{0,4},{4,8},{8,12},{12,14},{14,10},{10,6},{6,2},{2,0},{1,5},{5,9},... | collective-permute-start | bytes 798728 | tf_op jit(solution)/shard_map/ppermute | solution.py:473
  27.6 0.4 collective-permute-start.9
  28.1 1.5 %project_values.6 = (bf16[2,256,1024]{2,1,0:T(8,128)(2,1)S(1)}, bf16[2,48,2048]{2,1,0:T(8,128)(2,1)S(1)}, f32[2,48,128]{2,1,0:T(8,128)S(1)}) custom-call(f32[8,128]{1,0:T(8,128)S(1)} %get-tuple-element.93.mark_ref, bf16[256,1024]{1,0:T(8,128)(2,1)S(1)} %get-tuple-element.94.keys_ref, bf16[1040,128]{1,0:T(8,128)(2,1)S(1)} %collective-permute-done.refs_0_, ...), custom_call_target="tpu_custom_call" | custom-call | tf_op jit(solution)/shard_map/project_values/pallas_call | solution.py:160
  29.6 0.1 collective-permute-done.6.refs_1_
  29.7 2.1 %collective-permute-done.7.refs_2_ = bf16[1040,128]{1,0:T(8,128)(2,1)S(1)} collective-permute-done((bf16[1040,128]{1,0:T(8,128)(2,1)S(1)}, bf16[1040,128]{1,0:T(8,128)(2,1)S(1)}, u32[]{:S(2)}, u32[]{:S(2)}) %collective-permute-start.7) | collective-permute-done | bytes 266272 | tf_op jit(solution)/shard_map/ppermute | solution.py:473
  31.8 1.6 %collective-permute-start.10 = (bf16[1040,128]{1,0:T(8,128)(2,1)S(1)}, bf16[1040,128]{1,0:T(8,128)(2,1)S(1)}, u32[]{:S(2)}, u32[]{:S(2)}) collective-permute-start(bf16[1040,128]{1,0:T(8,128)(2,1)S(1)} %collective-permute-done.6.refs_1_), channel_id=1, source_target_pairs={{0,4},{4,8},{8,12},{12,14},{14,10},{10,6},{6,2},{2,0},{1,5},{5,9},... | collective-permute-start | bytes 798728 | tf_op jit(solution)/shard_map/ppermute | solution.py:473
  33.3 0.4 collective-permute-start.11
  33.8 0.8 project_queries.3
  34.6 1.3 %project_keys.7 = (bf16[256,1024]{1,0:T(8,128)(2,1)S(1)}, f32[8,128]{1,0:T(8,128)S(1)}) custom-call(bf16[1040,128]{1,0:T(8,128)(2,1)S(1)} %collective-permute-done.4.refs_0_, bf16[1040,128]{1,0:T(8,128)(2,1)S(1)} %collective-permute-done.6.refs_1_, bf16[1040,128]{1,0:T(8,128)(2,1)S(1)} %collective-permute-done.7.refs_2_, ...), custom_call_target="tpu_custom_call" | custom-call | tf_op jit(solution)/shard_map/project_keys/pallas_call | solution.py:115
  35.9 1.6 %collective-permute-done.9.refs_3_ = bf16[1040,128]{1,0:T(8,128)(2,1)S(1)} collective-permute-done((bf16[1040,128]{1,0:T(8,128)(2,1)S(1)}, bf16[1040,128]{1,0:T(8,128)(2,1)S(1)}, u32[]{:S(2)}, u32[]{:S(2)}) %collective-permute-start.9) | collective-permute-done | bytes 266272 | tf_op jit(solution)/shard_map/ppermute | solution.py:473
  37.5 1.6 %collective-permute-start.13 = (bf16[1040,128]{1,0:T(8,128)(2,1)S(1)}, bf16[1040,128]{1,0:T(8,128)(2,1)S(1)}, u32[]{:S(2)}, u32[]{:S(2)}) collective-permute-start(bf16[1040,128]{1,0:T(8,128)(2,1)S(1)} %collective-permute-done.8.refs_0_), channel_id=1, source_target_pairs={{0,4},{4,8},{8,12},{12,14},{14,10},{10,6},{6,2},{2,0},{1,5},{5,9},... | collective-permute-start | bytes 798728 | tf_op jit(solution)/shard_map/ppermute | solution.py:473
  39.0 0.4 collective-permute-start.14
  39.5 1.5 %project_values.7 = (bf16[2,256,1024]{2,1,0:T(8,128)(2,1)S(1)}, bf16[2,48,2048]{2,1,0:T(8,128)(2,1)S(1)}, f32[2,48,128]{2,1,0:T(8,128)S(1)}) custom-call(f32[8,128]{1,0:T(8,128)S(1)} %get-tuple-element.106.mark_ref, bf16[256,1024]{1,0:T(8,128)(2,1)S(1)} %get-tuple-element.107.keys_ref, bf16[1040,128]{1,0:T(8,128)(2,1)S(1)} %collective-permute-done.4.refs_0_, ...), custom_call_target="tpu_custom_call" | custom-call | tf_op jit(solution)/shard_map/project_values/pallas_call | solution.py:160
  41.0 0.1 collective-permute-done.10.refs_1_
  41.1 2.1 %collective-permute-done.11.refs_2_ = bf16[1040,128]{1,0:T(8,128)(2,1)S(1)} collective-permute-done((bf16[1040,128]{1,0:T(8,128)(2,1)S(1)}, bf16[1040,128]{1,0:T(8,128)(2,1)S(1)}, u32[]{:S(2)}, u32[]{:S(2)}) %collective-permute-start.11) | collective-permute-done | bytes 266272 | tf_op jit(solution)/shard_map/ppermute | solution.py:473
  43.2 1.3 %project_keys.8 = (bf16[256,1024]{1,0:T(8,128)(2,1)S(1)}, f32[8,128]{1,0:T(8,128)S(1)}) custom-call(bf16[1040,128]{1,0:T(8,128)(2,1)S(1)} %collective-permute-done.8.refs_0_, bf16[1040,128]{1,0:T(8,128)(2,1)S(1)} %collective-permute-done.10.refs_1_, bf16[1040,128]{1,0:T(8,128)(2,1)S(1)} %collective-permute-done.11.refs_2_, ...), custom_call_target="tpu_custom_call" | custom-call | tf_op jit(solution)/shard_map/project_keys/pallas_call | solution.py:115
  44.5 1.5 %project_values.8 = (bf16[2,256,1024]{2,1,0:T(8,128)(2,1)S(1)}, bf16[2,48,2048]{2,1,0:T(8,128)(2,1)S(1)}, f32[2,48,128]{2,1,0:T(8,128)S(1)}) custom-call(f32[8,128]{1,0:T(8,128)S(1)} %get-tuple-element.112.mark_ref, bf16[256,1024]{1,0:T(8,128)(2,1)S(1)} %get-tuple-element.113.keys_ref, bf16[1040,128]{1,0:T(8,128)(2,1)S(1)} %collective-permute-done.8.refs_0_, ...), custom_call_target="tpu_custom_call" | custom-call | tf_op jit(solution)/shard_map/project_values/pallas_call | solution.py:160
  46.0 1.0 %project_queries.4 = (bf16[2,48,1024]{2,1,0:T(8,128)(2,1)S(1)}, bf16[2,48,1024]{2,1,0:T(8,128)(2,1)S(1)}) custom-call(bf16[2,48,2048]{2,1,0:T(8,128)(2,1)S(1)} %get-tuple-element.115.refs_0_, bf16[2,48,2048]{2,1,0:T(8,128)(2,1)S(1)} %get-tuple-element.116.refs_1_, bf16[2048,1024]{1,0:T(8,128)(2,1)S(1)} %bitcast.12, bf16[1024,2048]{1,0:T(8,128)(2,1)S(1)} %bitcast.6), custom_call_target="tpu_custom_call" | custom-call | tf_op jit(solution)/shard_map/project_queries/pallas_call | solution.py:189
  47.0 0.4 collective-permute-done.14.refs_1_
  47.4 0.1 collective-permute-start.17
  47.6 0.7 project_keys.9
  48.3 0.8 project_values.9
  49.1 0.4 collective-permute-start.18
  49.5 0.8 project_queries.5.refs_14_
  50.4 0.0 collective-permute-done.15.refs_6_
  50.4 0.7 collective-permute-done.18.refs_9_
  51.1 0.7 arrange.1
  51.8 3.9 %attend.3 = (bf16[40,2048]{1,0:T(8,128)(2,1)S(1)}, bf16[40,2048]{1,0:T(8,128)(2,1)S(1)}) custom-call(bf16[2,16,128,1024]{3,2,1,0:T(8,128)(2,1)S(1)} %get-tuple-element.137.panel_ref, f32[8,40,1024]{2,1,0:T(8,128)S(1)} %get-tuple-element.138.queries_ref, f32[8,40,128]{2,1,0:T(8,128)S(1)} %get-tuple-element.145.places_ref, bf16[1024,2048]{1,0:T(8,128)(2,1)S(1)} %bitcast.8), custom_call_target="tpu_custom_call" | custom-call | flops 1207959552 | bytes 8388608 | tf_op jit(solution)/shard_map/attend/pallas_call | solution.py:326
  55.7 0.7 collective-permute-start.19
  56.4 2.0 %collective-permute-start.20 = (bf16[40,2048]{1,0:T(8,128)(2,1)S(1)}, bf16[40,2048]{1,0:T(8,128)(2,1)S(1)}, u32[]{:S(2)}, u32[]{:S(2)}) collective-permute-start(bf16[40,2048]{1,0:T(8,128)(2,1)S(1)} %get-tuple-element.153), channel_id=1, source_target_pairs={{0,10},{2,8},{4,14},{6,12},{8,2},{10,0},{12,6},{14,4},{1,11},{3,9}... | collective-permute-start | bytes 491528 | tf_op jit(solution)/shard_map/ppermute | solution.py:516
  58.4 5.3 %attend.4 = (bf16[40,2048]{1,0:T(8,128)(2,1)S(1)}, bf16[40,2048]{1,0:T(8,128)(2,1)S(1)}) custom-call(bf16[2,16,128,1024]{3,2,1,0:T(8,128)(2,1)S(1)} %get-tuple-element.137.panel_ref, f32[8,40,1024]{2,1,0:T(8,128)S(1)} %get-tuple-element.138.queries_ref, f32[8,40,128]{2,1,0:T(8,128)S(1)} %get-tuple-element.145.places_ref, bf16[1024,2048]{1,0:T(8,128)(2,1)S(1)} %bitcast.9), custom_call_target="tpu_custom_call" | custom-call | flops 1207959552 | bytes 8388608 | tf_op jit(solution)/shard_map/attend/pallas_call | solution.py:326
  63.7 0.1 collective-permute-start.21
  63.8 5.0 %collective-permute-start.22 = (bf16[40,2048]{1,0:T(8,128)(2,1)S(1)}, bf16[40,2048]{1,0:T(8,128)(2,1)S(1)}, u32[]{:S(2)}, u32[]{:S(2)}) collective-permute-start(bf16[40,2048]{1,0:T(8,128)(2,1)S(1)} %get-tuple-element.155), channel_id=1, source_target_pairs={{0,14},{2,12},{4,10},{6,8},{8,6},{10,4},{12,2},{14,0},{1,15},{3,13... | collective-permute-start | bytes 491528 | tf_op jit(solution)/shard_map/ppermute | solution.py:516
  68.8 4.7 %attend.5 = (bf16[40,2048]{1,0:T(8,128)(2,1)S(1)}, bf16[40,2048]{1,0:T(8,128)(2,1)S(1)}, bf16[40,2048]{1,0:T(8,128)(2,1)S(1)}, bf16[40,2048]{1,0:T(8,128)(2,1)S(1)}) custom-call(bf16[2,16,128,1024]{3,2,1,0:T(8,128)(2,1)S(1)} %get-tuple-element.137.panel_ref, f32[8,40,1024]{2,1,0:T(8,128)S(1)} %get-tuple-element.138.queries_ref, ...), custom_call_target="tpu_custom_call" | custom-call | flops 2415919104 | bytes 8388608 | tf_op jit(solution)/shard_map/attend/pallas_call | solution.py:326
  73.5 4.2 %collective-permute-done.19.refs_1_ = bf16[40,2048]{1,0:T(8,128)(2,1)S(1)} collective-permute-done((bf16[40,2048]{1,0:T(8,128)(2,1)S(1)}, bf16[40,2048]{1,0:T(8,128)(2,1)S(1)}, u32[]{:S(2)}, u32[]{:S(2)}) %collective-permute-start.19) | collective-permute-done | bytes 163872 | tf_op jit(solution)/shard_map/ppermute | solution.py:516
  77.7 1.7 %collective-permute-start.24 = (bf16[40,2048]{1,0:T(8,128)(2,1)S(1)}, bf16[40,2048]{1,0:T(8,128)(2,1)S(1)}, u32[]{:S(2)}, u32[]{:S(2)}) collective-permute-start(bf16[40,2048]{1,0:T(8,128)(2,1)S(1)} %get-tuple-element.157), channel_id=1, source_target_pairs={{0,4},{2,6},{4,0},{6,2},{8,12},{10,14},{12,8},{14,10},{1,5},{3,7},... | collective-permute-start | bytes 491528 | tf_op jit(solution)/shard_map/ppermute | solution.py:516
  79.5 1.5 %collective-permute-done.20.refs_2_ = bf16[40,2048]{1,0:T(8,128)(2,1)S(1)} collective-permute-done((bf16[40,2048]{1,0:T(8,128)(2,1)S(1)}, bf16[40,2048]{1,0:T(8,128)(2,1)S(1)}, u32[]{:S(2)}, u32[]{:S(2)}) %collective-permute-start.20) | collective-permute-done | bytes 163872 | tf_op jit(solution)/shard_map/ppermute | solution.py:516
  81.0 1.7 %collective-permute-start.25 = (bf16[40,2048]{1,0:T(8,128)(2,1)S(1)}, bf16[40,2048]{1,0:T(8,128)(2,1)S(1)}, u32[]{:S(2)}, u32[]{:S(2)}) collective-permute-start(bf16[40,2048]{1,0:T(8,128)(2,1)S(1)} %get-tuple-element.158), channel_id=1, source_target_pairs={{0,2},{2,0},{4,6},{6,4},{8,10},{10,8},{12,14},{14,12},{1,3},{3,1},... | collective-permute-start | bytes 491528 | tf_op jit(solution)/shard_map/ppermute | solution.py:516
  82.7 0.5 gate_mix.1
  83.2 1.0 %combine.2.refs_0_ = f32[128,2048]{1,0:T(8,128)S(1)} custom-call(bf16[256,240]{1,0:T(8,128)(2,1)S(1)} %get-tuple-element.85.mix_ref, bf16[40,2048]{1,0:T(8,128)(2,1)S(1)} %get-tuple-element.151.refs_0_, bf16[40,2048]{1,0:T(8,128)(2,1)S(1)} %collective-permute-done.19.refs_1_, bf16[40,2048]{1,0:T(8,128)(2,1)S(1)} %collective-permute-done.20.refs_2_, ...), custom_call_target="tpu_custom_call" | custom-call | tf_op jit(solution)/shard_map/combine/pallas_call | solution.py:433
  84.2 1.5 %collective-permute-done.23.refs_1_ = bf16[40,2048]{1,0:T(8,128)(2,1)S(1)} collective-permute-done((bf16[40,2048]{1,0:T(8,128)(2,1)S(1)}, bf16[40,2048]{1,0:T(8,128)(2,1)S(1)}, u32[]{:S(2)}, u32[]{:S(2)}) %collective-permute-start.23) | collective-permute-done | bytes 163872 | tf_op jit(solution)/shard_map/ppermute | solution.py:516
  85.8 1.9 %collective-permute-done.24.refs_2_ = bf16[40,2048]{1,0:T(8,128)(2,1)S(1)} collective-permute-done((bf16[40,2048]{1,0:T(8,128)(2,1)S(1)}, bf16[40,2048]{1,0:T(8,128)(2,1)S(1)}, u32[]{:S(2)}, u32[]{:S(2)}) %collective-permute-start.24) | collective-permute-done | bytes 163872 | tf_op jit(solution)/shard_map/ppermute | solution.py:516
  87.7 1.1 %combine.3 = bf16[128,2048]{1,0:T(8,128)(2,1)} custom-call(bf16[256,144]{1,0:T(8,128)(2,1)S(1)} %get-tuple-element.84.mix_ref, f32[128,2048]{1,0:T(8,128)S(1)} %combine.2.refs_0_, bf16[40,2048]{1,0:T(8,128)(2,1)S(1)} %collective-permute-done.23.refs_1_, bf16[40,2048]{1,0:T(8,128)(2,1)S(1)} %collective-permute-done.24.refs_2_, ...), custom_call_target="tpu_custom_call" | custom-call | tf_op jit(solution)/shard_map/combine/pallas_call | solution.py:433
  (31 shorter events, 0.1 us)
Async XLA Ops:
  2.0 10.5 %collective-permute-start = (bf16[1040,128]{1,0:T(8,128)(2,1)}, bf16[1040,128]{1,0:T(8,128)(2,1)S(1)}, u32[]{:S(2)}, u32[]{:S(2)}) collective-permute-start(bf16[1040,128]{1,0:T(8,128)(2,1)} %get-tuple-element.82.top_ref.refs_0_), channel_id=1, source_target_pairs={{0,4},{4,8},{8,12},{12,14},{14,10},{10,6},{6,2},{2,0},{1,5},{5,9},... | collective-permute-start | bytes 798728 | tf_op jit(solution)/shard_map/ppermute | solution.py:473
  5.1 9.5 %collective-permute-start.1 = (bf16[1040,128]{1,0:T(8,128)(2,1)}, bf16[1040,128]{1,0:T(8,128)(2,1)S(1)}, u32[]{:S(2)}, u32[]{:S(2)}) collective-permute-start(bf16[1040,128]{1,0:T(8,128)(2,1)} %get-tuple-element.83.bottom_ref.refs_1_), channel_id=1, source_target_pairs={{4,0},{8,4},{12,8},{14,12},{10,14},{6,10},{2,6},{0,2},{5,1},{9,5},... | collective-permute-start | bytes 798728 | tf_op jit(solution)/shard_map/ppermute | solution.py:473
  5.1 15.2 %collective-permute-start.3 = (bf16[1040,128]{1,0:T(8,128)(2,1)}, bf16[1040,128]{1,0:T(8,128)(2,1)S(1)}, u32[]{:S(2)}, u32[]{:S(2)}) collective-permute-start(bf16[1040,128]{1,0:T(8,128)(2,1)} %get-tuple-element.82.top_ref.refs_0_), channel_id=1, source_target_pairs={{4,0},{8,4},{12,8},{14,12},{10,14},{6,10},{2,6},{0,2},{5,1},{9,5},... | collective-permute-start | bytes 798728 | tf_op jit(solution)/shard_map/ppermute | solution.py:473
  7.1 13.3 %collective-permute-start.2 = (bf16[1040,128]{1,0:T(8,128)(2,1)}, bf16[1040,128]{1,0:T(8,128)(2,1)S(1)}, u32[]{:S(2)}, u32[]{:S(2)}) collective-permute-start(bf16[1040,128]{1,0:T(8,128)(2,1)} %get-tuple-element.83.bottom_ref.refs_1_), channel_id=1, source_target_pairs={{0,4},{4,8},{8,12},{12,14},{14,10},{10,6},{6,2},{2,0},{1,5},{5,9},... | collective-permute-start | bytes 798728 | tf_op jit(solution)/shard_map/ppermute | solution.py:473
  7.2 2.2 %copy-start.1 = (bf16[2048,1024]{1,0:T(8,128)(2,1)S(1)}, bf16[2048,1024]{1,0:T(8,128)(2,1)}, u32[]{:S(2)}) copy-start(bf16[2048,1024]{1,0:T(8,128)(2,1)} %refs_2_.6) | copy-start | bytes 12582916
  9.4 1.0 %copy-start.6 = (bf16[1040,128]{1,0:T(8,128)(2,1)S(1)}, bf16[1040,128]{1,0:T(8,128)(2,1)}, u32[]{:S(2)}) copy-start(bf16[1040,128]{1,0:T(8,128)(2,1)} %get-tuple-element.82.top_ref.refs_0_) | copy-start | bytes 798724
  10.3 1.0 %copy-start.8 = (bf16[1040,128]{1,0:T(8,128)(2,1)S(1)}, bf16[1040,128]{1,0:T(8,128)(2,1)}, u32[]{:S(2)}) copy-start(bf16[1040,128]{1,0:T(8,128)(2,1)} %get-tuple-element.83.bottom_ref.refs_1_) | copy-start | bytes 798724
  11.3 11.1 %copy-start.2 = (bf16[2048,1024]{1,0:T(8,128)(2,1)S(1)}, bf16[2048,1024]{1,0:T(8,128)(2,1)}, u32[]{:S(2)}) copy-start(bf16[2048,1024]{1,0:T(8,128)(2,1)} %refs_2_.6) | copy-start | bytes 12582916
  14.6 9.3 %collective-permute-start.4 = (bf16[1040,128]{1,0:T(8,128)(2,1)S(1)}, bf16[1040,128]{1,0:T(8,128)(2,1)S(1)}, u32[]{:S(2)}, u32[]{:S(2)}) collective-permute-start(bf16[1040,128]{1,0:T(8,128)(2,1)S(1)} %collective-permute-done.refs_0_), channel_id=1, source_target_pairs={{0,4},{4,8},{8,12},{12,14},{14,10},{10,6},{6,2},{2,0},{1,5},{5,9},... | collective-permute-start | bytes 798728 | tf_op jit(solution)/shard_map/ppermute | solution.py:473
  16.2 9.8 %collective-permute-start.5 = (bf16[1040,128]{1,0:T(8,128)(2,1)S(1)}, bf16[1040,128]{1,0:T(8,128)(2,1)S(1)}, u32[]{:S(2)}, u32[]{:S(2)}) collective-permute-start(bf16[1040,128]{1,0:T(8,128)(2,1)S(1)} %collective-permute-done.1.refs_3_), channel_id=1, source_target_pairs={{4,0},{8,4},{12,8},{14,12},{10,14},{6,10},{2,6},{0,2},{5,1},{9,5},... | collective-permute-start | bytes 798728 | tf_op jit(solution)/shard_map/ppermute | solution.py:473
  16.7 2.2 %copy-start.3 = (bf16[2048,1024]{1,0:T(8,128)(2,1)S(1)}, bf16[2048,1024]{1,0:T(8,128)(2,1)}, u32[]{:S(2)}) copy-start(bf16[2048,1024]{1,0:T(8,128)(2,1)} %refs_2_.7) | copy-start | bytes 12582916
  18.9 9.2 %copy-start.4 = (bf16[2048,1024]{1,0:T(8,128)(2,1)S(1)}, bf16[2048,1024]{1,0:T(8,128)(2,1)}, u32[]{:S(2)}) copy-start(bf16[2048,1024]{1,0:T(8,128)(2,1)} %refs_2_.7) | copy-start | bytes 12582916
  20.4 9.3 %collective-permute-start.6 = (bf16[1040,128]{1,0:T(8,128)(2,1)S(1)}, bf16[1040,128]{1,0:T(8,128)(2,1)S(1)}, u32[]{:S(2)}, u32[]{:S(2)}) collective-permute-start(bf16[1040,128]{1,0:T(8,128)(2,1)S(1)} %collective-permute-done.2.refs_1_), channel_id=1, source_target_pairs={{0,4},{4,8},{8,12},{12,14},{14,10},{10,6},{6,2},{2,0},{1,5},{5,9},... | collective-permute-start | bytes 798728 | tf_op jit(solution)/shard_map/ppermute | solution.py:473
  21.9 9.8 %collective-permute-start.7 = (bf16[1040,128]{1,0:T(8,128)(2,1)S(1)}, bf16[1040,128]{1,0:T(8,128)(2,1)S(1)}, u32[]{:S(2)}, u32[]{:S(2)}) collective-permute-start(bf16[1040,128]{1,0:T(8,128)(2,1)S(1)} %collective-permute-done.3.refs_2_), channel_id=1, source_target_pairs={{4,0},{8,4},{12,8},{14,12},{10,14},{6,10},{2,6},{0,2},{5,1},{9,5},... | collective-permute-start | bytes 798728 | tf_op jit(solution)/shard_map/ppermute | solution.py:473
  22.4 11.4 %copy-start.5 = (bf16[1,2048,1024]{2,1,0:T(8,128)(2,1)S(1)}, bf16[1,2048,1024]{2,1,0:T(8,128)(2,1)}, u32[]{:S(2)}) copy-start(bf16[1,2048,1024]{2,1,0:T(8,128)(2,1)} %param.14) | copy-start | bytes 12582916
  23.7 10.1 %copy-start = (bf16[1,1024,2048]{2,1,0:T(8,128)(2,1)S(1)}, bf16[1,1024,2048]{2,1,0:T(8,128)(2,1)}, u32[]{:S(2)}) copy-start(bf16[1,1024,2048]{2,1,0:T(8,128)(2,1)} %param.15) | copy-start | bytes 12582916
  26.1 9.8 %collective-permute-start.8 = (bf16[1040,128]{1,0:T(8,128)(2,1)S(1)}, bf16[1040,128]{1,0:T(8,128)(2,1)S(1)}, u32[]{:S(2)}, u32[]{:S(2)}) collective-permute-start(bf16[1040,128]{1,0:T(8,128)(2,1)S(1)} %collective-permute-done.4.refs_0_), channel_id=1, source_target_pairs={{0,4},{4,8},{8,12},{12,14},{14,10},{10,6},{6,2},{2,0},{1,5},{5,9},... | collective-permute-start | bytes 798728 | tf_op jit(solution)/shard_map/ppermute | solution.py:473
  27.6 9.8 %collective-permute-start.9 = (bf16[1040,128]{1,0:T(8,128)(2,1)S(1)}, bf16[1040,128]{1,0:T(8,128)(2,1)S(1)}, u32[]{:S(2)}, u32[]{:S(2)}) collective-permute-start(bf16[1040,128]{1,0:T(8,128)(2,1)S(1)} %collective-permute-done.5.refs_3_), channel_id=1, source_target_pairs={{4,0},{8,4},{12,8},{14,12},{10,14},{6,10},{2,6},{0,2},{5,1},{9,5},... | collective-permute-start | bytes 798728 | tf_op jit(solution)/shard_map/ppermute | solution.py:473
  28.1 18.9 %collective-permute-start.12 = (bf16[2,128,1024]{2,1,0:T(8,128)(2,1)S(1)}, bf16[2,128,1024]{2,1,0:T(8,128)(2,1)S(1)}, u32[]{:S(2)}, u32[]{:S(2)}) collective-permute-start(bf16[2,128,1024]{2,1,0:T(8,128)(2,1)S(1)} %get-tuple-element.89.refs_0_), channel_id=1, source_target_pairs={{0,1},{1,0},{2,3},{3,2},{4,5},{5,4},{6,7},{7,6},{8,9},{9,8},{10,11... | collective-permute-start | bytes 1572872 | tf_op jit(solution)/shard_map/ppermute | solution.py:476
  31.8 9.3 %collective-permute-start.10 = (bf16[1040,128]{1,0:T(8,128)(2,1)S(1)}, bf16[1040,128]{1,0:T(8,128)(2,1)S(1)}, u32[]{:S(2)}, u32[]{:S(2)}) collective-permute-start(bf16[1040,128]{1,0:T(8,128)(2,1)S(1)} %collective-permute-done.6.refs_1_), channel_id=1, source_target_pairs={{0,4},{4,8},{8,12},{12,14},{14,10},{10,6},{6,2},{2,0},{1,5},{5,9},... | collective-permute-start | bytes 798728 | tf_op jit(solution)/shard_map/ppermute | solution.py:473
  33.3 9.8 %collective-permute-start.11 = (bf16[1040,128]{1,0:T(8,128)(2,1)S(1)}, bf16[1040,128]{1,0:T(8,128)(2,1)S(1)}, u32[]{:S(2)}, u32[]{:S(2)}) collective-permute-start(bf16[1040,128]{1,0:T(8,128)(2,1)S(1)} %collective-permute-done.7.refs_2_), channel_id=1, source_target_pairs={{4,0},{8,4},{12,8},{14,12},{10,14},{6,10},{2,6},{0,2},{5,1},{9,5},... | collective-permute-start | bytes 798728 | tf_op jit(solution)/shard_map/ppermute | solution.py:473
  37.5 9.5 %collective-permute-start.13 = (bf16[1040,128]{1,0:T(8,128)(2,1)S(1)}, bf16[1040,128]{1,0:T(8,128)(2,1)S(1)}, u32[]{:S(2)}, u32[]{:S(2)}) collective-permute-start(bf16[1040,128]{1,0:T(8,128)(2,1)S(1)} %collective-permute-done.8.refs_0_), channel_id=1, source_target_pairs={{0,4},{4,8},{8,12},{12,14},{14,10},{10,6},{6,2},{2,0},{1,5},{5,9},... | collective-permute-start | bytes 798728 | tf_op jit(solution)/shard_map/ppermute | solution.py:473
  39.0 8.4 %collective-permute-start.14 = (bf16[1040,128]{1,0:T(8,128)(2,1)S(1)}, bf16[1040,128]{1,0:T(8,128)(2,1)S(1)}, u32[]{:S(2)}, u32[]{:S(2)}) collective-permute-start(bf16[1040,128]{1,0:T(8,128)(2,1)S(1)} %collective-permute-done.9.refs_3_), channel_id=1, source_target_pairs={{4,0},{8,4},{12,8},{14,12},{10,14},{6,10},{2,6},{0,2},{5,1},{9,5},... | collective-permute-start | bytes 798728 | tf_op jit(solution)/shard_map/ppermute | solution.py:473
  41.1 9.3 %collective-permute-start.15 = (bf16[2,256,1024]{2,1,0:T(8,128)(2,1)S(1)}, bf16[2,256,1024]{2,1,0:T(8,128)(2,1)S(1)}, u32[]{:S(2)}, u32[]{:S(2)}) collective-permute-start(bf16[2,256,1024]{2,1,0:T(8,128)(2,1)S(1)} %get-tuple-element.95.refs_1_), channel_id=1, source_target_pairs={{0,1},{1,0},{2,3},{3,2},{4,5},{5,4},{6,7},{7,6},{8,9},{9,8},{10,11... | collective-permute-start | bytes 3145736 | tf_op jit(solution)/shard_map/ppermute | solution.py:476
  43.2 7.9 %collective-permute-start.16 = (bf16[2,256,1024]{2,1,0:T(8,128)(2,1)S(1)}, bf16[2,256,1024]{2,1,0:T(8,128)(2,1)S(1)}, u32[]{:S(2)}, u32[]{:S(2)}) collective-permute-start(bf16[2,256,1024]{2,1,0:T(8,128)(2,1)S(1)} %get-tuple-element.108.refs_2_), channel_id=1, source_target_pairs={{0,1},{1,0},{2,3},{3,2},{4,5},{5,4},{6,7},{7,6},{8,9},{9,8},{10,11... | collective-permute-start | bytes 3145736 | tf_op jit(solution)/shard_map/ppermute | solution.py:476
  47.4 3.7 %collective-permute-start.17 = (bf16[2,256,1024]{2,1,0:T(8,128)(2,1)S(1)}, bf16[2,256,1024]{2,1,0:T(8,128)(2,1)S(1)}, u32[]{:S(2)}, u32[]{:S(2)}) collective-permute-start(bf16[2,256,1024]{2,1,0:T(8,128)(2,1)S(1)} %get-tuple-element.120.refs_3_), channel_id=1, source_target_pairs={{0,1},{1,0},{2,3},{3,2},{4,5},{5,4},{6,7},{7,6},{8,9},{9,8},{10,11... | collective-permute-start | bytes 3145736 | tf_op jit(solution)/shard_map/ppermute | solution.py:476
  49.1 2.0 %collective-permute-start.18 = (bf16[2,128,1024]{2,1,0:T(8,128)(2,1)S(1)}, bf16[2,128,1024]{2,1,0:T(8,128)(2,1)S(1)}, u32[]{:S(2)}, u32[]{:S(2)}) collective-permute-start(bf16[2,128,1024]{2,1,0:T(8,128)(2,1)S(1)} %get-tuple-element.125.refs_4_), channel_id=1, source_target_pairs={{0,1},{1,0},{2,3},{3,2},{4,5},{5,4},{6,7},{7,6},{8,9},{9,8},{10,11... | collective-permute-start | bytes 1572872 | tf_op jit(solution)/shard_map/ppermute | solution.py:476
  55.7 22.0 %collective-permute-start.19 = (bf16[40,2048]{1,0:T(8,128)(2,1)S(1)}, bf16[40,2048]{1,0:T(8,128)(2,1)S(1)}, u32[]{:S(2)}, u32[]{:S(2)}) collective-permute-start(bf16[40,2048]{1,0:T(8,128)(2,1)S(1)} %get-tuple-element.150), channel_id=1, source_target_pairs={{0,8},{2,10},{4,12},{6,14},{8,0},{10,2},{12,4},{14,6},{1,9},{3,11}... | collective-permute-start | bytes 491528 | tf_op jit(solution)/shard_map/ppermute | solution.py:516
  56.4 24.6 %collective-permute-start.20 = (bf16[40,2048]{1,0:T(8,128)(2,1)S(1)}, bf16[40,2048]{1,0:T(8,128)(2,1)S(1)}, u32[]{:S(2)}, u32[]{:S(2)}) collective-permute-start(bf16[40,2048]{1,0:T(8,128)(2,1)S(1)} %get-tuple-element.153), channel_id=1, source_target_pairs={{0,10},{2,8},{4,14},{6,12},{8,2},{10,0},{12,6},{14,4},{1,11},{3,9}... | collective-permute-start | bytes 491528 | tf_op jit(solution)/shard_map/ppermute | solution.py:516
  63.7 19.0 %copy-start.7 = (bf16[1040,128]{1,0:T(8,128)(2,1)S(1)}, bf16[1040,128]{1,0:T(8,128)(2,1)}, u32[]{:S(2)}) copy-start(bf16[1040,128]{1,0:T(8,128)(2,1)} %get-tuple-element.82.top_ref.refs_0_) | copy-start | bytes 798724
  63.7 19.0 %copy-start.9 = (bf16[1040,128]{1,0:T(8,128)(2,1)S(1)}, bf16[1040,128]{1,0:T(8,128)(2,1)}, u32[]{:S(2)}) copy-start(bf16[1040,128]{1,0:T(8,128)(2,1)} %get-tuple-element.83.bottom_ref.refs_1_) | copy-start | bytes 798724
  63.7 19.0 %copy-start.10 = (f32[2048,8]{0,1:T(8,128)S(1)}, f32[2048,8]{0,1:T(8,128)}, u32[]{:S(2)}) copy-start(f32[2048,8]{0,1:T(8,128)} %param.10) | copy-start | bytes 196612
  63.7 19.5 %collective-permute-start.21 = (bf16[40,2048]{1,0:T(8,128)(2,1)S(1)}, bf16[40,2048]{1,0:T(8,128)(2,1)S(1)}, u32[]{:S(2)}, u32[]{:S(2)}) collective-permute-start(bf16[40,2048]{1,0:T(8,128)(2,1)S(1)} %get-tuple-element.154), channel_id=1, source_target_pairs={{0,12},{2,14},{4,8},{6,10},{8,4},{10,6},{12,0},{14,2},{1,13},{3,15... | collective-permute-start | bytes 491528 | tf_op jit(solution)/shard_map/ppermute | solution.py:516
  63.8 19.4 %collective-permute-start.22 = (bf16[40,2048]{1,0:T(8,128)(2,1)S(1)}, bf16[40,2048]{1,0:T(8,128)(2,1)S(1)}, u32[]{:S(2)}, u32[]{:S(2)}) collective-permute-start(bf16[40,2048]{1,0:T(8,128)(2,1)S(1)} %get-tuple-element.155), channel_id=1, source_target_pairs={{0,14},{2,12},{4,10},{6,8},{8,6},{10,4},{12,2},{14,0},{1,15},{3,13... | collective-permute-start | bytes 491528 | tf_op jit(solution)/shard_map/ppermute | solution.py:516
  77.7 8.0 %collective-permute-start.23 = (bf16[40,2048]{1,0:T(8,128)(2,1)S(1)}, bf16[40,2048]{1,0:T(8,128)(2,1)S(1)}, u32[]{:S(2)}, u32[]{:S(2)}) collective-permute-start(bf16[40,2048]{1,0:T(8,128)(2,1)S(1)} %get-tuple-element.156), channel_id=1, source_target_pairs={{0,6},{2,4},{4,2},{6,0},{8,14},{10,12},{12,10},{14,8},{1,7},{3,5},... | collective-permute-start | bytes 491528 | tf_op jit(solution)/shard_map/ppermute | solution.py:516
  77.7 10.0 %collective-permute-start.24 = (bf16[40,2048]{1,0:T(8,128)(2,1)S(1)}, bf16[40,2048]{1,0:T(8,128)(2,1)S(1)}, u32[]{:S(2)}, u32[]{:S(2)}) collective-permute-start(bf16[40,2048]{1,0:T(8,128)(2,1)S(1)} %get-tuple-element.157), channel_id=1, source_target_pairs={{0,4},{2,6},{4,0},{6,2},{8,12},{10,14},{12,8},{14,10},{1,5},{3,7},... | collective-permute-start | bytes 491528 | tf_op jit(solution)/shard_map/ppermute | solution.py:516
  81.0 6.7 %collective-permute-start.25 = (bf16[40,2048]{1,0:T(8,128)(2,1)S(1)}, bf16[40,2048]{1,0:T(8,128)(2,1)S(1)}, u32[]{:S(2)}, u32[]{:S(2)}) collective-permute-start(bf16[40,2048]{1,0:T(8,128)(2,1)S(1)} %get-tuple-element.158), channel_id=1, source_target_pairs={{0,2},{2,0},{4,6},{6,4},{8,10},{10,8},{12,14},{14,12},{1,3},{3,1},... | collective-permute-start | bytes 491528 | tf_op jit(solution)/shard_map/ppermute | solution.py:516
where the time goes:
time: 89.3 us; the launch traced here: 89 us
  Pallas kernels  33.2 us (37%)
  starting transfers between devices  27.1 us (30%)
  waiting for transfers between devices  21.9 us (25%)
  local copies, waits for them, and re-layouts  6.31 us (7%)
    pallas_call x3, Pallas kernels, attend(): pl.pallas_call(functools.partial(attend_kernel, lots, heads), in_specs=[W...  13.9 us
    ppermute x7, starting transfers between devices, swap(): return lax.ppermute(piece, 'ctx', [(c, c ^ k) for c in range(ctx_count)])  11.3 us
    ppermute x7, starting transfers between devices, send(): lax.ppermute(parts[0], 'ctx', forward)  11.1 us
    ppermute x7, waiting for transfers between devices, send(): lax.ppermute(parts[1], 'ctx', backward)  11 us
    ppermute x7, waiting for transfers between devices, swap(): return lax.ppermute(piece, 'ctx', [(c, c ^ k) for c in range(ctx_count)])  9.18 us
    unnamed x22, local copies, waits for them, and re-layouts  6.31 us
    pallas_call x5, Pallas kernels, project_values(): pl.pallas_call(functools.partial(values_kernel, half, offsets, len(blocks...  6.14 us
    pallas_call x5, Pallas kernels, project_keys(): pl.pallas_call(functools.partial(keys_kernel, half, len(blocks)), in_spec...  5.3 us
  transfers between devices with their start and end apart: 26, of which 16 were waited for; matrix products, arithmetic and copies ran while one was open for 0% of the time, Pallas kernels for 29%

commit v1 on v0

--- a/solution.py
+++ b/solution.py
@@ -400,7 +400,11 @@
 
 
 def combine_kernel(ahead_count, mix_ref, *refs):
-    *refs, out_ref, held, sent = refs
+    if ahead_count > 0:
+        *refs, out_ref, held, sent = refs
+    else:
+        *refs, held = refs
+        out_ref = held
     ahead, pieces = refs[:ahead_count], refs[ahead_count:]
     tok_count, model_width = out_ref.shape
     copies = []
@@ -419,10 +423,11 @@
         for ref in ahead:
             total = total + ref[:, cols]
         held[:, cols] = total.astype(held.dtype)
-        copies.append(
-            pltpu.make_async_copy(held.at[:, cols], out_ref.at[:, cols], sent.at[len(copies)])
-        )
-        copies[-1].start()
+        if ahead_count > 0:
+            copies.append(
+                pltpu.make_async_copy(held.at[:, cols], out_ref.at[:, cols], sent.at[len(copies)])
+            )
+            copies[-1].start()
     for copy in copies:
         copy.wait()
 
@@ -430,15 +435,16 @@
 def combine(mix, pieces, ahead, dtype):
     tok_count = mix.shape[0] // TERMS
     model_width = pieces[0].shape[1]
+    scratch = [
+        pltpu.VMEM((tok_count, model_width), dtype),
+        pltpu.SemaphoreType.DMA((-(-model_width // 512),)),
+    ]
     return pl.pallas_call(
         functools.partial(combine_kernel, len(ahead)),
         in_specs=[WHOLE] * (1 + len(ahead) + len(pieces)),
-        out_specs=pl.BlockSpec(memory_space=pl.ANY),
+        out_specs=pl.BlockSpec(memory_space=pl.ANY) if ahead else WHOLE,
         out_shape=jax.ShapeDtypeStruct((tok_count, model_width), dtype),
-        scratch_shapes=[
-            pltpu.VMEM((tok_count, model_width), dtype),
-            pltpu.SemaphoreType.DMA((-(-model_width // 512),)),
-        ],
+        scratch_shapes=scratch if ahead else [],
         compiler_params=pltpu.CompilerParams(vmem_limit_bytes=24 * MIB),
         name="combine",
     )(mix, *ahead, *pieces)
@@ -522,6 +528,8 @@
         if start > 0:
             places, *pieces = tie(held[2], *pieces)
             held = [*held[:2], places]
+            if far:
+                pieces[-1], far[0][0] = tie(pieces[-1], far[0][0])
             far.append([swap(piece, start + r) for r, piece in enumerate(pieces)])
         else:
             near = pieces

time: 89.3 us -> 91 us (1.019)
  waiting for transfers between devices: 21.9 us -> 25.5 us
  starting transfers between devices: 27.1 us -> 25.6 us
    ppermute x7, waiting for transfers between devices: 9.18 us -> 12.8 us  [swap(): return lax.ppermute(piece, 'ctx', [(c, c ^ k) for c in range(ctx_count)])]
    ppermute x7, starting transfers between devices: 11.3 us -> 9.74 us  [swap(): return lax.ppermute(piece, 'ctx', [(c, c ^ k) for c in range(ctx_count)])]
  transfers between devices with their start and end apart: 26 -> 26, of which waited for: 16 -> 17; matrix products, arithmetic and copies ran while one was open for 0% -> 0% of each run, Pallas kernels for 29% -> 27%
where the time goes in v1:
time: 91 us; the launch traced here: 90.7 us
  Pallas kernels  32.9 us (36%)
  starting transfers between devices  25.6 us (28%)
  waiting for transfers between devices  25.5 us (28%)
  local copies, waits for them, and re-layouts  6.31 us (7%)
    pallas_call x3, Pallas kernels, attend(): pl.pallas_call(functools.partial(attend_kernel, lots, heads), in_specs=[W...  14.1 us
    ppermute x7, waiting for transfers between devices, swap(): return lax.ppermute(piece, 'ctx', [(c, c ^ k) for c in range(ctx_count)])  12.8 us
    ppermute x7, starting transfers between devices, send(): lax.ppermute(parts[0], 'ctx', forward)  11.1 us
    ppermute x7, waiting for transfers between devices, send(): lax.ppermute(parts[1], 'ctx', backward)  11 us
    ppermute x7, starting transfers between devices, swap(): return lax.ppermute(piece, 'ctx', [(c, c ^ k) for c in range(ctx_count)])  9.74 us
    unnamed x22, local copies, waits for them, and re-layouts  6.31 us
    pallas_call x5, Pallas kernels, project_values(): pl.pallas_call(functools.partial(values_kernel, half, offsets, len(blocks...  6.14 us
    pallas_call x5, Pallas kernels, project_keys(): pl.pallas_call(functools.partial(keys_kernel, half, len(blocks)), in_spec...  5.3 us
  transfers between devices with their start and end apart: 26, of which 17 were waited for; matrix products, arithmetic and copies ran while one was open for 0% of the time, Pallas kernels for 27%

profile of v1, /device:TPU:0, one launch (start us, length us, event | category | flops | bytes accessed | tf_op | source)
XLA Modules:
  0.0 90.7 jit_solution(7829666313059971464)
XLA Ops:
  0.0 2.0 %norm_rows.1 = (bf16[1040,128]{1,0:T(8,128)(2,1)}, bf16[1040,128]{1,0:T(8,128)(2,1)}) custom-call(bf16[128,2048]{1,0:T(8,128)(2,1)} %refs_0_.1, f32[1,2048]{1,0:T(1,128)} %bitcast.15, s32[2,128]{1,0:T(2,128)} %bitcast.16), custom_call_target="tpu_custom_call" | custom-call | tf_op jit(solution)/shard_map/norm_rows/pallas_call | solution.py:85
  2.0 3.1 %collective-permute-start = (bf16[1040,128]{1,0:T(8,128)(2,1)}, bf16[1040,128]{1,0:T(8,128)(2,1)S(1)}, u32[]{:S(2)}, u32[]{:S(2)}) collective-permute-start(bf16[1040,128]{1,0:T(8,128)(2,1)} %get-tuple-element.84.top_ref.refs_0_), channel_id=1, source_target_pairs={{0,4},{4,8},{8,12},{12,14},{14,10},{10,6},{6,2},{2,0},{1,5},{5,9},... | collective-permute-start | bytes 798728 | tf_op jit(solution)/shard_map/ppermute | solution.py:479
  5.1 0.0 collective-permute-start.1
  5.1 2.0 %collective-permute-start.3 = (bf16[1040,128]{1,0:T(8,128)(2,1)}, bf16[1040,128]{1,0:T(8,128)(2,1)S(1)}, u32[]{:S(2)}, u32[]{:S(2)}) collective-permute-start(bf16[1040,128]{1,0:T(8,128)(2,1)} %get-tuple-element.84.top_ref.refs_0_), channel_id=1, source_target_pairs={{4,0},{8,4},{12,8},{14,12},{10,14},{6,10},{2,6},{0,2},{5,1},{9,5},... | collective-permute-start | bytes 798728 | tf_op jit(solution)/shard_map/ppermute | solution.py:479
  7.1 0.1 collective-permute-start.2
  7.2 2.2 %copy-done.1 = bf16[2048,1024]{1,0:T(8,128)(2,1)S(1)} copy-done((bf16[2048,1024]{1,0:T(8,128)(2,1)S(1)}, bf16[2048,1024]{1,0:T(8,128)(2,1)}, u32[]{:S(2)}) %copy-start.1) | copy-done | bytes 4194328
  9.4 0.9 %copy-done.6 = bf16[1040,128]{1,0:T(8,128)(2,1)S(1)} copy-done((bf16[1040,128]{1,0:T(8,128)(2,1)S(1)}, bf16[1040,128]{1,0:T(8,128)(2,1)}, u32[]{:S(2)}) %copy-start.6) | copy-done | bytes 266264
  10.3 0.9 %copy-done.8 = bf16[1040,128]{1,0:T(8,128)(2,1)S(1)} copy-done((bf16[1040,128]{1,0:T(8,128)(2,1)S(1)}, bf16[1040,128]{1,0:T(8,128)(2,1)}, u32[]{:S(2)}) %copy-start.8) | copy-done | bytes 266264
  11.3 0.7 project_keys.5
  12.0 0.5 collective-permute-done.refs_0_
  12.5 2.2 %collective-permute-done.1.refs_3_ = bf16[1040,128]{1,0:T(8,128)(2,1)S(1)} collective-permute-done((bf16[1040,128]{1,0:T(8,128)(2,1)}, bf16[1040,128]{1,0:T(8,128)(2,1)S(1)}, u32[]{:S(2)}, u32[]{:S(2)}) %collective-permute-start.1) | collective-permute-done | bytes 266272 | tf_op jit(solution)/shard_map/ppermute | solution.py:479
  14.6 1.6 %collective-permute-start.4 = (bf16[1040,128]{1,0:T(8,128)(2,1)S(1)}, bf16[1040,128]{1,0:T(8,128)(2,1)S(1)}, u32[]{:S(2)}, u32[]{:S(2)}) collective-permute-start(bf16[1040,128]{1,0:T(8,128)(2,1)S(1)} %collective-permute-done.refs_0_), channel_id=1, source_target_pairs={{0,4},{4,8},{8,12},{12,14},{14,10},{10,6},{6,2},{2,0},{1,5},{5,9},... | collective-permute-start | bytes 798728 | tf_op jit(solution)/shard_map/ppermute | solution.py:479
  16.2 0.4 collective-permute-start.5
  16.7 2.2 %copy-done.3 = bf16[2048,1024]{1,0:T(8,128)(2,1)S(1)} copy-done((bf16[2048,1024]{1,0:T(8,128)(2,1)S(1)}, bf16[2048,1024]{1,0:T(8,128)(2,1)}, u32[]{:S(2)}) %copy-start.3) | copy-done | bytes 4194328
  18.9 0.8 project_values.5
  19.7 0.6 collective-permute-done.3.refs_2_
  20.4 1.6 %collective-permute-start.6 = (bf16[1040,128]{1,0:T(8,128)(2,1)S(1)}, bf16[1040,128]{1,0:T(8,128)(2,1)S(1)}, u32[]{:S(2)}, u32[]{:S(2)}) collective-permute-start(bf16[1040,128]{1,0:T(8,128)(2,1)S(1)} %collective-permute-done.2.refs_1_), channel_id=1, source_target_pairs={{0,4},{4,8},{8,12},{12,14},{14,10},{10,6},{6,2},{2,0},{1,5},{5,9},... | collective-permute-start | bytes 798728 | tf_op jit(solution)/shard_map/ppermute | solution.py:479
  21.9 0.4 collective-permute-start.7
  22.4 1.3 %project_keys.6 = (bf16[256,1024]{1,0:T(8,128)(2,1)S(1)}, f32[8,128]{1,0:T(8,128)S(1)}) custom-call(bf16[1040,128]{1,0:T(8,128)(2,1)S(1)} %collective-permute-done.refs_0_, bf16[1040,128]{1,0:T(8,128)(2,1)S(1)} %collective-permute-done.2.refs_1_, bf16[1040,128]{1,0:T(8,128)(2,1)S(1)} %collective-permute-done.3.refs_2_, ...), custom_call_target="tpu_custom_call" | custom-call | tf_op jit(solution)/shard_map/project_keys/pallas_call | solution.py:115
  23.7 0.3 collective-permute-done.4.refs_0_
  24.0 2.1 %collective-permute-done.5.refs_3_ = bf16[1040,128]{1,0:T(8,128)(2,1)S(1)} collective-permute-done((bf16[1040,128]{1,0:T(8,128)(2,1)S(1)}, bf16[1040,128]{1,0:T(8,128)(2,1)S(1)}, u32[]{:S(2)}, u32[]{:S(2)}) %collective-permute-start.5) | collective-permute-done | bytes 266272 | tf_op jit(solution)/shard_map/ppermute | solution.py:479
  26.1 1.6 %collective-permute-start.8 = (bf16[1040,128]{1,0:T(8,128)(2,1)S(1)}, bf16[1040,128]{1,0:T(8,128)(2,1)S(1)}, u32[]{:S(2)}, u32[]{:S(2)}) collective-permute-start(bf16[1040,128]{1,0:T(8,128)(2,1)S(1)} %collective-permute-done.4.refs_0_), channel_id=1, source_target_pairs={{0,4},{4,8},{8,12},{12,14},{14,10},{10,6},{6,2},{2,0},{1,5},{5,9},... | collective-permute-start | bytes 798728 | tf_op jit(solution)/shard_map/ppermute | solution.py:479
  27.6 0.4 collective-permute-start.9
  28.1 1.5 %project_values.6 = (bf16[2,256,1024]{2,1,0:T(8,128)(2,1)S(1)}, bf16[2,48,2048]{2,1,0:T(8,128)(2,1)S(1)}, f32[2,48,128]{2,1,0:T(8,128)S(1)}) custom-call(f32[8,128]{1,0:T(8,128)S(1)} %get-tuple-element.95.mark_ref, bf16[256,1024]{1,0:T(8,128)(2,1)S(1)} %get-tuple-element.96.keys_ref, bf16[1040,128]{1,0:T(8,128)(2,1)S(1)} %collective-permute-done.refs_0_, ...), custom_call_target="tpu_custom_call" | custom-call | tf_op jit(solution)/shard_map/project_values/pallas_call | solution.py:160
  29.6 0.1 collective-permute-done.6.refs_1_
  29.7 2.1 %collective-permute-done.7.refs_2_ = bf16[1040,128]{1,0:T(8,128)(2,1)S(1)} collective-permute-done((bf16[1040,128]{1,0:T(8,128)(2,1)S(1)}, bf16[1040,128]{1,0:T(8,128)(2,1)S(1)}, u32[]{:S(2)}, u32[]{:S(2)}) %collective-permute-start.7) | collective-permute-done | bytes 266272 | tf_op jit(solution)/shard_map/ppermute | solution.py:479
  31.8 1.6 %collective-permute-start.10 = (bf16[1040,128]{1,0:T(8,128)(2,1)S(1)}, bf16[1040,128]{1,0:T(8,128)(2,1)S(1)}, u32[]{:S(2)}, u32[]{:S(2)}) collective-permute-start(bf16[1040,128]{1,0:T(8,128)(2,1)S(1)} %collective-permute-done.6.refs_1_), channel_id=1, source_target_pairs={{0,4},{4,8},{8,12},{12,14},{14,10},{10,6},{6,2},{2,0},{1,5},{5,9},... | collective-permute-start | bytes 798728 | tf_op jit(solution)/shard_map/ppermute | solution.py:479
  33.3 0.4 collective-permute-start.11
  33.8 0.8 project_queries.3
  34.6 1.3 %project_keys.7 = (bf16[256,1024]{1,0:T(8,128)(2,1)S(1)}, f32[8,128]{1,0:T(8,128)S(1)}) custom-call(bf16[1040,128]{1,0:T(8,128)(2,1)S(1)} %collective-permute-done.4.refs_0_, bf16[1040,128]{1,0:T(8,128)(2,1)S(1)} %collective-permute-done.6.refs_1_, bf16[1040,128]{1,0:T(8,128)(2,1)S(1)} %collective-permute-done.7.refs_2_, ...), custom_call_target="tpu_custom_call" | custom-call | tf_op jit(solution)/shard_map/project_keys/pallas_call | solution.py:115
  35.9 1.6 %collective-permute-done.9.refs_3_ = bf16[1040,128]{1,0:T(8,128)(2,1)S(1)} collective-permute-done((bf16[1040,128]{1,0:T(8,128)(2,1)S(1)}, bf16[1040,128]{1,0:T(8,128)(2,1)S(1)}, u32[]{:S(2)}, u32[]{:S(2)}) %collective-permute-start.9) | collective-permute-done | bytes 266272 | tf_op jit(solution)/shard_map/ppermute | solution.py:479
  37.5 1.6 %collective-permute-start.13 = (bf16[1040,128]{1,0:T(8,128)(2,1)S(1)}, bf16[1040,128]{1,0:T(8,128)(2,1)S(1)}, u32[]{:S(2)}, u32[]{:S(2)}) collective-permute-start(bf16[1040,128]{1,0:T(8,128)(2,1)S(1)} %collective-permute-done.8.refs_0_), channel_id=1, source_target_pairs={{0,4},{4,8},{8,12},{12,14},{14,10},{10,6},{6,2},{2,0},{1,5},{5,9},... | collective-permute-start | bytes 798728 | tf_op jit(solution)/shard_map/ppermute | solution.py:479
  39.0 0.4 collective-permute-start.14
  39.5 1.5 %project_values.7 = (bf16[2,256,1024]{2,1,0:T(8,128)(2,1)S(1)}, bf16[2,48,2048]{2,1,0:T(8,128)(2,1)S(1)}, f32[2,48,128]{2,1,0:T(8,128)S(1)}) custom-call(f32[8,128]{1,0:T(8,128)S(1)} %get-tuple-element.108.mark_ref, bf16[256,1024]{1,0:T(8,128)(2,1)S(1)} %get-tuple-element.109.keys_ref, bf16[1040,128]{1,0:T(8,128)(2,1)S(1)} %collective-permute-done.4.refs_0_, ...), custom_call_target="tpu_custom_call" | custom-call | tf_op jit(solution)/shard_map/project_values/pallas_call | solution.py:160
  41.0 0.1 collective-permute-done.10.refs_1_
  41.1 2.1 %collective-permute-done.11.refs_2_ = bf16[1040,128]{1,0:T(8,128)(2,1)S(1)} collective-permute-done((bf16[1040,128]{1,0:T(8,128)(2,1)S(1)}, bf16[1040,128]{1,0:T(8,128)(2,1)S(1)}, u32[]{:S(2)}, u32[]{:S(2)}) %collective-permute-start.11) | collective-permute-done | bytes 266272 | tf_op jit(solution)/shard_map/ppermute | solution.py:479
  43.2 1.3 %project_keys.8 = (bf16[256,1024]{1,0:T(8,128)(2,1)S(1)}, f32[8,128]{1,0:T(8,128)S(1)}) custom-call(bf16[1040,128]{1,0:T(8,128)(2,1)S(1)} %collective-permute-done.8.refs_0_, bf16[1040,128]{1,0:T(8,128)(2,1)S(1)} %collective-permute-done.10.refs_1_, bf16[1040,128]{1,0:T(8,128)(2,1)S(1)} %collective-permute-done.11.refs_2_, ...), custom_call_target="tpu_custom_call" | custom-call | tf_op jit(solution)/shard_map/project_keys/pallas_call | solution.py:115
  44.5 1.5 %project_values.8 = (bf16[2,256,1024]{2,1,0:T(8,128)(2,1)S(1)}, bf16[2,48,2048]{2,1,0:T(8,128)(2,1)S(1)}, f32[2,48,128]{2,1,0:T(8,128)S(1)}) custom-call(f32[8,128]{1,0:T(8,128)S(1)} %get-tuple-element.114.mark_ref, bf16[256,1024]{1,0:T(8,128)(2,1)S(1)} %get-tuple-element.115.keys_ref, bf16[1040,128]{1,0:T(8,128)(2,1)S(1)} %collective-permute-done.8.refs_0_, ...), custom_call_target="tpu_custom_call" | custom-call | tf_op jit(solution)/shard_map/project_values/pallas_call | solution.py:160
  46.0 1.0 %project_queries.4 = (bf16[2,48,1024]{2,1,0:T(8,128)(2,1)S(1)}, bf16[2,48,1024]{2,1,0:T(8,128)(2,1)S(1)}) custom-call(bf16[2,48,2048]{2,1,0:T(8,128)(2,1)S(1)} %get-tuple-element.117.refs_0_, bf16[2,48,2048]{2,1,0:T(8,128)(2,1)S(1)} %get-tuple-element.118.refs_1_, bf16[2048,1024]{1,0:T(8,128)(2,1)S(1)} %bitcast.12, bf16[1024,2048]{1,0:T(8,128)(2,1)S(1)} %bitcast.6), custom_call_target="tpu_custom_call" | custom-call | tf_op jit(solution)/shard_map/project_queries/pallas_call | solution.py:189
  47.0 0.4 collective-permute-done.14.refs_1_
  47.4 0.1 collective-permute-start.17
  47.6 0.7 project_keys.9
  48.3 0.8 project_values.9
  49.1 0.4 collective-permute-start.18
  49.5 0.8 project_queries.5.refs_14_
  50.4 0.7 collective-permute-done.18.refs_9_
  51.1 0.7 arrange.1
  51.8 4.1 %attend.3 = (bf16[40,2048]{1,0:T(8,128)(2,1)S(1)}, bf16[40,2048]{1,0:T(8,128)(2,1)S(1)}) custom-call(bf16[2,16,128,1024]{3,2,1,0:T(8,128)(2,1)S(1)} %get-tuple-element.139.panel_ref, f32[8,40,1024]{2,1,0:T(8,128)S(1)} %get-tuple-element.140.queries_ref, f32[8,40,128]{2,1,0:T(8,128)S(1)} %get-tuple-element.147.places_ref, bf16[1024,2048]{1,0:T(8,128)(2,1)S(1)} %bitcast.8), custom_call_target="tpu_custom_call" | custom-call | flops 1207959552 | bytes 8388608 | tf_op jit(solution)/shard_map/attend/pallas_call | solution.py:326
  55.9 0.7 collective-permute-start.19
  56.6 2.0 %collective-permute-start.20 = (bf16[40,2048]{1,0:T(8,128)(2,1)S(1)}, bf16[40,2048]{1,0:T(8,128)(2,1)S(1)}, u32[]{:S(2)}, u32[]{:S(2)}) collective-permute-start(bf16[40,2048]{1,0:T(8,128)(2,1)S(1)} %get-tuple-element.157), channel_id=1, source_target_pairs={{0,10},{2,8},{4,14},{6,12},{8,2},{10,0},{12,6},{14,4},{1,11},{3,9}... | collective-permute-start | bytes 491528 | tf_op jit(solution)/shard_map/ppermute | solution.py:522
  58.6 5.3 %attend.4 = (bf16[40,2048]{1,0:T(8,128)(2,1)S(1)}, bf16[40,2048]{1,0:T(8,128)(2,1)S(1)}) custom-call(bf16[2,16,128,1024]{3,2,1,0:T(8,128)(2,1)S(1)} %get-tuple-element.139.panel_ref, f32[8,40,1024]{2,1,0:T(8,128)S(1)} %get-tuple-element.140.queries_ref, f32[8,40,128]{2,1,0:T(8,128)S(1)} %get-tuple-element.147.places_ref, bf16[1024,2048]{1,0:T(8,128)(2,1)S(1)} %bitcast.9), custom_call_target="tpu_custom_call" | custom-call | flops 1207959552 | bytes 8388608 | tf_op jit(solution)/shard_map/attend/pallas_call | solution.py:326
  63.9 0.1 collective-permute-start.21
  64.0 4.7 %attend.5 = (bf16[40,2048]{1,0:T(8,128)(2,1)S(1)}, bf16[40,2048]{1,0:T(8,128)(2,1)S(1)}, bf16[40,2048]{1,0:T(8,128)(2,1)S(1)}, bf16[40,2048]{1,0:T(8,128)(2,1)S(1)}) custom-call(bf16[2,16,128,1024]{3,2,1,0:T(8,128)(2,1)S(1)} %get-tuple-element.139.panel_ref, f32[8,40,1024]{2,1,0:T(8,128)S(1)} %get-tuple-element.140.queries_ref, ...), custom_call_target="tpu_custom_call" | custom-call | flops 2415919104 | bytes 8388608 | tf_op jit(solution)/shard_map/attend/pallas_call | solution.py:326
  68.8 5.7 %collective-permute-done.19.refs_1_ = bf16[40,2048]{1,0:T(8,128)(2,1)S(1)} collective-permute-done((bf16[40,2048]{1,0:T(8,128)(2,1)S(1)}, bf16[40,2048]{1,0:T(8,128)(2,1)S(1)}, u32[]{:S(2)}, u32[]{:S(2)}) %collective-permute-start.19) | collective-permute-done | bytes 163872 | tf_op jit(solution)/shard_map/ppermute | solution.py:522
  74.4 3.5 %collective-permute-start.22 = (bf16[40,2048]{1,0:T(8,128)(2,1)S(1)}, bf16[40,2048]{1,0:T(8,128)(2,1)S(1)}, u32[]{:S(2)}, u32[]{:S(2)}) collective-permute-start(bf16[40,2048]{1,0:T(8,128)(2,1)S(1)} %get-tuple-element.159), channel_id=1, source_target_pairs={{0,14},{2,12},{4,10},{6,8},{8,6},{10,4},{12,2},{14,0},{1,15},{3,13... | collective-permute-start | bytes 491528 | tf_op jit(solution)/shard_map/ppermute | solution.py:522
  77.9 1.7 %collective-permute-start.24 = (bf16[40,2048]{1,0:T(8,128)(2,1)S(1)}, bf16[40,2048]{1,0:T(8,128)(2,1)S(1)}, u32[]{:S(2)}, u32[]{:S(2)}) collective-permute-start(bf16[40,2048]{1,0:T(8,128)(2,1)S(1)} %get-tuple-element.161), channel_id=1, source_target_pairs={{0,4},{2,6},{4,0},{6,2},{8,12},{10,14},{12,8},{14,10},{1,5},{3,7},... | collective-permute-start | bytes 491528 | tf_op jit(solution)/shard_map/ppermute | solution.py:522
  79.7 1.7 %collective-permute-start.25 = (bf16[40,2048]{1,0:T(8,128)(2,1)S(1)}, bf16[40,2048]{1,0:T(8,128)(2,1)S(1)}, u32[]{:S(2)}, u32[]{:S(2)}) collective-permute-start(bf16[40,2048]{1,0:T(8,128)(2,1)S(1)} %get-tuple-element.162), channel_id=1, source_target_pairs={{0,2},{2,0},{4,6},{6,4},{8,10},{10,8},{12,14},{14,12},{1,3},{3,1},... | collective-permute-start | bytes 491528 | tf_op jit(solution)/shard_map/ppermute | solution.py:522
  81.4 0.5 gate_mix.1
  81.9 2.4 %collective-permute-done.22.refs_4_ = bf16[40,2048]{1,0:T(8,128)(2,1)S(1)} collective-permute-done((bf16[40,2048]{1,0:T(8,128)(2,1)S(1)}, bf16[40,2048]{1,0:T(8,128)(2,1)S(1)}, u32[]{:S(2)}, u32[]{:S(2)}) %collective-permute-start.22) | collective-permute-done | bytes 163872 | tf_op jit(solution)/shard_map/ppermute | solution.py:522
  84.3 0.4 combine.2.refs_0_
  84.8 2.2 %collective-permute-done.23.refs_1_ = bf16[40,2048]{1,0:T(8,128)(2,1)S(1)} collective-permute-done((bf16[40,2048]{1,0:T(8,128)(2,1)S(1)}, bf16[40,2048]{1,0:T(8,128)(2,1)S(1)}, u32[]{:S(2)}, u32[]{:S(2)}) %collective-permute-start.23) | collective-permute-done | bytes 163872 | tf_op jit(solution)/shard_map/ppermute | solution.py:522
  86.9 1.5 %collective-permute-done.24.refs_2_ = bf16[40,2048]{1,0:T(8,128)(2,1)S(1)} collective-permute-done((bf16[40,2048]{1,0:T(8,128)(2,1)S(1)}, bf16[40,2048]{1,0:T(8,128)(2,1)S(1)}, u32[]{:S(2)}, u32[]{:S(2)}) %collective-permute-start.24) | collective-permute-done | bytes 163872 | tf_op jit(solution)/shard_map/ppermute | solution.py:522
  88.4 1.0 %collective-permute-done.25.refs_3_ = bf16[40,2048]{1,0:T(8,128)(2,1)S(1)} collective-permute-done((bf16[40,2048]{1,0:T(8,128)(2,1)S(1)}, bf16[40,2048]{1,0:T(8,128)(2,1)S(1)}, u32[]{:S(2)}, u32[]{:S(2)}) %collective-permute-start.25) | collective-permute-done | bytes 163872 | tf_op jit(solution)/shard_map/ppermute | solution.py:522
  89.4 1.1 %combine.3 = bf16[128,2048]{1,0:T(8,128)(2,1)} custom-call(bf16[256,144]{1,0:T(8,128)(2,1)S(1)} %get-tuple-element.86.mix_ref, f32[128,2048]{1,0:T(8,128)S(1)} %combine.2.refs_0_, bf16[40,2048]{1,0:T(8,128)(2,1)S(1)} %collective-permute-done.23.refs_1_, bf16[40,2048]{1,0:T(8,128)(2,1)S(1)} %collective-permute-done.24.refs_2_, ...), custom_call_target="tpu_custom_call" | custom-call | tf_op jit(solution)/shard_map/combine/pallas_call | solution.py:442
  (31 shorter events, 0.1 us)
Async XLA Ops:
  2.0 10.5 %collective-permute-start = (bf16[1040,128]{1,0:T(8,128)(2,1)}, bf16[1040,128]{1,0:T(8,128)(2,1)S(1)}, u32[]{:S(2)}, u32[]{:S(2)}) collective-permute-start(bf16[1040,128]{1,0:T(8,128)(2,1)} %get-tuple-element.84.top_ref.refs_0_), channel_id=1, source_target_pairs={{0,4},{4,8},{8,12},{12,14},{14,10},{10,6},{6,2},{2,0},{1,5},{5,9},... | collective-permute-start | bytes 798728 | tf_op jit(solution)/shard_map/ppermute | solution.py:479
  5.1 9.5 %collective-permute-start.1 = (bf16[1040,128]{1,0:T(8,128)(2,1)}, bf16[1040,128]{1,0:T(8,128)(2,1)S(1)}, u32[]{:S(2)}, u32[]{:S(2)}) collective-permute-start(bf16[1040,128]{1,0:T(8,128)(2,1)} %get-tuple-element.85.bottom_ref.refs_1_), channel_id=1, source_target_pairs={{4,0},{8,4},{12,8},{14,12},{10,14},{6,10},{2,6},{0,2},{5,1},{9,5},... | collective-permute-start | bytes 798728 | tf_op jit(solution)/shard_map/ppermute | solution.py:479
  5.1 15.2 %collective-permute-start.3 = (bf16[1040,128]{1,0:T(8,128)(2,1)}, bf16[1040,128]{1,0:T(8,128)(2,1)S(1)}, u32[]{:S(2)}, u32[]{:S(2)}) collective-permute-start(bf16[1040,128]{1,0:T(8,128)(2,1)} %get-tuple-element.84.top_ref.refs_0_), channel_id=1, source_target_pairs={{4,0},{8,4},{12,8},{14,12},{10,14},{6,10},{2,6},{0,2},{5,1},{9,5},... | collective-permute-start | bytes 798728 | tf_op jit(solution)/shard_map/ppermute | solution.py:479
  7.1 13.3 %collective-permute-start.2 = (bf16[1040,128]{1,0:T(8,128)(2,1)}, bf16[1040,128]{1,0:T(8,128)(2,1)S(1)}, u32[]{:S(2)}, u32[]{:S(2)}) collective-permute-start(bf16[1040,128]{1,0:T(8,128)(2,1)} %get-tuple-element.85.bottom_ref.refs_1_), channel_id=1, source_target_pairs={{0,4},{4,8},{8,12},{12,14},{14,10},{10,6},{6,2},{2,0},{1,5},{5,9},... | collective-permute-start | bytes 798728 | tf_op jit(solution)/shard_map/ppermute | solution.py:479
  7.2 2.2 %copy-start.1 = (bf16[2048,1024]{1,0:T(8,128)(2,1)S(1)}, bf16[2048,1024]{1,0:T(8,128)(2,1)}, u32[]{:S(2)}) copy-start(bf16[2048,1024]{1,0:T(8,128)(2,1)} %refs_2_.6) | copy-start | bytes 12582916
  9.4 1.0 %copy-start.6 = (bf16[1040,128]{1,0:T(8,128)(2,1)S(1)}, bf16[1040,128]{1,0:T(8,128)(2,1)}, u32[]{:S(2)}) copy-start(bf16[1040,128]{1,0:T(8,128)(2,1)} %get-tuple-element.84.top_ref.refs_0_) | copy-start | bytes 798724
  10.3 1.0 %copy-start.8 = (bf16[1040,128]{1,0:T(8,128)(2,1)S(1)}, bf16[1040,128]{1,0:T(8,128)(2,1)}, u32[]{:S(2)}) copy-start(bf16[1040,128]{1,0:T(8,128)(2,1)} %get-tuple-element.85.bottom_ref.refs_1_) | copy-start | bytes 798724
  11.3 11.1 %copy-start.2 = (bf16[2048,1024]{1,0:T(8,128)(2,1)S(1)}, bf16[2048,1024]{1,0:T(8,128)(2,1)}, u32[]{:S(2)}) copy-start(bf16[2048,1024]{1,0:T(8,128)(2,1)} %refs_2_.6) | copy-start | bytes 12582916
  14.6 9.3 %collective-permute-start.4 = (bf16[1040,128]{1,0:T(8,128)(2,1)S(1)}, bf16[1040,128]{1,0:T(8,128)(2,1)S(1)}, u32[]{:S(2)}, u32[]{:S(2)}) collective-permute-start(bf16[1040,128]{1,0:T(8,128)(2,1)S(1)} %collective-permute-done.refs_0_), channel_id=1, source_target_pairs={{0,4},{4,8},{8,12},{12,14},{14,10},{10,6},{6,2},{2,0},{1,5},{5,9},... | collective-permute-start | bytes 798728 | tf_op jit(solution)/shard_map/ppermute | solution.py:479
  16.2 9.8 %collective-permute-start.5 = (bf16[1040,128]{1,0:T(8,128)(2,1)S(1)}, bf16[1040,128]{1,0:T(8,128)(2,1)S(1)}, u32[]{:S(2)}, u32[]{:S(2)}) collective-permute-start(bf16[1040,128]{1,0:T(8,128)(2,1)S(1)} %collective-permute-done.1.refs_3_), channel_id=1, source_target_pairs={{4,0},{8,4},{12,8},{14,12},{10,14},{6,10},{2,6},{0,2},{5,1},{9,5},... | collective-permute-start | bytes 798728 | tf_op jit(solution)/shard_map/ppermute | solution.py:479
  16.7 2.2 %copy-start.3 = (bf16[2048,1024]{1,0:T(8,128)(2,1)S(1)}, bf16[2048,1024]{1,0:T(8,128)(2,1)}, u32[]{:S(2)}) copy-start(bf16[2048,1024]{1,0:T(8,128)(2,1)} %refs_2_.7) | copy-start | bytes 12582916
  18.9 9.2 %copy-start.4 = (bf16[2048,1024]{1,0:T(8,128)(2,1)S(1)}, bf16[2048,1024]{1,0:T(8,128)(2,1)}, u32[]{:S(2)}) copy-start(bf16[2048,1024]{1,0:T(8,128)(2,1)} %refs_2_.7) | copy-start | bytes 12582916
  20.4 9.3 %collective-permute-start.6 = (bf16[1040,128]{1,0:T(8,128)(2,1)S(1)}, bf16[1040,128]{1,0:T(8,128)(2,1)S(1)}, u32[]{:S(2)}, u32[]{:S(2)}) collective-permute-start(bf16[1040,128]{1,0:T(8,128)(2,1)S(1)} %collective-permute-done.2.refs_1_), channel_id=1, source_target_pairs={{0,4},{4,8},{8,12},{12,14},{14,10},{10,6},{6,2},{2,0},{1,5},{5,9},... | collective-permute-start | bytes 798728 | tf_op jit(solution)/shard_map/ppermute | solution.py:479
  21.9 9.8 %collective-permute-start.7 = (bf16[1040,128]{1,0:T(8,128)(2,1)S(1)}, bf16[1040,128]{1,0:T(8,128)(2,1)S(1)}, u32[]{:S(2)}, u32[]{:S(2)}) collective-permute-start(bf16[1040,128]{1,0:T(8,128)(2,1)S(1)} %collective-permute-done.3.refs_2_), channel_id=1, source_target_pairs={{4,0},{8,4},{12,8},{14,12},{10,14},{6,10},{2,6},{0,2},{5,1},{9,5},... | collective-permute-start | bytes 798728 | tf_op jit(solution)/shard_map/ppermute | solution.py:479
  22.4 11.4 %copy-start.5 = (bf16[1,2048,1024]{2,1,0:T(8,128)(2,1)S(1)}, bf16[1,2048,1024]{2,1,0:T(8,128)(2,1)}, u32[]{:S(2)}) copy-start(bf16[1,2048,1024]{2,1,0:T(8,128)(2,1)} %param.14) | copy-start | bytes 12582916
  23.7 10.1 %copy-start = (bf16[1,1024,2048]{2,1,0:T(8,128)(2,1)S(1)}, bf16[1,1024,2048]{2,1,0:T(8,128)(2,1)}, u32[]{:S(2)}) copy-start(bf16[1,1024,2048]{2,1,0:T(8,128)(2,1)} %param.15) | copy-start | bytes 12582916
  26.1 9.8 %collective-permute-start.8 = (bf16[1040,128]{1,0:T(8,128)(2,1)S(1)}, bf16[1040,128]{1,0:T(8,128)(2,1)S(1)}, u32[]{:S(2)}, u32[]{:S(2)}) collective-permute-start(bf16[1040,128]{1,0:T(8,128)(2,1)S(1)} %collective-permute-done.4.refs_0_), channel_id=1, source_target_pairs={{0,4},{4,8},{8,12},{12,14},{14,10},{10,6},{6,2},{2,0},{1,5},{5,9},... | collective-permute-start | bytes 798728 | tf_op jit(solution)/shard_map/ppermute | solution.py:479
  27.6 9.8 %collective-permute-start.9 = (bf16[1040,128]{1,0:T(8,128)(2,1)S(1)}, bf16[1040,128]{1,0:T(8,128)(2,1)S(1)}, u32[]{:S(2)}, u32[]{:S(2)}) collective-permute-start(bf16[1040,128]{1,0:T(8,128)(2,1)S(1)} %collective-permute-done.5.refs_3_), channel_id=1, source_target_pairs={{4,0},{8,4},{12,8},{14,12},{10,14},{6,10},{2,6},{0,2},{5,1},{9,5},... | collective-permute-start | bytes 798728 | tf_op jit(solution)/shard_map/ppermute | solution.py:479
  28.1 18.9 %collective-permute-start.12 = (bf16[2,128,1024]{2,1,0:T(8,128)(2,1)S(1)}, bf16[2,128,1024]{2,1,0:T(8,128)(2,1)S(1)}, u32[]{:S(2)}, u32[]{:S(2)}) collective-permute-start(bf16[2,128,1024]{2,1,0:T(8,128)(2,1)S(1)} %get-tuple-element.91.refs_0_), channel_id=1, source_target_pairs={{0,1},{1,0},{2,3},{3,2},{4,5},{5,4},{6,7},{7,6},{8,9},{9,8},{10,11... | collective-permute-start | bytes 1572872 | tf_op jit(solution)/shard_map/ppermute | solution.py:482
  31.8 9.3 %collective-permute-start.10 = (bf16[1040,128]{1,0:T(8,128)(2,1)S(1)}, bf16[1040,128]{1,0:T(8,128)(2,1)S(1)}, u32[]{:S(2)}, u32[]{:S(2)}) collective-permute-start(bf16[1040,128]{1,0:T(8,128)(2,1)S(1)} %collective-permute-done.6.refs_1_), channel_id=1, source_target_pairs={{0,4},{4,8},{8,12},{12,14},{14,10},{10,6},{6,2},{2,0},{1,5},{5,9},... | collective-permute-start | bytes 798728 | tf_op jit(solution)/shard_map/ppermute | solution.py:479
  33.3 9.8 %collective-permute-start.11 = (bf16[1040,128]{1,0:T(8,128)(2,1)S(1)}, bf16[1040,128]{1,0:T(8,128)(2,1)S(1)}, u32[]{:S(2)}, u32[]{:S(2)}) collective-permute-start(bf16[1040,128]{1,0:T(8,128)(2,1)S(1)} %collective-permute-done.7.refs_2_), channel_id=1, source_target_pairs={{4,0},{8,4},{12,8},{14,12},{10,14},{6,10},{2,6},{0,2},{5,1},{9,5},... | collective-permute-start | bytes 798728 | tf_op jit(solution)/shard_map/ppermute | solution.py:479
  37.5 9.5 %collective-permute-start.13 = (bf16[1040,128]{1,0:T(8,128)(2,1)S(1)}, bf16[1040,128]{1,0:T(8,128)(2,1)S(1)}, u32[]{:S(2)}, u32[]{:S(2)}) collective-permute-start(bf16[1040,128]{1,0:T(8,128)(2,1)S(1)} %collective-permute-done.8.refs_0_), channel_id=1, source_target_pairs={{0,4},{4,8},{8,12},{12,14},{14,10},{10,6},{6,2},{2,0},{1,5},{5,9},... | collective-permute-start | bytes 798728 | tf_op jit(solution)/shard_map/ppermute | solution.py:479
  39.0 8.4 %collective-permute-start.14 = (bf16[1040,128]{1,0:T(8,128)(2,1)S(1)}, bf16[1040,128]{1,0:T(8,128)(2,1)S(1)}, u32[]{:S(2)}, u32[]{:S(2)}) collective-permute-start(bf16[1040,128]{1,0:T(8,128)(2,1)S(1)} %collective-permute-done.9.refs_3_), channel_id=1, source_target_pairs={{4,0},{8,4},{12,8},{14,12},{10,14},{6,10},{2,6},{0,2},{5,1},{9,5},... | collective-permute-start | bytes 798728 | tf_op jit(solution)/shard_map/ppermute | solution.py:479
  41.1 9.3 %collective-permute-start.15 = (bf16[2,256,1024]{2,1,0:T(8,128)(2,1)S(1)}, bf16[2,256,1024]{2,1,0:T(8,128)(2,1)S(1)}, u32[]{:S(2)}, u32[]{:S(2)}) collective-permute-start(bf16[2,256,1024]{2,1,0:T(8,128)(2,1)S(1)} %get-tuple-element.97.refs_1_), channel_id=1, source_target_pairs={{0,1},{1,0},{2,3},{3,2},{4,5},{5,4},{6,7},{7,6},{8,9},{9,8},{10,11... | collective-permute-start | bytes 3145736 | tf_op jit(solution)/shard_map/ppermute | solution.py:482
  43.2 7.9 %collective-permute-start.16 = (bf16[2,256,1024]{2,1,0:T(8,128)(2,1)S(1)}, bf16[2,256,1024]{2,1,0:T(8,128)(2,1)S(1)}, u32[]{:S(2)}, u32[]{:S(2)}) collective-permute-start(bf16[2,256,1024]{2,1,0:T(8,128)(2,1)S(1)} %get-tuple-element.110.refs_2_), channel_id=1, source_target_pairs={{0,1},{1,0},{2,3},{3,2},{4,5},{5,4},{6,7},{7,6},{8,9},{9,8},{10,11... | collective-permute-start | bytes 3145736 | tf_op jit(solution)/shard_map/ppermute | solution.py:482
  47.4 3.7 %collective-permute-start.17 = (bf16[2,256,1024]{2,1,0:T(8,128)(2,1)S(1)}, bf16[2,256,1024]{2,1,0:T(8,128)(2,1)S(1)}, u32[]{:S(2)}, u32[]{:S(2)}) collective-permute-start(bf16[2,256,1024]{2,1,0:T(8,128)(2,1)S(1)} %get-tuple-element.122.refs_3_), channel_id=1, source_target_pairs={{0,1},{1,0},{2,3},{3,2},{4,5},{5,4},{6,7},{7,6},{8,9},{9,8},{10,11... | collective-permute-start | bytes 3145736 | tf_op jit(solution)/shard_map/ppermute | solution.py:482
  49.1 2.0 %collective-permute-start.18 = (bf16[2,128,1024]{2,1,0:T(8,128)(2,1)S(1)}, bf16[2,128,1024]{2,1,0:T(8,128)(2,1)S(1)}, u32[]{:S(2)}, u32[]{:S(2)}) collective-permute-start(bf16[2,128,1024]{2,1,0:T(8,128)(2,1)S(1)} %get-tuple-element.127.refs_4_), channel_id=1, source_target_pairs={{0,1},{1,0},{2,3},{3,2},{4,5},{5,4},{6,7},{7,6},{8,9},{9,8},{10,11... | collective-permute-start | bytes 1572872 | tf_op jit(solution)/shard_map/ppermute | solution.py:482
  55.9 18.5 %collective-permute-start.19 = (bf16[40,2048]{1,0:T(8,128)(2,1)S(1)}, bf16[40,2048]{1,0:T(8,128)(2,1)S(1)}, u32[]{:S(2)}, u32[]{:S(2)}) collective-permute-start(bf16[40,2048]{1,0:T(8,128)(2,1)S(1)} %get-tuple-element.153), channel_id=1, source_target_pairs={{0,8},{2,10},{4,12},{6,14},{8,0},{10,2},{12,4},{14,6},{1,9},{3,11}... | collective-permute-start | bytes 491528 | tf_op jit(solution)/shard_map/ppermute | solution.py:522
  56.6 23.1 %collective-permute-start.20 = (bf16[40,2048]{1,0:T(8,128)(2,1)S(1)}, bf16[40,2048]{1,0:T(8,128)(2,1)S(1)}, u32[]{:S(2)}, u32[]{:S(2)}) collective-permute-start(bf16[40,2048]{1,0:T(8,128)(2,1)S(1)} %get-tuple-element.157), channel_id=1, source_target_pairs={{0,10},{2,8},{4,14},{6,12},{8,2},{10,0},{12,6},{14,4},{1,11},{3,9}... | collective-permute-start | bytes 491528 | tf_op jit(solution)/shard_map/ppermute | solution.py:522
  63.9 17.5 %copy-start.7 = (bf16[1040,128]{1,0:T(8,128)(2,1)S(1)}, bf16[1040,128]{1,0:T(8,128)(2,1)}, u32[]{:S(2)}) copy-start(bf16[1040,128]{1,0:T(8,128)(2,1)} %get-tuple-element.84.top_ref.refs_0_) | copy-start | bytes 798724
  63.9 17.5 %copy-start.9 = (bf16[1040,128]{1,0:T(8,128)(2,1)S(1)}, bf16[1040,128]{1,0:T(8,128)(2,1)}, u32[]{:S(2)}) copy-start(bf16[1040,128]{1,0:T(8,128)(2,1)} %get-tuple-element.85.bottom_ref.refs_1_) | copy-start | bytes 798724
  63.9 17.5 %copy-start.10 = (f32[2048,8]{0,1:T(8,128)S(1)}, f32[2048,8]{0,1:T(8,128)}, u32[]{:S(2)}) copy-start(f32[2048,8]{0,1:T(8,128)} %param.10) | copy-start | bytes 196612
  63.9 17.9 %collective-permute-start.21 = (bf16[40,2048]{1,0:T(8,128)(2,1)S(1)}, bf16[40,2048]{1,0:T(8,128)(2,1)S(1)}, u32[]{:S(2)}, u32[]{:S(2)}) collective-permute-start(bf16[40,2048]{1,0:T(8,128)(2,1)S(1)} %get-tuple-element.158), channel_id=1, source_target_pairs={{0,12},{2,14},{4,8},{6,10},{8,4},{10,6},{12,0},{14,2},{1,13},{3,15... | collective-permute-start | bytes 491528 | tf_op jit(solution)/shard_map/ppermute | solution.py:522
  74.4 9.9 %collective-permute-start.22 = (bf16[40,2048]{1,0:T(8,128)(2,1)S(1)}, bf16[40,2048]{1,0:T(8,128)(2,1)S(1)}, u32[]{:S(2)}, u32[]{:S(2)}) collective-permute-start(bf16[40,2048]{1,0:T(8,128)(2,1)S(1)} %get-tuple-element.159), channel_id=1, source_target_pairs={{0,14},{2,12},{4,10},{6,8},{8,6},{10,4},{12,2},{14,0},{1,15},{3,13... | collective-permute-start | bytes 491528 | tf_op jit(solution)/shard_map/ppermute | solution.py:522
  77.9 9.0 %collective-permute-start.23 = (bf16[40,2048]{1,0:T(8,128)(2,1)S(1)}, bf16[40,2048]{1,0:T(8,128)(2,1)S(1)}, u32[]{:S(2)}, u32[]{:S(2)}) collective-permute-start(bf16[40,2048]{1,0:T(8,128)(2,1)S(1)} %get-tuple-element.160), channel_id=1, source_target_pairs={{0,6},{2,4},{4,2},{6,0},{8,14},{10,12},{12,10},{14,8},{1,7},{3,5},... | collective-permute-start | bytes 491528 | tf_op jit(solution)/shard_map/ppermute | solution.py:522
  77.9 10.5 %collective-permute-start.24 = (bf16[40,2048]{1,0:T(8,128)(2,1)S(1)}, bf16[40,2048]{1,0:T(8,128)(2,1)S(1)}, u32[]{:S(2)}, u32[]{:S(2)}) collective-permute-start(bf16[40,2048]{1,0:T(8,128)(2,1)S(1)} %get-tuple-element.161), channel_id=1, source_target_pairs={{0,4},{2,6},{4,0},{6,2},{8,12},{10,14},{12,8},{14,10},{1,5},{3,7},... | collective-permute-start | bytes 491528 | tf_op jit(solution)/shard_map/ppermute | solution.py:522
  79.7 9.8 %collective-permute-start.25 = (bf16[40,2048]{1,0:T(8,128)(2,1)S(1)}, bf16[40,2048]{1,0:T(8,128)(2,1)S(1)}, u32[]{:S(2)}, u32[]{:S(2)}) collective-permute-start(bf16[40,2048]{1,0:T(8,128)(2,1)S(1)} %get-tuple-element.162), channel_id=1, source_target_pairs={{0,2},{2,0},{4,6},{6,4},{8,10},{10,8},{12,14},{14,12},{1,3},{3,1},... | collective-permute-start | bytes 491528 | tf_op jit(solution)/shard_map/ppermute | solution.py:522

commit v2 on v1

--- a/solution.py
+++ b/solution.py
@@ -198,24 +198,31 @@
     )(*picked, query_slab, next_slab)
 
 
+def arrange_other(panel_ref, offsets, other_ref):
+    tok_count = panel_ref.shape[2]
+    for g, offset in enumerate(offsets):
+        place = ring_owner(offset) * 2 + 1 - lax.axis_index("exp")
+        for which in range(2):
+            panel_ref[which, place] = other_ref[which, pl.ds(g * tok_count, tok_count)]
+
+
 def arrange_kernel(plan, *refs):
     count = len(plan)
-    own_refs, other_refs, query_refs, pos_refs = (refs[k * count : (k + 1) * count] for k in range(4))
-    panel_ref, queries_ref, places_ref = refs[4 * count :]
-    exp_count = 2
-    side = lax.axis_index("exp")
+    own_refs, query_refs, pos_refs = (refs[k * count : (k + 1) * count] for k in range(3))
+    other_refs = refs[3 * count : -3]
+    panel_ref, queries_ref, places_ref = refs[-3:]
     tok_count = panel_ref.shape[2]
-    for offsets, own_ref, other_ref, query_ref, pos_ref in zip(
-        plan, own_refs, other_refs, query_refs, pos_refs
-    ):
+    for offsets, own_ref, query_ref, pos_ref in zip(plan, own_refs, query_refs, pos_refs):
         for g, offset in enumerate(offsets):
             owner = ring_owner(offset)
-            part = pl.ds(g * tok_count, tok_count)
             for which in range(2):
-                panel_ref[which, owner * exp_count + side] = own_ref[which, part]
-                panel_ref[which, owner * exp_count + 1 - side] = other_ref[which, part]
+                panel_ref[which, owner * 2 + lax.axis_index("exp")] = own_ref[
+                    which, pl.ds(g * tok_count, tok_count)
+                ]
             queries_ref[owner] = query_ref[g].astype(jnp.float32)[:MOST]
             places_ref[owner] = pos_ref[g, :MOST]
+    for offsets, other_ref in zip(plan, other_refs):
+        arrange_other(panel_ref, offsets, other_ref)
 
 
 def arrange(owners, plan, own, other, queries, positions):
@@ -226,17 +233,29 @@
         jax.ShapeDtypeStruct((owners, MOST, width), jnp.float32),
         jax.ShapeDtypeStruct((owners, MOST, LANES), jnp.float32),
     ]
-    operands = (*own, *other, *queries, *positions)
-    return pl.pallas_call(
+    operands = (*own, *queries, *positions, *other[:-1])
+    panel, queries, places = pl.pallas_call(
         functools.partial(arrange_kernel, plan),
         in_specs=[WHOLE] * len(operands),
         out_specs=[WHOLE] * 3,
         out_shape=shapes,
-        compiler_params=pltpu.CompilerParams(
-            vmem_limit_bytes=8 * MIB
-        ),
+        compiler_params=pltpu.CompilerParams(vmem_limit_bytes=8 * MIB),
         name="arrange",
     )(*operands)
+
+    def last_kernel(held_ref, other_ref, panel_ref):
+        arrange_other(panel_ref, plan[-1], other_ref)
+
+    panel = pl.pallas_call(
+        last_kernel,
+        in_specs=[WHOLE] * 2,
+        out_specs=WHOLE,
+        out_shape=shapes[0],
+        input_output_aliases={0: 0},
+        compiler_params=pltpu.CompilerParams(vmem_limit_bytes=8 * MIB),
+        name="arrange_last",
+    )(panel, other[-1])
+    return panel, queries, places
 
 
 def attend_kernel(lots, heads, panel_ref, queries_ref, places_ref, weight_ref, *refs):
@@ -335,7 +354,7 @@
         ],
         compiler_params=pltpu.CompilerParams(vmem_limit_bytes=held * 9 // 8 + 4 * MIB),
         cost_estimate=pl.CostEstimate(
-            flops=count * 2 * SLOTS * width * (4 * length + 2 * model_width),
+            flops=count * 1 * SLOTS * width * (4 * length + 2 * model_width),
             bytes_accessed=4 * length * width,
             transcendentals=count * 2 * SLOTS * length * width // HS,
         ),
@@ -528,8 +547,6 @@
         if start > 0:
             places, *pieces = tie(held[2], *pieces)
             held = [*held[:2], places]
-            if far:
-                pieces[-1], far[0][0] = tie(pieces[-1], far[0][0])
             far.append([swap(piece, start + r) for r, piece in enumerate(pieces)])
         else:
             near = pieces

time: 91 us -> 88.8 us (0.976)
  waiting for transfers between devices: 25.5 us -> 21.8 us
  starting transfers between devices: 25.6 us -> 27.1 us
    ppermute x7, waiting for transfers between devices: 12.8 us -> 9.78 us  [swap(): return lax.ppermute(piece, 'ctx', [(c, c ^ k) for c in range(ctx_count)])]
    ppermute x7, starting transfers between devices: 4.21 us -> 2.26 us  [send(): lax.ppermute(parts[1], 'ctx', backward)]
    ppermute x7, starting transfers between devices: 11.1 us -> 13 us  [send(): lax.ppermute(parts[0], 'ctx', forward)]
    ppermute x7, starting transfers between devices: 9.74 us -> 11.3 us  [swap(): return lax.ppermute(piece, 'ctx', [(c, c ^ k) for c in range(ctx_count)])]
  transfers between devices with their start and end apart: 26 -> 26, of which waited for: 17 -> 15; matrix products, arithmetic and copies ran while one was open for 0% -> 0% of each run, Pallas kernels for 27% -> 29%
where the time goes in v2:
time: 88.8 us; the launch traced here: 88.6 us
  Pallas kernels  32.9 us (37%)
  starting transfers between devices  27.1 us (31%)
  waiting for transfers between devices  21.8 us (25%)
  local copies, waits for them, and re-layouts  6.31 us (7%)
    pallas_call x3, Pallas kernels, attend(): pl.pallas_call(functools.partial(attend_kernel, lots, heads), in_specs=[W...  14.1 us
    ppermute x7, starting transfers between devices, send(): lax.ppermute(parts[0], 'ctx', forward)  13 us
    ppermute x7, starting transfers between devices, swap(): return lax.ppermute(piece, 'ctx', [(c, c ^ k) for c in range(ctx_count)])  11.3 us
    ppermute x7, waiting for transfers between devices, send(): lax.ppermute(parts[1], 'ctx', backward)  11 us
    ppermute x7, waiting for transfers between devices, swap(): return lax.ppermute(piece, 'ctx', [(c, c ^ k) for c in range(ctx_count)])  9.78 us
    unnamed x22, local copies, waits for them, and re-layouts  6.31 us
    pallas_call x5, Pallas kernels, project_values(): pl.pallas_call(functools.partial(values_kernel, half, offsets, len(blocks...  6.15 us
    pallas_call x5, Pallas kernels, project_keys(): pl.pallas_call(functools.partial(keys_kernel, half, len(blocks)), in_spec...  5.29 us
  transfers between devices with their start and end apart: 26, of which 15 were waited for; matrix products, arithmetic and copies ran while one was open for 0% of the time, Pallas kernels for 29%

profile of v2, /device:TPU:0, one launch (start us, length us, event | category | flops | bytes accessed | tf_op | source)
XLA Modules:
  0.0 88.6 jit_solution(8567751729440251031)
XLA Ops:
  0.0 2.0 %norm_rows.1 = (bf16[1040,128]{1,0:T(8,128)(2,1)}, bf16[1040,128]{1,0:T(8,128)(2,1)}) custom-call(bf16[128,2048]{1,0:T(8,128)(2,1)} %refs_0_.1, f32[1,2048]{1,0:T(1,128)} %bitcast.15, s32[2,128]{1,0:T(2,128)} %bitcast.16), custom_call_target="tpu_custom_call" | custom-call | tf_op jit(solution)/shard_map/norm_rows/pallas_call | solution.py:85
  2.0 3.1 %collective-permute-start = (bf16[1040,128]{1,0:T(8,128)(2,1)}, bf16[1040,128]{1,0:T(8,128)(2,1)S(1)}, u32[]{:S(2)}, u32[]{:S(2)}) collective-permute-start(bf16[1040,128]{1,0:T(8,128)(2,1)} %get-tuple-element.82.top_ref.refs_0_), channel_id=1, source_target_pairs={{0,4},{4,8},{8,12},{12,14},{14,10},{10,6},{6,2},{2,0},{1,5},{5,9},... | collective-permute-start | bytes 798728 | tf_op jit(solution)/shard_map/ppermute | solution.py:498
  5.1 0.0 collective-permute-start.1
  5.1 2.0 %collective-permute-start.2 = (bf16[1040,128]{1,0:T(8,128)(2,1)}, bf16[1040,128]{1,0:T(8,128)(2,1)S(1)}, u32[]{:S(2)}, u32[]{:S(2)}) collective-permute-start(bf16[1040,128]{1,0:T(8,128)(2,1)} %get-tuple-element.83.bottom_ref.refs_1_), channel_id=1, source_target_pairs={{0,4},{4,8},{8,12},{12,14},{14,10},{10,6},{6,2},{2,0},{1,5},{5,9},... | collective-permute-start | bytes 798728 | tf_op jit(solution)/shard_map/ppermute | solution.py:498
  7.1 0.0 collective-permute-start.3
  7.2 2.2 %copy-done.1 = bf16[2048,1024]{1,0:T(8,128)(2,1)S(1)} copy-done((bf16[2048,1024]{1,0:T(8,128)(2,1)S(1)}, bf16[2048,1024]{1,0:T(8,128)(2,1)}, u32[]{:S(2)}) %copy-start.1) | copy-done | bytes 4194328
  9.3 0.9 %copy-done.6 = bf16[1040,128]{1,0:T(8,128)(2,1)S(1)} copy-done((bf16[1040,128]{1,0:T(8,128)(2,1)S(1)}, bf16[1040,128]{1,0:T(8,128)(2,1)}, u32[]{:S(2)}) %copy-start.6) | copy-done | bytes 266264
  10.3 0.9 %copy-done.8 = bf16[1040,128]{1,0:T(8,128)(2,1)S(1)} copy-done((bf16[1040,128]{1,0:T(8,128)(2,1)S(1)}, bf16[1040,128]{1,0:T(8,128)(2,1)}, u32[]{:S(2)}) %copy-start.8) | copy-done | bytes 266264
  11.2 0.7 project_keys.5
  12.0 0.5 collective-permute-done.refs_0_
  12.5 2.2 %collective-permute-done.1.refs_3_ = bf16[1040,128]{1,0:T(8,128)(2,1)S(1)} collective-permute-done((bf16[1040,128]{1,0:T(8,128)(2,1)}, bf16[1040,128]{1,0:T(8,128)(2,1)S(1)}, u32[]{:S(2)}, u32[]{:S(2)}) %collective-permute-start.1) | collective-permute-done | bytes 266272 | tf_op jit(solution)/shard_map/ppermute | solution.py:498
  14.6 1.6 %collective-permute-start.4 = (bf16[1040,128]{1,0:T(8,128)(2,1)S(1)}, bf16[1040,128]{1,0:T(8,128)(2,1)S(1)}, u32[]{:S(2)}, u32[]{:S(2)}) collective-permute-start(bf16[1040,128]{1,0:T(8,128)(2,1)S(1)} %collective-permute-done.refs_0_), channel_id=1, source_target_pairs={{0,4},{4,8},{8,12},{12,14},{14,10},{10,6},{6,2},{2,0},{1,5},{5,9},... | collective-permute-start | bytes 798728 | tf_op jit(solution)/shard_map/ppermute | solution.py:498
  16.2 0.4 collective-permute-start.5
  16.7 2.2 %copy-done.3 = bf16[2048,1024]{1,0:T(8,128)(2,1)S(1)} copy-done((bf16[2048,1024]{1,0:T(8,128)(2,1)S(1)}, bf16[2048,1024]{1,0:T(8,128)(2,1)}, u32[]{:S(2)}) %copy-start.3) | copy-done | bytes 4194328
  18.9 0.8 project_values.5
  19.7 0.6 collective-permute-done.3.refs_2_
  20.3 1.6 %collective-permute-start.6 = (bf16[1040,128]{1,0:T(8,128)(2,1)S(1)}, bf16[1040,128]{1,0:T(8,128)(2,1)S(1)}, u32[]{:S(2)}, u32[]{:S(2)}) collective-permute-start(bf16[1040,128]{1,0:T(8,128)(2,1)S(1)} %collective-permute-done.2.refs_1_), channel_id=1, source_target_pairs={{0,4},{4,8},{8,12},{12,14},{14,10},{10,6},{6,2},{2,0},{1,5},{5,9},... | collective-permute-start | bytes 798728 | tf_op jit(solution)/shard_map/ppermute | solution.py:498
  21.9 0.4 collective-permute-start.7
  22.4 1.3 %project_keys.6 = (bf16[256,1024]{1,0:T(8,128)(2,1)S(1)}, f32[8,128]{1,0:T(8,128)S(1)}) custom-call(bf16[1040,128]{1,0:T(8,128)(2,1)S(1)} %collective-permute-done.refs_0_, bf16[1040,128]{1,0:T(8,128)(2,1)S(1)} %collective-permute-done.2.refs_1_, bf16[1040,128]{1,0:T(8,128)(2,1)S(1)} %collective-permute-done.3.refs_2_, ...), custom_call_target="tpu_custom_call" | custom-call | tf_op jit(solution)/shard_map/project_keys/pallas_call | solution.py:115
  23.7 0.3 collective-permute-done.4.refs_0_
  24.0 2.1 %collective-permute-done.5.refs_3_ = bf16[1040,128]{1,0:T(8,128)(2,1)S(1)} collective-permute-done((bf16[1040,128]{1,0:T(8,128)(2,1)S(1)}, bf16[1040,128]{1,0:T(8,128)(2,1)S(1)}, u32[]{:S(2)}, u32[]{:S(2)}) %collective-permute-start.5) | collective-permute-done | bytes 266272 | tf_op jit(solution)/shard_map/ppermute | solution.py:498
  26.1 1.6 %collective-permute-start.8 = (bf16[1040,128]{1,0:T(8,128)(2,1)S(1)}, bf16[1040,128]{1,0:T(8,128)(2,1)S(1)}, u32[]{:S(2)}, u32[]{:S(2)}) collective-permute-start(bf16[1040,128]{1,0:T(8,128)(2,1)S(1)} %collective-permute-done.4.refs_0_), channel_id=1, source_target_pairs={{0,4},{4,8},{8,12},{12,14},{14,10},{10,6},{6,2},{2,0},{1,5},{5,9},... | collective-permute-start | bytes 798728 | tf_op jit(solution)/shard_map/ppermute | solution.py:498
  27.6 0.4 collective-permute-start.9
  28.1 1.5 %project_values.6 = (bf16[2,256,1024]{2,1,0:T(8,128)(2,1)S(1)}, bf16[2,48,2048]{2,1,0:T(8,128)(2,1)S(1)}, f32[2,48,128]{2,1,0:T(8,128)S(1)}) custom-call(f32[8,128]{1,0:T(8,128)S(1)} %get-tuple-element.93.mark_ref, bf16[256,1024]{1,0:T(8,128)(2,1)S(1)} %get-tuple-element.94.keys_ref, bf16[1040,128]{1,0:T(8,128)(2,1)S(1)} %collective-permute-done.refs_0_, ...), custom_call_target="tpu_custom_call" | custom-call | tf_op jit(solution)/shard_map/project_values/pallas_call | solution.py:160
  29.6 0.1 collective-permute-done.6.refs_1_
  29.7 2.1 %collective-permute-done.7.refs_2_ = bf16[1040,128]{1,0:T(8,128)(2,1)S(1)} collective-permute-done((bf16[1040,128]{1,0:T(8,128)(2,1)S(1)}, bf16[1040,128]{1,0:T(8,128)(2,1)S(1)}, u32[]{:S(2)}, u32[]{:S(2)}) %collective-permute-start.7) | collective-permute-done | bytes 266272 | tf_op jit(solution)/shard_map/ppermute | solution.py:498
  31.8 1.6 %collective-permute-start.10 = (bf16[1040,128]{1,0:T(8,128)(2,1)S(1)}, bf16[1040,128]{1,0:T(8,128)(2,1)S(1)}, u32[]{:S(2)}, u32[]{:S(2)}) collective-permute-start(bf16[1040,128]{1,0:T(8,128)(2,1)S(1)} %collective-permute-done.6.refs_1_), channel_id=1, source_target_pairs={{0,4},{4,8},{8,12},{12,14},{14,10},{10,6},{6,2},{2,0},{1,5},{5,9},... | collective-permute-start | bytes 798728 | tf_op jit(solution)/shard_map/ppermute | solution.py:498
  33.3 0.4 collective-permute-start.11
  33.8 0.8 project_queries.3
  34.6 1.3 %project_keys.7 = (bf16[256,1024]{1,0:T(8,128)(2,1)S(1)}, f32[8,128]{1,0:T(8,128)S(1)}) custom-call(bf16[1040,128]{1,0:T(8,128)(2,1)S(1)} %collective-permute-done.4.refs_0_, bf16[1040,128]{1,0:T(8,128)(2,1)S(1)} %collective-permute-done.6.refs_1_, bf16[1040,128]{1,0:T(8,128)(2,1)S(1)} %collective-permute-done.7.refs_2_, ...), custom_call_target="tpu_custom_call" | custom-call | tf_op jit(solution)/shard_map/project_keys/pallas_call | solution.py:115
  35.9 1.6 %collective-permute-done.9.refs_3_ = bf16[1040,128]{1,0:T(8,128)(2,1)S(1)} collective-permute-done((bf16[1040,128]{1,0:T(8,128)(2,1)S(1)}, bf16[1040,128]{1,0:T(8,128)(2,1)S(1)}, u32[]{:S(2)}, u32[]{:S(2)}) %collective-permute-start.9) | collective-permute-done | bytes 266272 | tf_op jit(solution)/shard_map/ppermute | solution.py:498
  37.5 1.6 %collective-permute-start.13 = (bf16[1040,128]{1,0:T(8,128)(2,1)S(1)}, bf16[1040,128]{1,0:T(8,128)(2,1)S(1)}, u32[]{:S(2)}, u32[]{:S(2)}) collective-permute-start(bf16[1040,128]{1,0:T(8,128)(2,1)S(1)} %collective-permute-done.8.refs_0_), channel_id=1, source_target_pairs={{0,4},{4,8},{8,12},{12,14},{14,10},{10,6},{6,2},{2,0},{1,5},{5,9},... | collective-permute-start | bytes 798728 | tf_op jit(solution)/shard_map/ppermute | solution.py:498
  39.0 0.4 collective-permute-start.14
  39.5 1.5 %project_values.7 = (bf16[2,256,1024]{2,1,0:T(8,128)(2,1)S(1)}, bf16[2,48,2048]{2,1,0:T(8,128)(2,1)S(1)}, f32[2,48,128]{2,1,0:T(8,128)S(1)}) custom-call(f32[8,128]{1,0:T(8,128)S(1)} %get-tuple-element.106.mark_ref, bf16[256,1024]{1,0:T(8,128)(2,1)S(1)} %get-tuple-element.107.keys_ref, bf16[1040,128]{1,0:T(8,128)(2,1)S(1)} %collective-permute-done.4.refs_0_, ...), custom_call_target="tpu_custom_call" | custom-call | tf_op jit(solution)/shard_map/project_values/pallas_call | solution.py:160
  41.0 0.1 collective-permute-done.10.refs_1_
  41.1 2.1 %collective-permute-done.11.refs_2_ = bf16[1040,128]{1,0:T(8,128)(2,1)S(1)} collective-permute-done((bf16[1040,128]{1,0:T(8,128)(2,1)S(1)}, bf16[1040,128]{1,0:T(8,128)(2,1)S(1)}, u32[]{:S(2)}, u32[]{:S(2)}) %collective-permute-start.11) | collective-permute-done | bytes 266272 | tf_op jit(solution)/shard_map/ppermute | solution.py:498
  43.2 1.3 %project_keys.8 = (bf16[256,1024]{1,0:T(8,128)(2,1)S(1)}, f32[8,128]{1,0:T(8,128)S(1)}) custom-call(bf16[1040,128]{1,0:T(8,128)(2,1)S(1)} %collective-permute-done.8.refs_0_, bf16[1040,128]{1,0:T(8,128)(2,1)S(1)} %collective-permute-done.10.refs_1_, bf16[1040,128]{1,0:T(8,128)(2,1)S(1)} %collective-permute-done.11.refs_2_, ...), custom_call_target="tpu_custom_call" | custom-call | tf_op jit(solution)/shard_map/project_keys/pallas_call | solution.py:115
  44.5 1.5 %project_values.8 = (bf16[2,256,1024]{2,1,0:T(8,128)(2,1)S(1)}, bf16[2,48,2048]{2,1,0:T(8,128)(2,1)S(1)}, f32[2,48,128]{2,1,0:T(8,128)S(1)}) custom-call(f32[8,128]{1,0:T(8,128)S(1)} %get-tuple-element.112.mark_ref, bf16[256,1024]{1,0:T(8,128)(2,1)S(1)} %get-tuple-element.113.keys_ref, bf16[1040,128]{1,0:T(8,128)(2,1)S(1)} %collective-permute-done.8.refs_0_, ...), custom_call_target="tpu_custom_call" | custom-call | tf_op jit(solution)/shard_map/project_values/pallas_call | solution.py:160
  46.0 1.0 %project_queries.4 = (bf16[2,48,1024]{2,1,0:T(8,128)(2,1)S(1)}, bf16[2,48,1024]{2,1,0:T(8,128)(2,1)S(1)}) custom-call(bf16[2,48,2048]{2,1,0:T(8,128)(2,1)S(1)} %get-tuple-element.115.refs_0_, bf16[2,48,2048]{2,1,0:T(8,128)(2,1)S(1)} %get-tuple-element.116.refs_1_, bf16[2048,1024]{1,0:T(8,128)(2,1)S(1)} %bitcast.12, bf16[1024,2048]{1,0:T(8,128)(2,1)S(1)} %bitcast.6), custom_call_target="tpu_custom_call" | custom-call | tf_op jit(solution)/shard_map/project_queries/pallas_call | solution.py:189
  47.0 0.4 collective-permute-done.14.refs_1_
  47.4 0.1 collective-permute-start.17
  47.6 0.7 project_keys.9
  48.3 0.8 project_values.9
  49.1 0.4 collective-permute-start.18
  49.5 0.8 project_queries.5.refs_9_
  50.4 0.7 arrange.1
  51.1 0.0 collective-permute-done.18.other_ref
  51.1 0.1 arrange_last.1.panel_ref
  51.2 4.1 %attend.3 = (bf16[40,2048]{1,0:T(8,128)(2,1)S(1)}, bf16[40,2048]{1,0:T(8,128)(2,1)S(1)}) custom-call(bf16[2,16,128,1024]{3,2,1,0:T(8,128)(2,1)S(1)} %arrange_last.1.panel_ref, f32[8,40,1024]{2,1,0:T(8,128)S(1)} %get-tuple-element.138.queries_ref, f32[8,40,128]{2,1,0:T(8,128)S(1)} %get-tuple-element.145.places_ref, bf16[1024,2048]{1,0:T(8,128)(2,1)S(1)} %bitcast.8), custom_call_target="tpu_custom_call" | custom-call | flops 603979776 | bytes 8388608 | tf_op jit(solution)/shard_map/attend/pallas_call | solution.py:345
  55.3 0.7 collective-permute-start.19
  56.0 2.0 %collective-permute-start.20 = (bf16[40,2048]{1,0:T(8,128)(2,1)S(1)}, bf16[40,2048]{1,0:T(8,128)(2,1)S(1)}, u32[]{:S(2)}, u32[]{:S(2)}) collective-permute-start(bf16[40,2048]{1,0:T(8,128)(2,1)S(1)} %get-tuple-element.153), channel_id=1, source_target_pairs={{0,10},{2,8},{4,14},{6,12},{8,2},{10,0},{12,6},{14,4},{1,11},{3,9}... | collective-permute-start | bytes 491528 | tf_op jit(solution)/shard_map/ppermute | solution.py:541
  58.0 5.3 %attend.4 = (bf16[40,2048]{1,0:T(8,128)(2,1)S(1)}, bf16[40,2048]{1,0:T(8,128)(2,1)S(1)}) custom-call(bf16[2,16,128,1024]{3,2,1,0:T(8,128)(2,1)S(1)} %arrange_last.1.panel_ref, f32[8,40,1024]{2,1,0:T(8,128)S(1)} %get-tuple-element.138.queries_ref, f32[8,40,128]{2,1,0:T(8,128)S(1)} %get-tuple-element.145.places_ref, bf16[1024,2048]{1,0:T(8,128)(2,1)S(1)} %bitcast.9), custom_call_target="tpu_custom_call" | custom-call | flops 603979776 | bytes 8388608 | tf_op jit(solution)/shard_map/attend/pallas_call | solution.py:345
  63.3 0.1 collective-permute-start.21
  63.4 5.0 %collective-permute-start.22 = (bf16[40,2048]{1,0:T(8,128)(2,1)S(1)}, bf16[40,2048]{1,0:T(8,128)(2,1)S(1)}, u32[]{:S(2)}, u32[]{:S(2)}) collective-permute-start(bf16[40,2048]{1,0:T(8,128)(2,1)S(1)} %get-tuple-element.155), channel_id=1, source_target_pairs={{0,14},{2,12},{4,10},{6,8},{8,6},{10,4},{12,2},{14,0},{1,15},{3,13... | collective-permute-start | bytes 491528 | tf_op jit(solution)/shard_map/ppermute | solution.py:541
  68.4 4.7 %attend.5 = (bf16[40,2048]{1,0:T(8,128)(2,1)S(1)}, bf16[40,2048]{1,0:T(8,128)(2,1)S(1)}, bf16[40,2048]{1,0:T(8,128)(2,1)S(1)}, bf16[40,2048]{1,0:T(8,128)(2,1)S(1)}) custom-call(bf16[2,16,128,1024]{3,2,1,0:T(8,128)(2,1)S(1)} %arrange_last.1.panel_ref, f32[8,40,1024]{2,1,0:T(8,128)S(1)} %get-tuple-element.138.queries_ref, ...), custom_call_target="tpu_custom_call" | custom-call | flops 1207959552 | bytes 8388608 | tf_op jit(solution)/shard_map/attend/pallas_call | solution.py:345
  73.1 4.2 %collective-permute-done.19.refs_1_ = bf16[40,2048]{1,0:T(8,128)(2,1)S(1)} collective-permute-done((bf16[40,2048]{1,0:T(8,128)(2,1)S(1)}, bf16[40,2048]{1,0:T(8,128)(2,1)S(1)}, u32[]{:S(2)}, u32[]{:S(2)}) %collective-permute-start.19) | collective-permute-done | bytes 163872 | tf_op jit(solution)/shard_map/ppermute | solution.py:541
  77.3 1.7 %collective-permute-start.24 = (bf16[40,2048]{1,0:T(8,128)(2,1)S(1)}, bf16[40,2048]{1,0:T(8,128)(2,1)S(1)}, u32[]{:S(2)}, u32[]{:S(2)}) collective-permute-start(bf16[40,2048]{1,0:T(8,128)(2,1)S(1)} %get-tuple-element.157), channel_id=1, source_target_pairs={{0,4},{2,6},{4,0},{6,2},{8,12},{10,14},{12,8},{14,10},{1,5},{3,7},... | collective-permute-start | bytes 491528 | tf_op jit(solution)/shard_map/ppermute | solution.py:541
  79.1 1.5 %collective-permute-done.20.refs_2_ = bf16[40,2048]{1,0:T(8,128)(2,1)S(1)} collective-permute-done((bf16[40,2048]{1,0:T(8,128)(2,1)S(1)}, bf16[40,2048]{1,0:T(8,128)(2,1)S(1)}, u32[]{:S(2)}, u32[]{:S(2)}) %collective-permute-start.20) | collective-permute-done | bytes 163872 | tf_op jit(solution)/shard_map/ppermute | solution.py:541
  80.6 1.7 %collective-permute-start.25 = (bf16[40,2048]{1,0:T(8,128)(2,1)S(1)}, bf16[40,2048]{1,0:T(8,128)(2,1)S(1)}, u32[]{:S(2)}, u32[]{:S(2)}) collective-permute-start(bf16[40,2048]{1,0:T(8,128)(2,1)S(1)} %get-tuple-element.158), channel_id=1, source_target_pairs={{0,2},{2,0},{4,6},{6,4},{8,10},{10,8},{12,14},{14,12},{1,3},{3,1},... | collective-permute-start | bytes 491528 | tf_op jit(solution)/shard_map/ppermute | solution.py:541
  82.3 0.5 gate_mix.1
  82.8 0.4 combine.2.refs_0_
  83.2 2.1 %collective-permute-done.23.refs_1_ = bf16[40,2048]{1,0:T(8,128)(2,1)S(1)} collective-permute-done((bf16[40,2048]{1,0:T(8,128)(2,1)S(1)}, bf16[40,2048]{1,0:T(8,128)(2,1)S(1)}, u32[]{:S(2)}, u32[]{:S(2)}) %collective-permute-start.23) | collective-permute-done | bytes 163872 | tf_op jit(solution)/shard_map/ppermute | solution.py:541
  85.3 1.9 %collective-permute-done.24.refs_2_ = bf16[40,2048]{1,0:T(8,128)(2,1)S(1)} collective-permute-done((bf16[40,2048]{1,0:T(8,128)(2,1)S(1)}, bf16[40,2048]{1,0:T(8,128)(2,1)S(1)}, u32[]{:S(2)}, u32[]{:S(2)}) %collective-permute-start.24) | collective-permute-done | bytes 163872 | tf_op jit(solution)/shard_map/ppermute | solution.py:541
  87.3 1.1 %combine.3 = bf16[128,2048]{1,0:T(8,128)(2,1)} custom-call(bf16[256,144]{1,0:T(8,128)(2,1)S(1)} %get-tuple-element.84.mix_ref, f32[128,2048]{1,0:T(8,128)S(1)} %combine.2.refs_0_, bf16[40,2048]{1,0:T(8,128)(2,1)S(1)} %collective-permute-done.23.refs_1_, bf16[40,2048]{1,0:T(8,128)(2,1)S(1)} %collective-permute-done.24.refs_2_, ...), custom_call_target="tpu_custom_call" | custom-call | tf_op jit(solution)/shard_map/combine/pallas_call | solution.py:461
  (32 shorter events, 0.1 us)
Async XLA Ops:
  2.0 10.5 %collective-permute-start = (bf16[1040,128]{1,0:T(8,128)(2,1)}, bf16[1040,128]{1,0:T(8,128)(2,1)S(1)}, u32[]{:S(2)}, u32[]{:S(2)}) collective-permute-start(bf16[1040,128]{1,0:T(8,128)(2,1)} %get-tuple-element.82.top_ref.refs_0_), channel_id=1, source_target_pairs={{0,4},{4,8},{8,12},{12,14},{14,10},{10,6},{6,2},{2,0},{1,5},{5,9},... | collective-permute-start | bytes 798728 | tf_op jit(solution)/shard_map/ppermute | solution.py:498
  5.1 9.5 %collective-permute-start.1 = (bf16[1040,128]{1,0:T(8,128)(2,1)}, bf16[1040,128]{1,0:T(8,128)(2,1)S(1)}, u32[]{:S(2)}, u32[]{:S(2)}) collective-permute-start(bf16[1040,128]{1,0:T(8,128)(2,1)} %get-tuple-element.83.bottom_ref.refs_1_), channel_id=1, source_target_pairs={{4,0},{8,4},{12,8},{14,12},{10,14},{6,10},{2,6},{0,2},{5,1},{9,5},... | collective-permute-start | bytes 798728 | tf_op jit(solution)/shard_map/ppermute | solution.py:498
  5.1 14.6 %collective-permute-start.2 = (bf16[1040,128]{1,0:T(8,128)(2,1)}, bf16[1040,128]{1,0:T(8,128)(2,1)S(1)}, u32[]{:S(2)}, u32[]{:S(2)}) collective-permute-start(bf16[1040,128]{1,0:T(8,128)(2,1)} %get-tuple-element.83.bottom_ref.refs_1_), channel_id=1, source_target_pairs={{0,4},{4,8},{8,12},{12,14},{14,10},{10,6},{6,2},{2,0},{1,5},{5,9},... | collective-permute-start | bytes 798728 | tf_op jit(solution)/shard_map/ppermute | solution.py:498
  7.1 13.2 %collective-permute-start.3 = (bf16[1040,128]{1,0:T(8,128)(2,1)}, bf16[1040,128]{1,0:T(8,128)(2,1)S(1)}, u32[]{:S(2)}, u32[]{:S(2)}) collective-permute-start(bf16[1040,128]{1,0:T(8,128)(2,1)} %get-tuple-element.82.top_ref.refs_0_), channel_id=1, source_target_pairs={{4,0},{8,4},{12,8},{14,12},{10,14},{6,10},{2,6},{0,2},{5,1},{9,5},... | collective-permute-start | bytes 798728 | tf_op jit(solution)/shard_map/ppermute | solution.py:498
  7.1 2.2 %copy-start.1 = (bf16[2048,1024]{1,0:T(8,128)(2,1)S(1)}, bf16[2048,1024]{1,0:T(8,128)(2,1)}, u32[]{:S(2)}) copy-start(bf16[2048,1024]{1,0:T(8,128)(2,1)} %refs_2_.6) | copy-start | bytes 12582916
  9.3 1.0 %copy-start.6 = (bf16[1040,128]{1,0:T(8,128)(2,1)S(1)}, bf16[1040,128]{1,0:T(8,128)(2,1)}, u32[]{:S(2)}) copy-start(bf16[1040,128]{1,0:T(8,128)(2,1)} %get-tuple-element.82.top_ref.refs_0_) | copy-start | bytes 798724
  10.3 1.0 %copy-start.8 = (bf16[1040,128]{1,0:T(8,128)(2,1)S(1)}, bf16[1040,128]{1,0:T(8,128)(2,1)}, u32[]{:S(2)}) copy-start(bf16[1040,128]{1,0:T(8,128)(2,1)} %get-tuple-element.83.bottom_ref.refs_1_) | copy-start | bytes 798724
  11.2 11.1 %copy-start.2 = (bf16[2048,1024]{1,0:T(8,128)(2,1)S(1)}, bf16[2048,1024]{1,0:T(8,128)(2,1)}, u32[]{:S(2)}) copy-start(bf16[2048,1024]{1,0:T(8,128)(2,1)} %refs_2_.6) | copy-start | bytes 12582916
  14.6 9.3 %collective-permute-start.4 = (bf16[1040,128]{1,0:T(8,128)(2,1)S(1)}, bf16[1040,128]{1,0:T(8,128)(2,1)S(1)}, u32[]{:S(2)}, u32[]{:S(2)}) collective-permute-start(bf16[1040,128]{1,0:T(8,128)(2,1)S(1)} %collective-permute-done.refs_0_), channel_id=1, source_target_pairs={{0,4},{4,8},{8,12},{12,14},{14,10},{10,6},{6,2},{2,0},{1,5},{5,9},... | collective-permute-start | bytes 798728 | tf_op jit(solution)/shard_map/ppermute | solution.py:498
  16.2 9.8 %collective-permute-start.5 = (bf16[1040,128]{1,0:T(8,128)(2,1)S(1)}, bf16[1040,128]{1,0:T(8,128)(2,1)S(1)}, u32[]{:S(2)}, u32[]{:S(2)}) collective-permute-start(bf16[1040,128]{1,0:T(8,128)(2,1)S(1)} %collective-permute-done.1.refs_3_), channel_id=1, source_target_pairs={{4,0},{8,4},{12,8},{14,12},{10,14},{6,10},{2,6},{0,2},{5,1},{9,5},... | collective-permute-start | bytes 798728 | tf_op jit(solution)/shard_map/ppermute | solution.py:498
  16.7 2.2 %copy-start.3 = (bf16[2048,1024]{1,0:T(8,128)(2,1)S(1)}, bf16[2048,1024]{1,0:T(8,128)(2,1)}, u32[]{:S(2)}) copy-start(bf16[2048,1024]{1,0:T(8,128)(2,1)} %refs_2_.7) | copy-start | bytes 12582916
  18.9 9.2 %copy-start.4 = (bf16[2048,1024]{1,0:T(8,128)(2,1)S(1)}, bf16[2048,1024]{1,0:T(8,128)(2,1)}, u32[]{:S(2)}) copy-start(bf16[2048,1024]{1,0:T(8,128)(2,1)} %refs_2_.7) | copy-start | bytes 12582916
  20.3 9.3 %collective-permute-start.6 = (bf16[1040,128]{1,0:T(8,128)(2,1)S(1)}, bf16[1040,128]{1,0:T(8,128)(2,1)S(1)}, u32[]{:S(2)}, u32[]{:S(2)}) collective-permute-start(bf16[1040,128]{1,0:T(8,128)(2,1)S(1)} %collective-permute-done.2.refs_1_), channel_id=1, source_target_pairs={{0,4},{4,8},{8,12},{12,14},{14,10},{10,6},{6,2},{2,0},{1,5},{5,9},... | collective-permute-start | bytes 798728 | tf_op jit(solution)/shard_map/ppermute | solution.py:498
  21.9 9.8 %collective-permute-start.7 = (bf16[1040,128]{1,0:T(8,128)(2,1)S(1)}, bf16[1040,128]{1,0:T(8,128)(2,1)S(1)}, u32[]{:S(2)}, u32[]{:S(2)}) collective-permute-start(bf16[1040,128]{1,0:T(8,128)(2,1)S(1)} %collective-permute-done.3.refs_2_), channel_id=1, source_target_pairs={{4,0},{8,4},{12,8},{14,12},{10,14},{6,10},{2,6},{0,2},{5,1},{9,5},... | collective-permute-start | bytes 798728 | tf_op jit(solution)/shard_map/ppermute | solution.py:498
  22.4 11.4 %copy-start.5 = (bf16[1,2048,1024]{2,1,0:T(8,128)(2,1)S(1)}, bf16[1,2048,1024]{2,1,0:T(8,128)(2,1)}, u32[]{:S(2)}) copy-start(bf16[1,2048,1024]{2,1,0:T(8,128)(2,1)} %param.14) | copy-start | bytes 12582916
  23.7 10.1 %copy-start = (bf16[1,1024,2048]{2,1,0:T(8,128)(2,1)S(1)}, bf16[1,1024,2048]{2,1,0:T(8,128)(2,1)}, u32[]{:S(2)}) copy-start(bf16[1,1024,2048]{2,1,0:T(8,128)(2,1)} %param.15) | copy-start | bytes 12582916
  26.1 9.8 %collective-permute-start.8 = (bf16[1040,128]{1,0:T(8,128)(2,1)S(1)}, bf16[1040,128]{1,0:T(8,128)(2,1)S(1)}, u32[]{:S(2)}, u32[]{:S(2)}) collective-permute-start(bf16[1040,128]{1,0:T(8,128)(2,1)S(1)} %collective-permute-done.4.refs_0_), channel_id=1, source_target_pairs={{0,4},{4,8},{8,12},{12,14},{14,10},{10,6},{6,2},{2,0},{1,5},{5,9},... | collective-permute-start | bytes 798728 | tf_op jit(solution)/shard_map/ppermute | solution.py:498
  27.6 9.8 %collective-permute-start.9 = (bf16[1040,128]{1,0:T(8,128)(2,1)S(1)}, bf16[1040,128]{1,0:T(8,128)(2,1)S(1)}, u32[]{:S(2)}, u32[]{:S(2)}) collective-permute-start(bf16[1040,128]{1,0:T(8,128)(2,1)S(1)} %collective-permute-done.5.refs_3_), channel_id=1, source_target_pairs={{4,0},{8,4},{12,8},{14,12},{10,14},{6,10},{2,6},{0,2},{5,1},{9,5},... | collective-permute-start | bytes 798728 | tf_op jit(solution)/shard_map/ppermute | solution.py:498
  28.1 18.9 %collective-permute-start.12 = (bf16[2,128,1024]{2,1,0:T(8,128)(2,1)S(1)}, bf16[2,128,1024]{2,1,0:T(8,128)(2,1)S(1)}, u32[]{:S(2)}, u32[]{:S(2)}) collective-permute-start(bf16[2,128,1024]{2,1,0:T(8,128)(2,1)S(1)} %get-tuple-element.89.refs_0_), channel_id=1, source_target_pairs={{0,1},{1,0},{2,3},{3,2},{4,5},{5,4},{6,7},{7,6},{8,9},{9,8},{10,11... | collective-permute-start | bytes 1572872 | tf_op jit(solution)/shard_map/ppermute | solution.py:501
  31.8 9.3 %collective-permute-start.10 = (bf16[1040,128]{1,0:T(8,128)(2,1)S(1)}, bf16[1040,128]{1,0:T(8,128)(2,1)S(1)}, u32[]{:S(2)}, u32[]{:S(2)}) collective-permute-start(bf16[1040,128]{1,0:T(8,128)(2,1)S(1)} %collective-permute-done.6.refs_1_), channel_id=1, source_target_pairs={{0,4},{4,8},{8,12},{12,14},{14,10},{10,6},{6,2},{2,0},{1,5},{5,9},... | collective-permute-start | bytes 798728 | tf_op jit(solution)/shard_map/ppermute | solution.py:498
  33.3 9.8 %collective-permute-start.11 = (bf16[1040,128]{1,0:T(8,128)(2,1)S(1)}, bf16[1040,128]{1,0:T(8,128)(2,1)S(1)}, u32[]{:S(2)}, u32[]{:S(2)}) collective-permute-start(bf16[1040,128]{1,0:T(8,128)(2,1)S(1)} %collective-permute-done.7.refs_2_), channel_id=1, source_target_pairs={{4,0},{8,4},{12,8},{14,12},{10,14},{6,10},{2,6},{0,2},{5,1},{9,5},... | collective-permute-start | bytes 798728 | tf_op jit(solution)/shard_map/ppermute | solution.py:498
  37.5 9.5 %collective-permute-start.13 = (bf16[1040,128]{1,0:T(8,128)(2,1)S(1)}, bf16[1040,128]{1,0:T(8,128)(2,1)S(1)}, u32[]{:S(2)}, u32[]{:S(2)}) collective-permute-start(bf16[1040,128]{1,0:T(8,128)(2,1)S(1)} %collective-permute-done.8.refs_0_), channel_id=1, source_target_pairs={{0,4},{4,8},{8,12},{12,14},{14,10},{10,6},{6,2},{2,0},{1,5},{5,9},... | collective-permute-start | bytes 798728 | tf_op jit(solution)/shard_map/ppermute | solution.py:498
  39.0 8.4 %collective-permute-start.14 = (bf16[1040,128]{1,0:T(8,128)(2,1)S(1)}, bf16[1040,128]{1,0:T(8,128)(2,1)S(1)}, u32[]{:S(2)}, u32[]{:S(2)}) collective-permute-start(bf16[1040,128]{1,0:T(8,128)(2,1)S(1)} %collective-permute-done.9.refs_3_), channel_id=1, source_target_pairs={{4,0},{8,4},{12,8},{14,12},{10,14},{6,10},{2,6},{0,2},{5,1},{9,5},... | collective-permute-start | bytes 798728 | tf_op jit(solution)/shard_map/ppermute | solution.py:498
  41.1 9.3 %collective-permute-start.15 = (bf16[2,256,1024]{2,1,0:T(8,128)(2,1)S(1)}, bf16[2,256,1024]{2,1,0:T(8,128)(2,1)S(1)}, u32[]{:S(2)}, u32[]{:S(2)}) collective-permute-start(bf16[2,256,1024]{2,1,0:T(8,128)(2,1)S(1)} %get-tuple-element.95.refs_1_), channel_id=1, source_target_pairs={{0,1},{1,0},{2,3},{3,2},{4,5},{5,4},{6,7},{7,6},{8,9},{9,8},{10,11... | collective-permute-start | bytes 3145736 | tf_op jit(solution)/shard_map/ppermute | solution.py:501
  43.2 7.2 %collective-permute-start.16 = (bf16[2,256,1024]{2,1,0:T(8,128)(2,1)S(1)}, bf16[2,256,1024]{2,1,0:T(8,128)(2,1)S(1)}, u32[]{:S(2)}, u32[]{:S(2)}) collective-permute-start(bf16[2,256,1024]{2,1,0:T(8,128)(2,1)S(1)} %get-tuple-element.108.refs_2_), channel_id=1, source_target_pairs={{0,1},{1,0},{2,3},{3,2},{4,5},{5,4},{6,7},{7,6},{8,9},{9,8},{10,11... | collective-permute-start | bytes 3145736 | tf_op jit(solution)/shard_map/ppermute | solution.py:501
  47.4 3.0 %collective-permute-start.17 = (bf16[2,256,1024]{2,1,0:T(8,128)(2,1)S(1)}, bf16[2,256,1024]{2,1,0:T(8,128)(2,1)S(1)}, u32[]{:S(2)}, u32[]{:S(2)}) collective-permute-start(bf16[2,256,1024]{2,1,0:T(8,128)(2,1)S(1)} %get-tuple-element.120.refs_3_), channel_id=1, source_target_pairs={{0,1},{1,0},{2,3},{3,2},{4,5},{5,4},{6,7},{7,6},{8,9},{9,8},{10,11... | collective-permute-start | bytes 3145736 | tf_op jit(solution)/shard_map/ppermute | solution.py:501
  49.1 2.0 %collective-permute-start.18 = (bf16[2,128,1024]{2,1,0:T(8,128)(2,1)S(1)}, bf16[2,128,1024]{2,1,0:T(8,128)(2,1)S(1)}, u32[]{:S(2)}, u32[]{:S(2)}) collective-permute-start(bf16[2,128,1024]{2,1,0:T(8,128)(2,1)S(1)} %get-tuple-element.125.refs_4_), channel_id=1, source_target_pairs={{0,1},{1,0},{2,3},{3,2},{4,5},{5,4},{6,7},{7,6},{8,9},{9,8},{10,11... | collective-permute-start | bytes 1572872 | tf_op jit(solution)/shard_map/ppermute | solution.py:501
  55.3 22.0 %collective-permute-start.19 = (bf16[40,2048]{1,0:T(8,128)(2,1)S(1)}, bf16[40,2048]{1,0:T(8,128)(2,1)S(1)}, u32[]{:S(2)}, u32[]{:S(2)}) collective-permute-start(bf16[40,2048]{1,0:T(8,128)(2,1)S(1)} %get-tuple-element.150), channel_id=1, source_target_pairs={{0,8},{2,10},{4,12},{6,14},{8,0},{10,2},{12,4},{14,6},{1,9},{3,11}... | collective-permute-start | bytes 491528 | tf_op jit(solution)/shard_map/ppermute | solution.py:541
  56.0 24.6 %collective-permute-start.20 = (bf16[40,2048]{1,0:T(8,128)(2,1)S(1)}, bf16[40,2048]{1,0:T(8,128)(2,1)S(1)}, u32[]{:S(2)}, u32[]{:S(2)}) collective-permute-start(bf16[40,2048]{1,0:T(8,128)(2,1)S(1)} %get-tuple-element.153), channel_id=1, source_target_pairs={{0,10},{2,8},{4,14},{6,12},{8,2},{10,0},{12,6},{14,4},{1,11},{3,9}... | collective-permute-start | bytes 491528 | tf_op jit(solution)/shard_map/ppermute | solution.py:541
  63.3 19.0 %copy-start.7 = (bf16[1040,128]{1,0:T(8,128)(2,1)S(1)}, bf16[1040,128]{1,0:T(8,128)(2,1)}, u32[]{:S(2)}) copy-start(bf16[1040,128]{1,0:T(8,128)(2,1)} %get-tuple-element.82.top_ref.refs_0_) | copy-start | bytes 798724
  63.3 19.0 %copy-start.9 = (bf16[1040,128]{1,0:T(8,128)(2,1)S(1)}, bf16[1040,128]{1,0:T(8,128)(2,1)}, u32[]{:S(2)}) copy-start(bf16[1040,128]{1,0:T(8,128)(2,1)} %get-tuple-element.83.bottom_ref.refs_1_) | copy-start | bytes 798724
  63.3 19.0 %copy-start.10 = (f32[2048,8]{0,1:T(8,128)S(1)}, f32[2048,8]{0,1:T(8,128)}, u32[]{:S(2)}) copy-start(f32[2048,8]{0,1:T(8,128)} %param.10) | copy-start | bytes 196612
  63.3 19.5 %collective-permute-start.21 = (bf16[40,2048]{1,0:T(8,128)(2,1)S(1)}, bf16[40,2048]{1,0:T(8,128)(2,1)S(1)}, u32[]{:S(2)}, u32[]{:S(2)}) collective-permute-start(bf16[40,2048]{1,0:T(8,128)(2,1)S(1)} %get-tuple-element.154), channel_id=1, source_target_pairs={{0,12},{2,14},{4,8},{6,10},{8,4},{10,6},{12,0},{14,2},{1,13},{3,15... | collective-permute-start | bytes 491528 | tf_op jit(solution)/shard_map/ppermute | solution.py:541
  63.4 19.4 %collective-permute-start.22 = (bf16[40,2048]{1,0:T(8,128)(2,1)S(1)}, bf16[40,2048]{1,0:T(8,128)(2,1)S(1)}, u32[]{:S(2)}, u32[]{:S(2)}) collective-permute-start(bf16[40,2048]{1,0:T(8,128)(2,1)S(1)} %get-tuple-element.155), channel_id=1, source_target_pairs={{0,14},{2,12},{4,10},{6,8},{8,6},{10,4},{12,2},{14,0},{1,15},{3,13... | collective-permute-start | bytes 491528 | tf_op jit(solution)/shard_map/ppermute | solution.py:541
  77.3 8.0 %collective-permute-start.23 = (bf16[40,2048]{1,0:T(8,128)(2,1)S(1)}, bf16[40,2048]{1,0:T(8,128)(2,1)S(1)}, u32[]{:S(2)}, u32[]{:S(2)}) collective-permute-start(bf16[40,2048]{1,0:T(8,128)(2,1)S(1)} %get-tuple-element.156), channel_id=1, source_target_pairs={{0,6},{2,4},{4,2},{6,0},{8,14},{10,12},{12,10},{14,8},{1,7},{3,5},... | collective-permute-start | bytes 491528 | tf_op jit(solution)/shard_map/ppermute | solution.py:541
  77.3 10.0 %collective-permute-start.24 = (bf16[40,2048]{1,0:T(8,128)(2,1)S(1)}, bf16[40,2048]{1,0:T(8,128)(2,1)S(1)}, u32[]{:S(2)}, u32[]{:S(2)}) collective-permute-start(bf16[40,2048]{1,0:T(8,128)(2,1)S(1)} %get-tuple-element.157), channel_id=1, source_target_pairs={{0,4},{2,6},{4,0},{6,2},{8,12},{10,14},{12,8},{14,10},{1,5},{3,7},... | collective-permute-start | bytes 491528 | tf_op jit(solution)/shard_map/ppermute | solution.py:541
  80.6 6.7 %collective-permute-start.25 = (bf16[40,2048]{1,0:T(8,128)(2,1)S(1)}, bf16[40,2048]{1,0:T(8,128)(2,1)S(1)}, u32[]{:S(2)}, u32[]{:S(2)}) collective-permute-start(bf16[40,2048]{1,0:T(8,128)(2,1)S(1)} %get-tuple-element.158), channel_id=1, source_target_pairs={{0,2},{2,0},{4,6},{6,4},{8,10},{10,8},{12,14},{14,12},{1,3},{3,1},... | collective-permute-start | bytes 491528 | tf_op jit(solution)/shard_map/ppermute | solution.py:541

commit v3 on v2

--- a/solution.py
+++ b/solution.py
@@ -550,7 +550,8 @@
             far.append([swap(piece, start + r) for r, piece in enumerate(pieces)])
         else:
             near = pieces
-    *near, far[0][0] = tie(*near, far[0][0])
+    near = list(near)
+    *near[:-1], far[0][0] = tie(*near[:-1], far[0][0])
     near = [near[0]] + [swap(near[r], r) for r in range(1, half)]
 
     pieces = [*near, *far[0], *far[1]]

time: 88.8 us -> 88.8 us (level)
  starting transfers between devices: 27.1 us -> 25.4 us
  waiting for transfers between devices: 21.8 us -> 23.5 us
    ppermute x7, starting transfers between devices: 11.3 us -> 9.6 us  [swap(): return lax.ppermute(piece, 'ctx', [(c, c ^ k) for c in range(ctx_count)])]
    ppermute x7, waiting for transfers between devices: 9.78 us -> 11.4 us  [swap(): return lax.ppermute(piece, 'ctx', [(c, c ^ k) for c in range(ctx_count)])]
where the time goes in v3:
time: 88.8 us; the launch traced here: 88.6 us
  Pallas kernels  32.9 us (37%)
  starting transfers between devices  25.4 us (29%)
  waiting for transfers between devices  23.5 us (26%)
  local copies, waits for them, and re-layouts  6.31 us (7%)
    pallas_call x3, Pallas kernels, attend(): pl.pallas_call(functools.partial(attend_kernel, lots, heads), in_specs=[W...  14.1 us
    ppermute x7, starting transfers between devices, send(): lax.ppermute(parts[0], 'ctx', forward)  13 us
    ppermute x7, waiting for transfers between devices, swap(): return lax.ppermute(piece, 'ctx', [(c, c ^ k) for c in range(ctx_count)])  11.4 us
    ppermute x7, waiting for transfers between devices, send(): lax.ppermute(parts[1], 'ctx', backward)  11 us
    ppermute x7, starting transfers between devices, swap(): return lax.ppermute(piece, 'ctx', [(c, c ^ k) for c in range(ctx_count)])  9.6 us
    unnamed x22, local copies, waits for them, and re-layouts  6.31 us
    pallas_call x5, Pallas kernels, project_values(): pl.pallas_call(functools.partial(values_kernel, half, offsets, len(blocks...  6.15 us
    pallas_call x5, Pallas kernels, project_keys(): pl.pallas_call(functools.partial(keys_kernel, half, len(blocks)), in_spec...  5.29 us
  transfers between devices with their start and end apart: 26, of which 15 were waited for; matrix products, arithmetic and copies ran while one was open for 0% of the time, Pallas kernels for 29%

profile of v3, /device:TPU:0, one launch (start us, length us, event | category | flops | bytes accessed | tf_op | source)
XLA Modules:
  0.0 88.6 jit_solution(2741820365791198542)
XLA Ops:
  0.0 2.0 %norm_rows.1 = (bf16[1040,128]{1,0:T(8,128)(2,1)}, bf16[1040,128]{1,0:T(8,128)(2,1)}) custom-call(bf16[128,2048]{1,0:T(8,128)(2,1)} %refs_0_.1, f32[1,2048]{1,0:T(1,128)} %bitcast.15, s32[2,128]{1,0:T(2,128)} %bitcast.16), custom_call_target="tpu_custom_call" | custom-call | tf_op jit(solution)/shard_map/norm_rows/pallas_call | solution.py:85
  2.0 3.1 %collective-permute-start = (bf16[1040,128]{1,0:T(8,128)(2,1)}, bf16[1040,128]{1,0:T(8,128)(2,1)S(1)}, u32[]{:S(2)}, u32[]{:S(2)}) collective-permute-start(bf16[1040,128]{1,0:T(8,128)(2,1)} %get-tuple-element.81.top_ref.refs_0_), channel_id=1, source_target_pairs={{0,4},{4,8},{8,12},{12,14},{14,10},{10,6},{6,2},{2,0},{1,5},{5,9},... | collective-permute-start | bytes 798728 | tf_op jit(solution)/shard_map/ppermute | solution.py:498
  5.1 0.0 collective-permute-start.1
  5.1 2.0 %collective-permute-start.2 = (bf16[1040,128]{1,0:T(8,128)(2,1)}, bf16[1040,128]{1,0:T(8,128)(2,1)S(1)}, u32[]{:S(2)}, u32[]{:S(2)}) collective-permute-start(bf16[1040,128]{1,0:T(8,128)(2,1)} %get-tuple-element.82.bottom_ref.refs_1_), channel_id=1, source_target_pairs={{0,4},{4,8},{8,12},{12,14},{14,10},{10,6},{6,2},{2,0},{1,5},{5,9},... | collective-permute-start | bytes 798728 | tf_op jit(solution)/shard_map/ppermute | solution.py:498
  7.1 0.0 collective-permute-start.3
  7.2 2.2 %copy-done.1 = bf16[2048,1024]{1,0:T(8,128)(2,1)S(1)} copy-done((bf16[2048,1024]{1,0:T(8,128)(2,1)S(1)}, bf16[2048,1024]{1,0:T(8,128)(2,1)}, u32[]{:S(2)}) %copy-start.1) | copy-done | bytes 4194328
  9.3 0.9 %copy-done.6 = bf16[1040,128]{1,0:T(8,128)(2,1)S(1)} copy-done((bf16[1040,128]{1,0:T(8,128)(2,1)S(1)}, bf16[1040,128]{1,0:T(8,128)(2,1)}, u32[]{:S(2)}) %copy-start.6) | copy-done | bytes 266264
  10.3 0.9 %copy-done.8 = bf16[1040,128]{1,0:T(8,128)(2,1)S(1)} copy-done((bf16[1040,128]{1,0:T(8,128)(2,1)S(1)}, bf16[1040,128]{1,0:T(8,128)(2,1)}, u32[]{:S(2)}) %copy-start.8) | copy-done | bytes 266264
  11.2 0.7 project_keys.5
  12.0 0.5 collective-permute-done.refs_0_
  12.5 2.2 %collective-permute-done.1.refs_3_ = bf16[1040,128]{1,0:T(8,128)(2,1)S(1)} collective-permute-done((bf16[1040,128]{1,0:T(8,128)(2,1)}, bf16[1040,128]{1,0:T(8,128)(2,1)S(1)}, u32[]{:S(2)}, u32[]{:S(2)}) %collective-permute-start.1) | collective-permute-done | bytes 266272 | tf_op jit(solution)/shard_map/ppermute | solution.py:498
  14.6 1.6 %collective-permute-start.4 = (bf16[1040,128]{1,0:T(8,128)(2,1)S(1)}, bf16[1040,128]{1,0:T(8,128)(2,1)S(1)}, u32[]{:S(2)}, u32[]{:S(2)}) collective-permute-start(bf16[1040,128]{1,0:T(8,128)(2,1)S(1)} %collective-permute-done.refs_0_), channel_id=1, source_target_pairs={{0,4},{4,8},{8,12},{12,14},{14,10},{10,6},{6,2},{2,0},{1,5},{5,9},... | collective-permute-start | bytes 798728 | tf_op jit(solution)/shard_map/ppermute | solution.py:498
  16.2 0.4 collective-permute-start.5
  16.7 2.2 %copy-done.3 = bf16[2048,1024]{1,0:T(8,128)(2,1)S(1)} copy-done((bf16[2048,1024]{1,0:T(8,128)(2,1)S(1)}, bf16[2048,1024]{1,0:T(8,128)(2,1)}, u32[]{:S(2)}) %copy-start.3) | copy-done | bytes 4194328
  18.9 0.8 project_values.5
  19.7 0.6 collective-permute-done.3.refs_2_
  20.3 1.6 %collective-permute-start.6 = (bf16[1040,128]{1,0:T(8,128)(2,1)S(1)}, bf16[1040,128]{1,0:T(8,128)(2,1)S(1)}, u32[]{:S(2)}, u32[]{:S(2)}) collective-permute-start(bf16[1040,128]{1,0:T(8,128)(2,1)S(1)} %collective-permute-done.2.refs_1_), channel_id=1, source_target_pairs={{0,4},{4,8},{8,12},{12,14},{14,10},{10,6},{6,2},{2,0},{1,5},{5,9},... | collective-permute-start | bytes 798728 | tf_op jit(solution)/shard_map/ppermute | solution.py:498
  21.9 0.4 collective-permute-start.7
  22.4 1.3 %project_keys.6 = (bf16[256,1024]{1,0:T(8,128)(2,1)S(1)}, f32[8,128]{1,0:T(8,128)S(1)}) custom-call(bf16[1040,128]{1,0:T(8,128)(2,1)S(1)} %collective-permute-done.refs_0_, bf16[1040,128]{1,0:T(8,128)(2,1)S(1)} %collective-permute-done.2.refs_1_, bf16[1040,128]{1,0:T(8,128)(2,1)S(1)} %collective-permute-done.3.refs_2_, ...), custom_call_target="tpu_custom_call" | custom-call | tf_op jit(solution)/shard_map/project_keys/pallas_call | solution.py:115
  23.7 0.3 collective-permute-done.4.refs_0_
  24.0 2.1 %collective-permute-done.5.refs_3_ = bf16[1040,128]{1,0:T(8,128)(2,1)S(1)} collective-permute-done((bf16[1040,128]{1,0:T(8,128)(2,1)S(1)}, bf16[1040,128]{1,0:T(8,128)(2,1)S(1)}, u32[]{:S(2)}, u32[]{:S(2)}) %collective-permute-start.5) | collective-permute-done | bytes 266272 | tf_op jit(solution)/shard_map/ppermute | solution.py:498
  26.1 1.6 %collective-permute-start.8 = (bf16[1040,128]{1,0:T(8,128)(2,1)S(1)}, bf16[1040,128]{1,0:T(8,128)(2,1)S(1)}, u32[]{:S(2)}, u32[]{:S(2)}) collective-permute-start(bf16[1040,128]{1,0:T(8,128)(2,1)S(1)} %collective-permute-done.4.refs_0_), channel_id=1, source_target_pairs={{0,4},{4,8},{8,12},{12,14},{14,10},{10,6},{6,2},{2,0},{1,5},{5,9},... | collective-permute-start | bytes 798728 | tf_op jit(solution)/shard_map/ppermute | solution.py:498
  27.6 0.4 collective-permute-start.9
  28.1 1.5 %project_values.6 = (bf16[2,256,1024]{2,1,0:T(8,128)(2,1)S(1)}, bf16[2,48,2048]{2,1,0:T(8,128)(2,1)S(1)}, f32[2,48,128]{2,1,0:T(8,128)S(1)}) custom-call(f32[8,128]{1,0:T(8,128)S(1)} %get-tuple-element.92.mark_ref, bf16[256,1024]{1,0:T(8,128)(2,1)S(1)} %get-tuple-element.93.keys_ref, bf16[1040,128]{1,0:T(8,128)(2,1)S(1)} %collective-permute-done.refs_0_, ...), custom_call_target="tpu_custom_call" | custom-call | tf_op jit(solution)/shard_map/project_values/pallas_call | solution.py:160
  29.6 0.1 collective-permute-done.6.refs_1_
  29.7 2.1 %collective-permute-done.7.refs_2_ = bf16[1040,128]{1,0:T(8,128)(2,1)S(1)} collective-permute-done((bf16[1040,128]{1,0:T(8,128)(2,1)S(1)}, bf16[1040,128]{1,0:T(8,128)(2,1)S(1)}, u32[]{:S(2)}, u32[]{:S(2)}) %collective-permute-start.7) | collective-permute-done | bytes 266272 | tf_op jit(solution)/shard_map/ppermute | solution.py:498
  31.8 1.6 %collective-permute-start.10 = (bf16[1040,128]{1,0:T(8,128)(2,1)S(1)}, bf16[1040,128]{1,0:T(8,128)(2,1)S(1)}, u32[]{:S(2)}, u32[]{:S(2)}) collective-permute-start(bf16[1040,128]{1,0:T(8,128)(2,1)S(1)} %collective-permute-done.6.refs_1_), channel_id=1, source_target_pairs={{0,4},{4,8},{8,12},{12,14},{14,10},{10,6},{6,2},{2,0},{1,5},{5,9},... | collective-permute-start | bytes 798728 | tf_op jit(solution)/shard_map/ppermute | solution.py:498
  33.3 0.4 collective-permute-start.11
  33.8 0.8 project_queries.3
  34.6 1.3 %project_keys.7 = (bf16[256,1024]{1,0:T(8,128)(2,1)S(1)}, f32[8,128]{1,0:T(8,128)S(1)}) custom-call(bf16[1040,128]{1,0:T(8,128)(2,1)S(1)} %collective-permute-done.4.refs_0_, bf16[1040,128]{1,0:T(8,128)(2,1)S(1)} %collective-permute-done.6.refs_1_, bf16[1040,128]{1,0:T(8,128)(2,1)S(1)} %collective-permute-done.7.refs_2_, ...), custom_call_target="tpu_custom_call" | custom-call | tf_op jit(solution)/shard_map/project_keys/pallas_call | solution.py:115
  35.9 1.6 %collective-permute-done.9.refs_3_ = bf16[1040,128]{1,0:T(8,128)(2,1)S(1)} collective-permute-done((bf16[1040,128]{1,0:T(8,128)(2,1)S(1)}, bf16[1040,128]{1,0:T(8,128)(2,1)S(1)}, u32[]{:S(2)}, u32[]{:S(2)}) %collective-permute-start.9) | collective-permute-done | bytes 266272 | tf_op jit(solution)/shard_map/ppermute | solution.py:498
  37.5 1.6 %collective-permute-start.13 = (bf16[1040,128]{1,0:T(8,128)(2,1)S(1)}, bf16[1040,128]{1,0:T(8,128)(2,1)S(1)}, u32[]{:S(2)}, u32[]{:S(2)}) collective-permute-start(bf16[1040,128]{1,0:T(8,128)(2,1)S(1)} %collective-permute-done.8.refs_0_), channel_id=1, source_target_pairs={{0,4},{4,8},{8,12},{12,14},{14,10},{10,6},{6,2},{2,0},{1,5},{5,9},... | collective-permute-start | bytes 798728 | tf_op jit(solution)/shard_map/ppermute | solution.py:498
  39.0 0.4 collective-permute-start.14
  39.5 1.5 %project_values.7 = (bf16[2,256,1024]{2,1,0:T(8,128)(2,1)S(1)}, bf16[2,48,2048]{2,1,0:T(8,128)(2,1)S(1)}, f32[2,48,128]{2,1,0:T(8,128)S(1)}) custom-call(f32[8,128]{1,0:T(8,128)S(1)} %get-tuple-element.105.mark_ref, bf16[256,1024]{1,0:T(8,128)(2,1)S(1)} %get-tuple-element.106.keys_ref, bf16[1040,128]{1,0:T(8,128)(2,1)S(1)} %collective-permute-done.4.refs_0_, ...), custom_call_target="tpu_custom_call" | custom-call | tf_op jit(solution)/shard_map/project_values/pallas_call | solution.py:160
  41.0 0.1 collective-permute-done.10.refs_1_
  41.1 2.1 %collective-permute-done.11.refs_2_ = bf16[1040,128]{1,0:T(8,128)(2,1)S(1)} collective-permute-done((bf16[1040,128]{1,0:T(8,128)(2,1)S(1)}, bf16[1040,128]{1,0:T(8,128)(2,1)S(1)}, u32[]{:S(2)}, u32[]{:S(2)}) %collective-permute-start.11) | collective-permute-done | bytes 266272 | tf_op jit(solution)/shard_map/ppermute | solution.py:498
  43.2 1.3 %project_keys.8 = (bf16[256,1024]{1,0:T(8,128)(2,1)S(1)}, f32[8,128]{1,0:T(8,128)S(1)}) custom-call(bf16[1040,128]{1,0:T(8,128)(2,1)S(1)} %collective-permute-done.8.refs_0_, bf16[1040,128]{1,0:T(8,128)(2,1)S(1)} %collective-permute-done.10.refs_1_, bf16[1040,128]{1,0:T(8,128)(2,1)S(1)} %collective-permute-done.11.refs_2_, ...), custom_call_target="tpu_custom_call" | custom-call | tf_op jit(solution)/shard_map/project_keys/pallas_call | solution.py:115
  44.5 1.5 %project_values.8 = (bf16[2,256,1024]{2,1,0:T(8,128)(2,1)S(1)}, bf16[2,48,2048]{2,1,0:T(8,128)(2,1)S(1)}, f32[2,48,128]{2,1,0:T(8,128)S(1)}) custom-call(f32[8,128]{1,0:T(8,128)S(1)} %get-tuple-element.111.mark_ref, bf16[256,1024]{1,0:T(8,128)(2,1)S(1)} %get-tuple-element.112.keys_ref, bf16[1040,128]{1,0:T(8,128)(2,1)S(1)} %collective-permute-done.8.refs_0_, ...), custom_call_target="tpu_custom_call" | custom-call | tf_op jit(solution)/shard_map/project_values/pallas_call | solution.py:160
  46.0 1.0 %project_queries.4 = (bf16[2,48,1024]{2,1,0:T(8,128)(2,1)S(1)}, bf16[2,48,1024]{2,1,0:T(8,128)(2,1)S(1)}) custom-call(bf16[2,48,2048]{2,1,0:T(8,128)(2,1)S(1)} %get-tuple-element.114.refs_0_, bf16[2,48,2048]{2,1,0:T(8,128)(2,1)S(1)} %get-tuple-element.115.refs_1_, bf16[2048,1024]{1,0:T(8,128)(2,1)S(1)} %bitcast.12, bf16[1024,2048]{1,0:T(8,128)(2,1)S(1)} %bitcast.6), custom_call_target="tpu_custom_call" | custom-call | tf_op jit(solution)/shard_map/project_queries/pallas_call | solution.py:189
  47.0 0.4 collective-permute-done.14.refs_1_
  47.4 0.1 collective-permute-start.17
  47.6 0.7 project_keys.9
  48.3 0.8 project_values.9
  49.1 0.4 collective-permute-start.18
  49.5 0.8 project_queries.5.refs_9_
  50.4 0.7 arrange.1
  51.1 0.0 collective-permute-done.18.other_ref
  51.1 0.1 arrange_last.1.panel_ref
  51.2 4.1 %attend.3 = (bf16[40,2048]{1,0:T(8,128)(2,1)S(1)}, bf16[40,2048]{1,0:T(8,128)(2,1)S(1)}) custom-call(bf16[2,16,128,1024]{3,2,1,0:T(8,128)(2,1)S(1)} %arrange_last.1.panel_ref, f32[8,40,1024]{2,1,0:T(8,128)S(1)} %get-tuple-element.137.queries_ref, f32[8,40,128]{2,1,0:T(8,128)S(1)} %get-tuple-element.144.places_ref, bf16[1024,2048]{1,0:T(8,128)(2,1)S(1)} %bitcast.8), custom_call_target="tpu_custom_call" | custom-call | flops 603979776 | bytes 8388608 | tf_op jit(solution)/shard_map/attend/pallas_call | solution.py:345
  55.3 0.7 collective-permute-start.19
  56.0 2.0 %collective-permute-start.20 = (bf16[40,2048]{1,0:T(8,128)(2,1)S(1)}, bf16[40,2048]{1,0:T(8,128)(2,1)S(1)}, u32[]{:S(2)}, u32[]{:S(2)}) collective-permute-start(bf16[40,2048]{1,0:T(8,128)(2,1)S(1)} %get-tuple-element.151), channel_id=1, source_target_pairs={{0,10},{2,8},{4,14},{6,12},{8,2},{10,0},{12,6},{14,4},{1,11},{3,9}... | collective-permute-start | bytes 491528 | tf_op jit(solution)/shard_map/ppermute | solution.py:541
  58.0 5.3 %attend.4 = (bf16[40,2048]{1,0:T(8,128)(2,1)S(1)}, bf16[40,2048]{1,0:T(8,128)(2,1)S(1)}) custom-call(bf16[2,16,128,1024]{3,2,1,0:T(8,128)(2,1)S(1)} %arrange_last.1.panel_ref, f32[8,40,1024]{2,1,0:T(8,128)S(1)} %get-tuple-element.137.queries_ref, f32[8,40,128]{2,1,0:T(8,128)S(1)} %get-tuple-element.144.places_ref, bf16[1024,2048]{1,0:T(8,128)(2,1)S(1)} %bitcast.9), custom_call_target="tpu_custom_call" | custom-call | flops 603979776 | bytes 8388608 | tf_op jit(solution)/shard_map/attend/pallas_call | solution.py:345
  63.3 0.1 collective-permute-start.21
  63.4 5.0 %collective-permute-start.22 = (bf16[40,2048]{1,0:T(8,128)(2,1)S(1)}, bf16[40,2048]{1,0:T(8,128)(2,1)S(1)}, u32[]{:S(2)}, u32[]{:S(2)}) collective-permute-start(bf16[40,2048]{1,0:T(8,128)(2,1)S(1)} %get-tuple-element.153), channel_id=1, source_target_pairs={{0,14},{2,12},{4,10},{6,8},{8,6},{10,4},{12,2},{14,0},{1,15},{3,13... | collective-permute-start | bytes 491528 | tf_op jit(solution)/shard_map/ppermute | solution.py:541
  68.4 4.7 %attend.5 = (bf16[40,2048]{1,0:T(8,128)(2,1)S(1)}, bf16[40,2048]{1,0:T(8,128)(2,1)S(1)}, bf16[40,2048]{1,0:T(8,128)(2,1)S(1)}, bf16[40,2048]{1,0:T(8,128)(2,1)S(1)}) custom-call(bf16[2,16,128,1024]{3,2,1,0:T(8,128)(2,1)S(1)} %arrange_last.1.panel_ref, f32[8,40,1024]{2,1,0:T(8,128)S(1)} %get-tuple-element.137.queries_ref, ...), custom_call_target="tpu_custom_call" | custom-call | flops 1207959552 | bytes 8388608 | tf_op jit(solution)/shard_map/attend/pallas_call | solution.py:345
  73.1 0.1 collective-permute-start.23
  73.2 4.2 %collective-permute-done.19.refs_1_ = bf16[40,2048]{1,0:T(8,128)(2,1)S(1)} collective-permute-done((bf16[40,2048]{1,0:T(8,128)(2,1)S(1)}, bf16[40,2048]{1,0:T(8,128)(2,1)S(1)}, u32[]{:S(2)}, u32[]{:S(2)}) %collective-permute-start.19) | collective-permute-done | bytes 163872 | tf_op jit(solution)/shard_map/ppermute | solution.py:541
  77.4 3.2 %collective-permute-done.20.refs_2_ = bf16[40,2048]{1,0:T(8,128)(2,1)S(1)} collective-permute-done((bf16[40,2048]{1,0:T(8,128)(2,1)S(1)}, bf16[40,2048]{1,0:T(8,128)(2,1)S(1)}, u32[]{:S(2)}, u32[]{:S(2)}) %collective-permute-start.20) | collective-permute-done | bytes 163872 | tf_op jit(solution)/shard_map/ppermute | solution.py:541
  80.6 1.7 %collective-permute-start.25 = (bf16[40,2048]{1,0:T(8,128)(2,1)S(1)}, bf16[40,2048]{1,0:T(8,128)(2,1)S(1)}, u32[]{:S(2)}, u32[]{:S(2)}) collective-permute-start(bf16[40,2048]{1,0:T(8,128)(2,1)S(1)} %get-tuple-element.156), channel_id=1, source_target_pairs={{0,2},{2,0},{4,6},{6,4},{8,10},{10,8},{12,14},{14,12},{1,3},{3,1},... | collective-permute-start | bytes 491528 | tf_op jit(solution)/shard_map/ppermute | solution.py:541
  82.3 0.5 gate_mix.1
  82.8 0.4 combine.2.refs_0_
  83.3 0.3 collective-permute-done.23.refs_1_
  83.6 3.7 %collective-permute-done.24.refs_2_ = bf16[40,2048]{1,0:T(8,128)(2,1)S(1)} collective-permute-done((bf16[40,2048]{1,0:T(8,128)(2,1)S(1)}, bf16[40,2048]{1,0:T(8,128)(2,1)S(1)}, u32[]{:S(2)}, u32[]{:S(2)}) %collective-permute-start.24) | collective-permute-done | bytes 163872 | tf_op jit(solution)/shard_map/ppermute | solution.py:541
  87.3 1.1 %combine.3 = bf16[128,2048]{1,0:T(8,128)(2,1)} custom-call(bf16[256,144]{1,0:T(8,128)(2,1)S(1)} %get-tuple-element.83.mix_ref, f32[128,2048]{1,0:T(8,128)S(1)} %combine.2.refs_0_, bf16[40,2048]{1,0:T(8,128)(2,1)S(1)} %collective-permute-done.23.refs_1_, bf16[40,2048]{1,0:T(8,128)(2,1)S(1)} %collective-permute-done.24.refs_2_, ...), custom_call_target="tpu_custom_call" | custom-call | tf_op jit(solution)/shard_map/combine/pallas_call | solution.py:461
  (32 shorter events, 0.1 us)
Async XLA Ops:
  2.0 10.5 %collective-permute-start = (bf16[1040,128]{1,0:T(8,128)(2,1)}, bf16[1040,128]{1,0:T(8,128)(2,1)S(1)}, u32[]{:S(2)}, u32[]{:S(2)}) collective-permute-start(bf16[1040,128]{1,0:T(8,128)(2,1)} %get-tuple-element.81.top_ref.refs_0_), channel_id=1, source_target_pairs={{0,4},{4,8},{8,12},{12,14},{14,10},{10,6},{6,2},{2,0},{1,5},{5,9},... | collective-permute-start | bytes 798728 | tf_op jit(solution)/shard_map/ppermute | solution.py:498
  5.1 9.5 %collective-permute-start.1 = (bf16[1040,128]{1,0:T(8,128)(2,1)}, bf16[1040,128]{1,0:T(8,128)(2,1)S(1)}, u32[]{:S(2)}, u32[]{:S(2)}) collective-permute-start(bf16[1040,128]{1,0:T(8,128)(2,1)} %get-tuple-element.82.bottom_ref.refs_1_), channel_id=1, source_target_pairs={{4,0},{8,4},{12,8},{14,12},{10,14},{6,10},{2,6},{0,2},{5,1},{9,5},... | collective-permute-start | bytes 798728 | tf_op jit(solution)/shard_map/ppermute | solution.py:498
  5.1 14.6 %collective-permute-start.2 = (bf16[1040,128]{1,0:T(8,128)(2,1)}, bf16[1040,128]{1,0:T(8,128)(2,1)S(1)}, u32[]{:S(2)}, u32[]{:S(2)}) collective-permute-start(bf16[1040,128]{1,0:T(8,128)(2,1)} %get-tuple-element.82.bottom_ref.refs_1_), channel_id=1, source_target_pairs={{0,4},{4,8},{8,12},{12,14},{14,10},{10,6},{6,2},{2,0},{1,5},{5,9},... | collective-permute-start | bytes 798728 | tf_op jit(solution)/shard_map/ppermute | solution.py:498
  7.1 13.2 %collective-permute-start.3 = (bf16[1040,128]{1,0:T(8,128)(2,1)}, bf16[1040,128]{1,0:T(8,128)(2,1)S(1)}, u32[]{:S(2)}, u32[]{:S(2)}) collective-permute-start(bf16[1040,128]{1,0:T(8,128)(2,1)} %get-tuple-element.81.top_ref.refs_0_), channel_id=1, source_target_pairs={{4,0},{8,4},{12,8},{14,12},{10,14},{6,10},{2,6},{0,2},{5,1},{9,5},... | collective-permute-start | bytes 798728 | tf_op jit(solution)/shard_map/ppermute | solution.py:498
  7.1 2.2 %copy-start.1 = (bf16[2048,1024]{1,0:T(8,128)(2,1)S(1)}, bf16[2048,1024]{1,0:T(8,128)(2,1)}, u32[]{:S(2)}) copy-start(bf16[2048,1024]{1,0:T(8,128)(2,1)} %refs_2_.6) | copy-start | bytes 12582916
  9.3 1.0 %copy-start.6 = (bf16[1040,128]{1,0:T(8,128)(2,1)S(1)}, bf16[1040,128]{1,0:T(8,128)(2,1)}, u32[]{:S(2)}) copy-start(bf16[1040,128]{1,0:T(8,128)(2,1)} %get-tuple-element.81.top_ref.refs_0_) | copy-start | bytes 798724
  10.3 1.0 %copy-start.8 = (bf16[1040,128]{1,0:T(8,128)(2,1)S(1)}, bf16[1040,128]{1,0:T(8,128)(2,1)}, u32[]{:S(2)}) copy-start(bf16[1040,128]{1,0:T(8,128)(2,1)} %get-tuple-element.82.bottom_ref.refs_1_) | copy-start | bytes 798724
  11.2 11.1 %copy-start.2 = (bf16[2048,1024]{1,0:T(8,128)(2,1)S(1)}, bf16[2048,1024]{1,0:T(8,128)(2,1)}, u32[]{:S(2)}) copy-start(bf16[2048,1024]{1,0:T(8,128)(2,1)} %refs_2_.6) | copy-start | bytes 12582916
  14.6 9.3 %collective-permute-start.4 = (bf16[1040,128]{1,0:T(8,128)(2,1)S(1)}, bf16[1040,128]{1,0:T(8,128)(2,1)S(1)}, u32[]{:S(2)}, u32[]{:S(2)}) collective-permute-start(bf16[1040,128]{1,0:T(8,128)(2,1)S(1)} %collective-permute-done.refs_0_), channel_id=1, source_target_pairs={{0,4},{4,8},{8,12},{12,14},{14,10},{10,6},{6,2},{2,0},{1,5},{5,9},... | collective-permute-start | bytes 798728 | tf_op jit(solution)/shard_map/ppermute | solution.py:498
  16.2 9.8 %collective-permute-start.5 = (bf16[1040,128]{1,0:T(8,128)(2,1)S(1)}, bf16[1040,128]{1,0:T(8,128)(2,1)S(1)}, u32[]{:S(2)}, u32[]{:S(2)}) collective-permute-start(bf16[1040,128]{1,0:T(8,128)(2,1)S(1)} %collective-permute-done.1.refs_3_), channel_id=1, source_target_pairs={{4,0},{8,4},{12,8},{14,12},{10,14},{6,10},{2,6},{0,2},{5,1},{9,5},... | collective-permute-start | bytes 798728 | tf_op jit(solution)/shard_map/ppermute | solution.py:498
  16.7 2.2 %copy-start.3 = (bf16[2048,1024]{1,0:T(8,128)(2,1)S(1)}, bf16[2048,1024]{1,0:T(8,128)(2,1)}, u32[]{:S(2)}) copy-start(bf16[2048,1024]{1,0:T(8,128)(2,1)} %refs_2_.7) | copy-start | bytes 12582916
  18.9 9.2 %copy-start.4 = (bf16[2048,1024]{1,0:T(8,128)(2,1)S(1)}, bf16[2048,1024]{1,0:T(8,128)(2,1)}, u32[]{:S(2)}) copy-start(bf16[2048,1024]{1,0:T(8,128)(2,1)} %refs_2_.7) | copy-start | bytes 12582916
  20.3 9.3 %collective-permute-start.6 = (bf16[1040,128]{1,0:T(8,128)(2,1)S(1)}, bf16[1040,128]{1,0:T(8,128)(2,1)S(1)}, u32[]{:S(2)}, u32[]{:S(2)}) collective-permute-start(bf16[1040,128]{1,0:T(8,128)(2,1)S(1)} %collective-permute-done.2.refs_1_), channel_id=1, source_target_pairs={{0,4},{4,8},{8,12},{12,14},{14,10},{10,6},{6,2},{2,0},{1,5},{5,9},... | collective-permute-start | bytes 798728 | tf_op jit(solution)/shard_map/ppermute | solution.py:498
  21.9 9.8 %collective-permute-start.7 = (bf16[1040,128]{1,0:T(8,128)(2,1)S(1)}, bf16[1040,128]{1,0:T(8,128)(2,1)S(1)}, u32[]{:S(2)}, u32[]{:S(2)}) collective-permute-start(bf16[1040,128]{1,0:T(8,128)(2,1)S(1)} %collective-permute-done.3.refs_2_), channel_id=1, source_target_pairs={{4,0},{8,4},{12,8},{14,12},{10,14},{6,10},{2,6},{0,2},{5,1},{9,5},... | collective-permute-start | bytes 798728 | tf_op jit(solution)/shard_map/ppermute | solution.py:498
  22.4 11.4 %copy-start.5 = (bf16[1,2048,1024]{2,1,0:T(8,128)(2,1)S(1)}, bf16[1,2048,1024]{2,1,0:T(8,128)(2,1)}, u32[]{:S(2)}) copy-start(bf16[1,2048,1024]{2,1,0:T(8,128)(2,1)} %param.14) | copy-start | bytes 12582916
  23.7 10.1 %copy-start = (bf16[1,1024,2048]{2,1,0:T(8,128)(2,1)S(1)}, bf16[1,1024,2048]{2,1,0:T(8,128)(2,1)}, u32[]{:S(2)}) copy-start(bf16[1,1024,2048]{2,1,0:T(8,128)(2,1)} %param.15) | copy-start | bytes 12582916
  26.1 9.8 %collective-permute-start.8 = (bf16[1040,128]{1,0:T(8,128)(2,1)S(1)}, bf16[1040,128]{1,0:T(8,128)(2,1)S(1)}, u32[]{:S(2)}, u32[]{:S(2)}) collective-permute-start(bf16[1040,128]{1,0:T(8,128)(2,1)S(1)} %collective-permute-done.4.refs_0_), channel_id=1, source_target_pairs={{0,4},{4,8},{8,12},{12,14},{14,10},{10,6},{6,2},{2,0},{1,5},{5,9},... | collective-permute-start | bytes 798728 | tf_op jit(solution)/shard_map/ppermute | solution.py:498
  27.6 9.8 %collective-permute-start.9 = (bf16[1040,128]{1,0:T(8,128)(2,1)S(1)}, bf16[1040,128]{1,0:T(8,128)(2,1)S(1)}, u32[]{:S(2)}, u32[]{:S(2)}) collective-permute-start(bf16[1040,128]{1,0:T(8,128)(2,1)S(1)} %collective-permute-done.5.refs_3_), channel_id=1, source_target_pairs={{4,0},{8,4},{12,8},{14,12},{10,14},{6,10},{2,6},{0,2},{5,1},{9,5},... | collective-permute-start | bytes 798728 | tf_op jit(solution)/shard_map/ppermute | solution.py:498
  28.1 18.9 %collective-permute-start.12 = (bf16[2,128,1024]{2,1,0:T(8,128)(2,1)S(1)}, bf16[2,128,1024]{2,1,0:T(8,128)(2,1)S(1)}, u32[]{:S(2)}, u32[]{:S(2)}) collective-permute-start(bf16[2,128,1024]{2,1,0:T(8,128)(2,1)S(1)} %get-tuple-element.88.refs_0_), channel_id=1, source_target_pairs={{0,1},{1,0},{2,3},{3,2},{4,5},{5,4},{6,7},{7,6},{8,9},{9,8},{10,11... | collective-permute-start | bytes 1572872 | tf_op jit(solution)/shard_map/ppermute | solution.py:501
  31.8 9.3 %collective-permute-start.10 = (bf16[1040,128]{1,0:T(8,128)(2,1)S(1)}, bf16[1040,128]{1,0:T(8,128)(2,1)S(1)}, u32[]{:S(2)}, u32[]{:S(2)}) collective-permute-start(bf16[1040,128]{1,0:T(8,128)(2,1)S(1)} %collective-permute-done.6.refs_1_), channel_id=1, source_target_pairs={{0,4},{4,8},{8,12},{12,14},{14,10},{10,6},{6,2},{2,0},{1,5},{5,9},... | collective-permute-start | bytes 798728 | tf_op jit(solution)/shard_map/ppermute | solution.py:498
  33.3 9.8 %collective-permute-start.11 = (bf16[1040,128]{1,0:T(8,128)(2,1)S(1)}, bf16[1040,128]{1,0:T(8,128)(2,1)S(1)}, u32[]{:S(2)}, u32[]{:S(2)}) collective-permute-start(bf16[1040,128]{1,0:T(8,128)(2,1)S(1)} %collective-permute-done.7.refs_2_), channel_id=1, source_target_pairs={{4,0},{8,4},{12,8},{14,12},{10,14},{6,10},{2,6},{0,2},{5,1},{9,5},... | collective-permute-start | bytes 798728 | tf_op jit(solution)/shard_map/ppermute | solution.py:498
  37.5 9.5 %collective-permute-start.13 = (bf16[1040,128]{1,0:T(8,128)(2,1)S(1)}, bf16[1040,128]{1,0:T(8,128)(2,1)S(1)}, u32[]{:S(2)}, u32[]{:S(2)}) collective-permute-start(bf16[1040,128]{1,0:T(8,128)(2,1)S(1)} %collective-permute-done.8.refs_0_), channel_id=1, source_target_pairs={{0,4},{4,8},{8,12},{12,14},{14,10},{10,6},{6,2},{2,0},{1,5},{5,9},... | collective-permute-start | bytes 798728 | tf_op jit(solution)/shard_map/ppermute | solution.py:498
  39.0 8.4 %collective-permute-start.14 = (bf16[1040,128]{1,0:T(8,128)(2,1)S(1)}, bf16[1040,128]{1,0:T(8,128)(2,1)S(1)}, u32[]{:S(2)}, u32[]{:S(2)}) collective-permute-start(bf16[1040,128]{1,0:T(8,128)(2,1)S(1)} %collective-permute-done.9.refs_3_), channel_id=1, source_target_pairs={{4,0},{8,4},{12,8},{14,12},{10,14},{6,10},{2,6},{0,2},{5,1},{9,5},... | collective-permute-start | bytes 798728 | tf_op jit(solution)/shard_map/ppermute | solution.py:498
  41.1 9.3 %collective-permute-start.15 = (bf16[2,256,1024]{2,1,0:T(8,128)(2,1)S(1)}, bf16[2,256,1024]{2,1,0:T(8,128)(2,1)S(1)}, u32[]{:S(2)}, u32[]{:S(2)}) collective-permute-start(bf16[2,256,1024]{2,1,0:T(8,128)(2,1)S(1)} %get-tuple-element.94.refs_1_), channel_id=1, source_target_pairs={{0,1},{1,0},{2,3},{3,2},{4,5},{5,4},{6,7},{7,6},{8,9},{9,8},{10,11... | collective-permute-start | bytes 3145736 | tf_op jit(solution)/shard_map/ppermute | solution.py:501
  43.2 7.2 %collective-permute-start.16 = (bf16[2,256,1024]{2,1,0:T(8,128)(2,1)S(1)}, bf16[2,256,1024]{2,1,0:T(8,128)(2,1)S(1)}, u32[]{:S(2)}, u32[]{:S(2)}) collective-permute-start(bf16[2,256,1024]{2,1,0:T(8,128)(2,1)S(1)} %get-tuple-element.107.refs_2_), channel_id=1, source_target_pairs={{0,1},{1,0},{2,3},{3,2},{4,5},{5,4},{6,7},{7,6},{8,9},{9,8},{10,11... | collective-permute-start | bytes 3145736 | tf_op jit(solution)/shard_map/ppermute | solution.py:501
  47.4 3.0 %collective-permute-start.17 = (bf16[2,256,1024]{2,1,0:T(8,128)(2,1)S(1)}, bf16[2,256,1024]{2,1,0:T(8,128)(2,1)S(1)}, u32[]{:S(2)}, u32[]{:S(2)}) collective-permute-start(bf16[2,256,1024]{2,1,0:T(8,128)(2,1)S(1)} %get-tuple-element.119.refs_3_), channel_id=1, source_target_pairs={{0,1},{1,0},{2,3},{3,2},{4,5},{5,4},{6,7},{7,6},{8,9},{9,8},{10,11... | collective-permute-start | bytes 3145736 | tf_op jit(solution)/shard_map/ppermute | solution.py:501
  49.1 2.0 %collective-permute-start.18 = (bf16[2,128,1024]{2,1,0:T(8,128)(2,1)S(1)}, bf16[2,128,1024]{2,1,0:T(8,128)(2,1)S(1)}, u32[]{:S(2)}, u32[]{:S(2)}) collective-permute-start(bf16[2,128,1024]{2,1,0:T(8,128)(2,1)S(1)} %get-tuple-element.124.refs_4_), channel_id=1, source_target_pairs={{0,1},{1,0},{2,3},{3,2},{4,5},{5,4},{6,7},{7,6},{8,9},{9,8},{10,11... | collective-permute-start | bytes 1572872 | tf_op jit(solution)/shard_map/ppermute | solution.py:501
  55.3 22.1 %collective-permute-start.19 = (bf16[40,2048]{1,0:T(8,128)(2,1)S(1)}, bf16[40,2048]{1,0:T(8,128)(2,1)S(1)}, u32[]{:S(2)}, u32[]{:S(2)}) collective-permute-start(bf16[40,2048]{1,0:T(8,128)(2,1)S(1)} %get-tuple-element.148), channel_id=1, source_target_pairs={{0,8},{2,10},{4,12},{6,14},{8,0},{10,2},{12,4},{14,6},{1,9},{3,11}... | collective-permute-start | bytes 491528 | tf_op jit(solution)/shard_map/ppermute | solution.py:541
  56.0 24.6 %collective-permute-start.20 = (bf16[40,2048]{1,0:T(8,128)(2,1)S(1)}, bf16[40,2048]{1,0:T(8,128)(2,1)S(1)}, u32[]{:S(2)}, u32[]{:S(2)}) collective-permute-start(bf16[40,2048]{1,0:T(8,128)(2,1)S(1)} %get-tuple-element.151), channel_id=1, source_target_pairs={{0,10},{2,8},{4,14},{6,12},{8,2},{10,0},{12,6},{14,4},{1,11},{3,9}... | collective-permute-start | bytes 491528 | tf_op jit(solution)/shard_map/ppermute | solution.py:541
  63.3 19.1 %copy-start.7 = (bf16[1040,128]{1,0:T(8,128)(2,1)S(1)}, bf16[1040,128]{1,0:T(8,128)(2,1)}, u32[]{:S(2)}) copy-start(bf16[1040,128]{1,0:T(8,128)(2,1)} %get-tuple-element.81.top_ref.refs_0_) | copy-start | bytes 798724
  63.3 19.1 %copy-start.9 = (bf16[1040,128]{1,0:T(8,128)(2,1)S(1)}, bf16[1040,128]{1,0:T(8,128)(2,1)}, u32[]{:S(2)}) copy-start(bf16[1040,128]{1,0:T(8,128)(2,1)} %get-tuple-element.82.bottom_ref.refs_1_) | copy-start | bytes 798724
  63.3 19.1 %copy-start.10 = (f32[2048,8]{0,1:T(8,128)S(1)}, f32[2048,8]{0,1:T(8,128)}, u32[]{:S(2)}) copy-start(f32[2048,8]{0,1:T(8,128)} %param.10) | copy-start | bytes 196612
  63.3 19.5 %collective-permute-start.21 = (bf16[40,2048]{1,0:T(8,128)(2,1)S(1)}, bf16[40,2048]{1,0:T(8,128)(2,1)S(1)}, u32[]{:S(2)}, u32[]{:S(2)}) collective-permute-start(bf16[40,2048]{1,0:T(8,128)(2,1)S(1)} %get-tuple-element.152), channel_id=1, source_target_pairs={{0,12},{2,14},{4,8},{6,10},{8,4},{10,6},{12,0},{14,2},{1,13},{3,15... | collective-permute-start | bytes 491528 | tf_op jit(solution)/shard_map/ppermute | solution.py:541
  63.4 19.4 %collective-permute-start.22 = (bf16[40,2048]{1,0:T(8,128)(2,1)S(1)}, bf16[40,2048]{1,0:T(8,128)(2,1)S(1)}, u32[]{:S(2)}, u32[]{:S(2)}) collective-permute-start(bf16[40,2048]{1,0:T(8,128)(2,1)S(1)} %get-tuple-element.153), channel_id=1, source_target_pairs={{0,14},{2,12},{4,10},{6,8},{8,6},{10,4},{12,2},{14,0},{1,15},{3,13... | collective-permute-start | bytes 491528 | tf_op jit(solution)/shard_map/ppermute | solution.py:541
  73.1 10.5 %collective-permute-start.23 = (bf16[40,2048]{1,0:T(8,128)(2,1)S(1)}, bf16[40,2048]{1,0:T(8,128)(2,1)S(1)}, u32[]{:S(2)}, u32[]{:S(2)}) collective-permute-start(bf16[40,2048]{1,0:T(8,128)(2,1)S(1)} %get-tuple-element.154), channel_id=1, source_target_pairs={{0,6},{2,4},{4,2},{6,0},{8,14},{10,12},{12,10},{14,8},{1,7},{3,5},... | collective-permute-start | bytes 491528 | tf_op jit(solution)/shard_map/ppermute | solution.py:541
  77.4 9.9 %collective-permute-start.24 = (bf16[40,2048]{1,0:T(8,128)(2,1)S(1)}, bf16[40,2048]{1,0:T(8,128)(2,1)S(1)}, u32[]{:S(2)}, u32[]{:S(2)}) collective-permute-start(bf16[40,2048]{1,0:T(8,128)(2,1)S(1)} %get-tuple-element.155), channel_id=1, source_target_pairs={{0,4},{2,6},{4,0},{6,2},{8,12},{10,14},{12,8},{14,10},{1,5},{3,7},... | collective-permute-start | bytes 491528 | tf_op jit(solution)/shard_map/ppermute | solution.py:541
  80.6 6.7 %collective-permute-start.25 = (bf16[40,2048]{1,0:T(8,128)(2,1)S(1)}, bf16[40,2048]{1,0:T(8,128)(2,1)S(1)}, u32[]{:S(2)}, u32[]{:S(2)}) collective-permute-start(bf16[40,2048]{1,0:T(8,128)(2,1)S(1)} %get-tuple-element.156), channel_id=1, source_target_pairs={{0,2},{2,0},{4,6},{6,4},{8,10},{10,8},{12,14},{14,12},{1,3},{3,1},... | collective-permute-start | bytes 491528 | tf_op jit(solution)/shard_map/ppermute | solution.py:541

commit v4 on v3

--- a/solution.py
+++ b/solution.py
@@ -16,6 +16,7 @@
 LANES = 128
 CODES = 16
 TERMS = 2
+PART = 256
 MIB = 1 << 20
 WHOLE = pl.BlockSpec(memory_space=pltpu.VMEM)
 
@@ -427,7 +428,7 @@
     ahead, pieces = refs[:ahead_count], refs[ahead_count:]
     tok_count, model_width = out_ref.shape
     copies = []
-    step = min(model_width, 512)
+    step = min(model_width, PART)
     spare = jnp.zeros((SLOTS - MOST, step), jnp.float32)
     for start in range(0, model_width, step):
         cols = pl.ds(start, step)
@@ -456,7 +457,7 @@
     model_width = pieces[0].shape[1]
     scratch = [
         pltpu.VMEM((tok_count, model_width), dtype),
-        pltpu.SemaphoreType.DMA((-(-model_width // 512),)),
+        pltpu.SemaphoreType.DMA((-(-model_width // PART),)),
     ]
     return pl.pallas_call(
         functools.partial(combine_kernel, len(ahead)),

time: 88.8 us -> 88.9 us (level)
  no operation moved by 1% of the time
where the time goes in v4:
time: 88.9 us; the launch traced here: 88.6 us
  Pallas kernels  32.9 us (37%)
  starting transfers between devices  25.4 us (29%)
  waiting for transfers between devices  23.5 us (26%)
  local copies, waits for them, and re-layouts  6.31 us (7%)
    pallas_call x3, Pallas kernels, attend(): pl.pallas_call(functools.partial(attend_kernel, lots, heads), in_specs=[W...  14.1 us
    ppermute x7, starting transfers between devices, send(): lax.ppermute(parts[0], 'ctx', forward)  13 us
    ppermute x7, waiting for transfers between devices, swap(): return lax.ppermute(piece, 'ctx', [(c, c ^ k) for c in range(ctx_count)])  11.4 us
    ppermute x7, waiting for transfers between devices, send(): lax.ppermute(parts[1], 'ctx', backward)  11 us
    ppermute x7, starting transfers between devices, swap(): return lax.ppermute(piece, 'ctx', [(c, c ^ k) for c in range(ctx_count)])  9.6 us
    unnamed x22, local copies, waits for them, and re-layouts  6.31 us
    pallas_call x5, Pallas kernels, project_values(): pl.pallas_call(functools.partial(values_kernel, half, offsets, len(blocks...  6.15 us
    pallas_call x5, Pallas kernels, project_keys(): pl.pallas_call(functools.partial(keys_kernel, half, len(blocks)), in_spec...  5.29 us
  transfers between devices with their start and end apart: 26, of which 15 were waited for; matrix products, arithmetic and copies ran while one was open for 0% of the time, Pallas kernels for 29%

profile of v4, /device:TPU:0, one launch (start us, length us, event | category | flops | bytes accessed | tf_op | source)
XLA Modules:
  0.0 88.6 jit_solution(16449614482112096584)
XLA Ops:
  0.0 2.0 %norm_rows.1 = (bf16[1040,128]{1,0:T(8,128)(2,1)}, bf16[1040,128]{1,0:T(8,128)(2,1)}) custom-call(bf16[128,2048]{1,0:T(8,128)(2,1)} %refs_0_.1, f32[1,2048]{1,0:T(1,128)} %bitcast.15, s32[2,128]{1,0:T(2,128)} %bitcast.16), custom_call_target="tpu_custom_call" | custom-call | tf_op jit(solution)/shard_map/norm_rows/pallas_call | solution.py:86
  2.0 3.1 %collective-permute-start = (bf16[1040,128]{1,0:T(8,128)(2,1)}, bf16[1040,128]{1,0:T(8,128)(2,1)S(1)}, u32[]{:S(2)}, u32[]{:S(2)}) collective-permute-start(bf16[1040,128]{1,0:T(8,128)(2,1)} %get-tuple-element.81.top_ref.refs_0_), channel_id=1, source_target_pairs={{0,4},{4,8},{8,12},{12,14},{14,10},{10,6},{6,2},{2,0},{1,5},{5,9},... | collective-permute-start | bytes 798728 | tf_op jit(solution)/shard_map/ppermute | solution.py:499
  5.1 0.0 collective-permute-start.1
  5.1 2.0 %collective-permute-start.2 = (bf16[1040,128]{1,0:T(8,128)(2,1)}, bf16[1040,128]{1,0:T(8,128)(2,1)S(1)}, u32[]{:S(2)}, u32[]{:S(2)}) collective-permute-start(bf16[1040,128]{1,0:T(8,128)(2,1)} %get-tuple-element.82.bottom_ref.refs_1_), channel_id=1, source_target_pairs={{0,4},{4,8},{8,12},{12,14},{14,10},{10,6},{6,2},{2,0},{1,5},{5,9},... | collective-permute-start | bytes 798728 | tf_op jit(solution)/shard_map/ppermute | solution.py:499
  7.1 0.0 collective-permute-start.3
  7.2 2.2 %copy-done.1 = bf16[2048,1024]{1,0:T(8,128)(2,1)S(1)} copy-done((bf16[2048,1024]{1,0:T(8,128)(2,1)S(1)}, bf16[2048,1024]{1,0:T(8,128)(2,1)}, u32[]{:S(2)}) %copy-start.1) | copy-done | bytes 4194328
  9.3 0.9 %copy-done.6 = bf16[1040,128]{1,0:T(8,128)(2,1)S(1)} copy-done((bf16[1040,128]{1,0:T(8,128)(2,1)S(1)}, bf16[1040,128]{1,0:T(8,128)(2,1)}, u32[]{:S(2)}) %copy-start.6) | copy-done | bytes 266264
  10.3 0.9 %copy-done.8 = bf16[1040,128]{1,0:T(8,128)(2,1)S(1)} copy-done((bf16[1040,128]{1,0:T(8,128)(2,1)S(1)}, bf16[1040,128]{1,0:T(8,128)(2,1)}, u32[]{:S(2)}) %copy-start.8) | copy-done | bytes 266264
  11.2 0.7 project_keys.5
  12.0 0.5 collective-permute-done.refs_0_
  12.5 2.2 %collective-permute-done.1.refs_3_ = bf16[1040,128]{1,0:T(8,128)(2,1)S(1)} collective-permute-done((bf16[1040,128]{1,0:T(8,128)(2,1)}, bf16[1040,128]{1,0:T(8,128)(2,1)S(1)}, u32[]{:S(2)}, u32[]{:S(2)}) %collective-permute-start.1) | collective-permute-done | bytes 266272 | tf_op jit(solution)/shard_map/ppermute | solution.py:499
  14.6 1.6 %collective-permute-start.4 = (bf16[1040,128]{1,0:T(8,128)(2,1)S(1)}, bf16[1040,128]{1,0:T(8,128)(2,1)S(1)}, u32[]{:S(2)}, u32[]{:S(2)}) collective-permute-start(bf16[1040,128]{1,0:T(8,128)(2,1)S(1)} %collective-permute-done.refs_0_), channel_id=1, source_target_pairs={{0,4},{4,8},{8,12},{12,14},{14,10},{10,6},{6,2},{2,0},{1,5},{5,9},... | collective-permute-start | bytes 798728 | tf_op jit(solution)/shard_map/ppermute | solution.py:499
  16.2 0.4 collective-permute-start.5
  16.7 2.2 %copy-done.3 = bf16[2048,1024]{1,0:T(8,128)(2,1)S(1)} copy-done((bf16[2048,1024]{1,0:T(8,128)(2,1)S(1)}, bf16[2048,1024]{1,0:T(8,128)(2,1)}, u32[]{:S(2)}) %copy-start.3) | copy-done | bytes 4194328
  18.9 0.8 project_values.5
  19.7 0.6 collective-permute-done.3.refs_2_
  20.3 1.6 %collective-permute-start.6 = (bf16[1040,128]{1,0:T(8,128)(2,1)S(1)}, bf16[1040,128]{1,0:T(8,128)(2,1)S(1)}, u32[]{:S(2)}, u32[]{:S(2)}) collective-permute-start(bf16[1040,128]{1,0:T(8,128)(2,1)S(1)} %collective-permute-done.2.refs_1_), channel_id=1, source_target_pairs={{0,4},{4,8},{8,12},{12,14},{14,10},{10,6},{6,2},{2,0},{1,5},{5,9},... | collective-permute-start | bytes 798728 | tf_op jit(solution)/shard_map/ppermute | solution.py:499
  21.9 0.4 collective-permute-start.7
  22.4 1.3 %project_keys.6 = (bf16[256,1024]{1,0:T(8,128)(2,1)S(1)}, f32[8,128]{1,0:T(8,128)S(1)}) custom-call(bf16[1040,128]{1,0:T(8,128)(2,1)S(1)} %collective-permute-done.refs_0_, bf16[1040,128]{1,0:T(8,128)(2,1)S(1)} %collective-permute-done.2.refs_1_, bf16[1040,128]{1,0:T(8,128)(2,1)S(1)} %collective-permute-done.3.refs_2_, ...), custom_call_target="tpu_custom_call" | custom-call | tf_op jit(solution)/shard_map/project_keys/pallas_call | solution.py:116
  23.7 0.3 collective-permute-done.4.refs_0_
  24.0 2.1 %collective-permute-done.5.refs_3_ = bf16[1040,128]{1,0:T(8,128)(2,1)S(1)} collective-permute-done((bf16[1040,128]{1,0:T(8,128)(2,1)S(1)}, bf16[1040,128]{1,0:T(8,128)(2,1)S(1)}, u32[]{:S(2)}, u32[]{:S(2)}) %collective-permute-start.5) | collective-permute-done | bytes 266272 | tf_op jit(solution)/shard_map/ppermute | solution.py:499
  26.1 1.6 %collective-permute-start.8 = (bf16[1040,128]{1,0:T(8,128)(2,1)S(1)}, bf16[1040,128]{1,0:T(8,128)(2,1)S(1)}, u32[]{:S(2)}, u32[]{:S(2)}) collective-permute-start(bf16[1040,128]{1,0:T(8,128)(2,1)S(1)} %collective-permute-done.4.refs_0_), channel_id=1, source_target_pairs={{0,4},{4,8},{8,12},{12,14},{14,10},{10,6},{6,2},{2,0},{1,5},{5,9},... | collective-permute-start | bytes 798728 | tf_op jit(solution)/shard_map/ppermute | solution.py:499
  27.6 0.4 collective-permute-start.9
  28.1 1.5 %project_values.6 = (bf16[2,256,1024]{2,1,0:T(8,128)(2,1)S(1)}, bf16[2,48,2048]{2,1,0:T(8,128)(2,1)S(1)}, f32[2,48,128]{2,1,0:T(8,128)S(1)}) custom-call(f32[8,128]{1,0:T(8,128)S(1)} %get-tuple-element.92.mark_ref, bf16[256,1024]{1,0:T(8,128)(2,1)S(1)} %get-tuple-element.93.keys_ref, bf16[1040,128]{1,0:T(8,128)(2,1)S(1)} %collective-permute-done.refs_0_, ...), custom_call_target="tpu_custom_call" | custom-call | tf_op jit(solution)/shard_map/project_values/pallas_call | solution.py:161
  29.6 0.1 collective-permute-done.6.refs_1_
  29.7 2.1 %collective-permute-done.7.refs_2_ = bf16[1040,128]{1,0:T(8,128)(2,1)S(1)} collective-permute-done((bf16[1040,128]{1,0:T(8,128)(2,1)S(1)}, bf16[1040,128]{1,0:T(8,128)(2,1)S(1)}, u32[]{:S(2)}, u32[]{:S(2)}) %collective-permute-start.7) | collective-permute-done | bytes 266272 | tf_op jit(solution)/shard_map/ppermute | solution.py:499
  31.8 1.6 %collective-permute-start.10 = (bf16[1040,128]{1,0:T(8,128)(2,1)S(1)}, bf16[1040,128]{1,0:T(8,128)(2,1)S(1)}, u32[]{:S(2)}, u32[]{:S(2)}) collective-permute-start(bf16[1040,128]{1,0:T(8,128)(2,1)S(1)} %collective-permute-done.6.refs_1_), channel_id=1, source_target_pairs={{0,4},{4,8},{8,12},{12,14},{14,10},{10,6},{6,2},{2,0},{1,5},{5,9},... | collective-permute-start | bytes 798728 | tf_op jit(solution)/shard_map/ppermute | solution.py:499
  33.3 0.4 collective-permute-start.11
  33.8 0.8 project_queries.3
  34.6 1.3 %project_keys.7 = (bf16[256,1024]{1,0:T(8,128)(2,1)S(1)}, f32[8,128]{1,0:T(8,128)S(1)}) custom-call(bf16[1040,128]{1,0:T(8,128)(2,1)S(1)} %collective-permute-done.4.refs_0_, bf16[1040,128]{1,0:T(8,128)(2,1)S(1)} %collective-permute-done.6.refs_1_, bf16[1040,128]{1,0:T(8,128)(2,1)S(1)} %collective-permute-done.7.refs_2_, ...), custom_call_target="tpu_custom_call" | custom-call | tf_op jit(solution)/shard_map/project_keys/pallas_call | solution.py:116
  35.9 1.6 %collective-permute-done.9.refs_3_ = bf16[1040,128]{1,0:T(8,128)(2,1)S(1)} collective-permute-done((bf16[1040,128]{1,0:T(8,128)(2,1)S(1)}, bf16[1040,128]{1,0:T(8,128)(2,1)S(1)}, u32[]{:S(2)}, u32[]{:S(2)}) %collective-permute-start.9) | collective-permute-done | bytes 266272 | tf_op jit(solution)/shard_map/ppermute | solution.py:499
  37.5 1.6 %collective-permute-start.13 = (bf16[1040,128]{1,0:T(8,128)(2,1)S(1)}, bf16[1040,128]{1,0:T(8,128)(2,1)S(1)}, u32[]{:S(2)}, u32[]{:S(2)}) collective-permute-start(bf16[1040,128]{1,0:T(8,128)(2,1)S(1)} %collective-permute-done.8.refs_0_), channel_id=1, source_target_pairs={{0,4},{4,8},{8,12},{12,14},{14,10},{10,6},{6,2},{2,0},{1,5},{5,9},... | collective-permute-start | bytes 798728 | tf_op jit(solution)/shard_map/ppermute | solution.py:499
  39.0 0.4 collective-permute-start.14
  39.5 1.5 %project_values.7 = (bf16[2,256,1024]{2,1,0:T(8,128)(2,1)S(1)}, bf16[2,48,2048]{2,1,0:T(8,128)(2,1)S(1)}, f32[2,48,128]{2,1,0:T(8,128)S(1)}) custom-call(f32[8,128]{1,0:T(8,128)S(1)} %get-tuple-element.105.mark_ref, bf16[256,1024]{1,0:T(8,128)(2,1)S(1)} %get-tuple-element.106.keys_ref, bf16[1040,128]{1,0:T(8,128)(2,1)S(1)} %collective-permute-done.4.refs_0_, ...), custom_call_target="tpu_custom_call" | custom-call | tf_op jit(solution)/shard_map/project_values/pallas_call | solution.py:161
  41.0 0.1 collective-permute-done.10.refs_1_
  41.1 2.1 %collective-permute-done.11.refs_2_ = bf16[1040,128]{1,0:T(8,128)(2,1)S(1)} collective-permute-done((bf16[1040,128]{1,0:T(8,128)(2,1)S(1)}, bf16[1040,128]{1,0:T(8,128)(2,1)S(1)}, u32[]{:S(2)}, u32[]{:S(2)}) %collective-permute-start.11) | collective-permute-done | bytes 266272 | tf_op jit(solution)/shard_map/ppermute | solution.py:499
  43.2 1.3 %project_keys.8 = (bf16[256,1024]{1,0:T(8,128)(2,1)S(1)}, f32[8,128]{1,0:T(8,128)S(1)}) custom-call(bf16[1040,128]{1,0:T(8,128)(2,1)S(1)} %collective-permute-done.8.refs_0_, bf16[1040,128]{1,0:T(8,128)(2,1)S(1)} %collective-permute-done.10.refs_1_, bf16[1040,128]{1,0:T(8,128)(2,1)S(1)} %collective-permute-done.11.refs_2_, ...), custom_call_target="tpu_custom_call" | custom-call | tf_op jit(solution)/shard_map/project_keys/pallas_call | solution.py:116
  44.5 1.5 %project_values.8 = (bf16[2,256,1024]{2,1,0:T(8,128)(2,1)S(1)}, bf16[2,48,2048]{2,1,0:T(8,128)(2,1)S(1)}, f32[2,48,128]{2,1,0:T(8,128)S(1)}) custom-call(f32[8,128]{1,0:T(8,128)S(1)} %get-tuple-element.111.mark_ref, bf16[256,1024]{1,0:T(8,128)(2,1)S(1)} %get-tuple-element.112.keys_ref, bf16[1040,128]{1,0:T(8,128)(2,1)S(1)} %collective-permute-done.8.refs_0_, ...), custom_call_target="tpu_custom_call" | custom-call | tf_op jit(solution)/shard_map/project_values/pallas_call | solution.py:161
  46.0 1.0 %project_queries.4 = (bf16[2,48,1024]{2,1,0:T(8,128)(2,1)S(1)}, bf16[2,48,1024]{2,1,0:T(8,128)(2,1)S(1)}) custom-call(bf16[2,48,2048]{2,1,0:T(8,128)(2,1)S(1)} %get-tuple-element.114.refs_0_, bf16[2,48,2048]{2,1,0:T(8,128)(2,1)S(1)} %get-tuple-element.115.refs_1_, bf16[2048,1024]{1,0:T(8,128)(2,1)S(1)} %bitcast.12, bf16[1024,2048]{1,0:T(8,128)(2,1)S(1)} %bitcast.6), custom_call_target="tpu_custom_call" | custom-call | tf_op jit(solution)/shard_map/project_queries/pallas_call | solution.py:190
  47.0 0.4 collective-permute-done.14.refs_1_
  47.4 0.1 collective-permute-start.17
  47.6 0.7 project_keys.9
  48.3 0.8 project_values.9
  49.1 0.4 collective-permute-start.18
  49.5 0.8 project_queries.5.refs_9_
  50.4 0.7 arrange.1
  51.1 0.0 collective-permute-done.18.other_ref
  51.1 0.1 arrange_last.1.panel_ref
  51.2 4.1 %attend.3 = (bf16[40,2048]{1,0:T(8,128)(2,1)S(1)}, bf16[40,2048]{1,0:T(8,128)(2,1)S(1)}) custom-call(bf16[2,16,128,1024]{3,2,1,0:T(8,128)(2,1)S(1)} %arrange_last.1.panel_ref, f32[8,40,1024]{2,1,0:T(8,128)S(1)} %get-tuple-element.137.queries_ref, f32[8,40,128]{2,1,0:T(8,128)S(1)} %get-tuple-element.144.places_ref, bf16[1024,2048]{1,0:T(8,128)(2,1)S(1)} %bitcast.8), custom_call_target="tpu_custom_call" | custom-call | flops 603979776 | bytes 8388608 | tf_op jit(solution)/shard_map/attend/pallas_call | solution.py:346
  55.3 0.7 collective-permute-start.19
  56.0 2.0 %collective-permute-start.20 = (bf16[40,2048]{1,0:T(8,128)(2,1)S(1)}, bf16[40,2048]{1,0:T(8,128)(2,1)S(1)}, u32[]{:S(2)}, u32[]{:S(2)}) collective-permute-start(bf16[40,2048]{1,0:T(8,128)(2,1)S(1)} %get-tuple-element.151), channel_id=1, source_target_pairs={{0,10},{2,8},{4,14},{6,12},{8,2},{10,0},{12,6},{14,4},{1,11},{3,9}... | collective-permute-start | bytes 491528 | tf_op jit(solution)/shard_map/ppermute | solution.py:542
  58.0 5.3 %attend.4 = (bf16[40,2048]{1,0:T(8,128)(2,1)S(1)}, bf16[40,2048]{1,0:T(8,128)(2,1)S(1)}) custom-call(bf16[2,16,128,1024]{3,2,1,0:T(8,128)(2,1)S(1)} %arrange_last.1.panel_ref, f32[8,40,1024]{2,1,0:T(8,128)S(1)} %get-tuple-element.137.queries_ref, f32[8,40,128]{2,1,0:T(8,128)S(1)} %get-tuple-element.144.places_ref, bf16[1024,2048]{1,0:T(8,128)(2,1)S(1)} %bitcast.9), custom_call_target="tpu_custom_call" | custom-call | flops 603979776 | bytes 8388608 | tf_op jit(solution)/shard_map/attend/pallas_call | solution.py:346
  63.3 0.1 collective-permute-start.21
  63.4 5.0 %collective-permute-start.22 = (bf16[40,2048]{1,0:T(8,128)(2,1)S(1)}, bf16[40,2048]{1,0:T(8,128)(2,1)S(1)}, u32[]{:S(2)}, u32[]{:S(2)}) collective-permute-start(bf16[40,2048]{1,0:T(8,128)(2,1)S(1)} %get-tuple-element.153), channel_id=1, source_target_pairs={{0,14},{2,12},{4,10},{6,8},{8,6},{10,4},{12,2},{14,0},{1,15},{3,13... | collective-permute-start | bytes 491528 | tf_op jit(solution)/shard_map/ppermute | solution.py:542
  68.4 4.7 %attend.5 = (bf16[40,2048]{1,0:T(8,128)(2,1)S(1)}, bf16[40,2048]{1,0:T(8,128)(2,1)S(1)}, bf16[40,2048]{1,0:T(8,128)(2,1)S(1)}, bf16[40,2048]{1,0:T(8,128)(2,1)S(1)}) custom-call(bf16[2,16,128,1024]{3,2,1,0:T(8,128)(2,1)S(1)} %arrange_last.1.panel_ref, f32[8,40,1024]{2,1,0:T(8,128)S(1)} %get-tuple-element.137.queries_ref, ...), custom_call_target="tpu_custom_call" | custom-call | flops 1207959552 | bytes 8388608 | tf_op jit(solution)/shard_map/attend/pallas_call | solution.py:346
  73.1 0.1 collective-permute-start.23
  73.2 4.2 %collective-permute-done.19.refs_1_ = bf16[40,2048]{1,0:T(8,128)(2,1)S(1)} collective-permute-done((bf16[40,2048]{1,0:T(8,128)(2,1)S(1)}, bf16[40,2048]{1,0:T(8,128)(2,1)S(1)}, u32[]{:S(2)}, u32[]{:S(2)}) %collective-permute-start.19) | collective-permute-done | bytes 163872 | tf_op jit(solution)/shard_map/ppermute | solution.py:542
  77.4 3.2 %collective-permute-done.20.refs_2_ = bf16[40,2048]{1,0:T(8,128)(2,1)S(1)} collective-permute-done((bf16[40,2048]{1,0:T(8,128)(2,1)S(1)}, bf16[40,2048]{1,0:T(8,128)(2,1)S(1)}, u32[]{:S(2)}, u32[]{:S(2)}) %collective-permute-start.20) | collective-permute-done | bytes 163872 | tf_op jit(solution)/shard_map/ppermute | solution.py:542
  80.6 1.7 %collective-permute-start.25 = (bf16[40,2048]{1,0:T(8,128)(2,1)S(1)}, bf16[40,2048]{1,0:T(8,128)(2,1)S(1)}, u32[]{:S(2)}, u32[]{:S(2)}) collective-permute-start(bf16[40,2048]{1,0:T(8,128)(2,1)S(1)} %get-tuple-element.156), channel_id=1, source_target_pairs={{0,2},{2,0},{4,6},{6,4},{8,10},{10,8},{12,14},{14,12},{1,3},{3,1},... | collective-permute-start | bytes 491528 | tf_op jit(solution)/shard_map/ppermute | solution.py:542
  82.3 0.5 gate_mix.1
  82.8 0.4 combine.2.refs_0_
  83.3 0.3 collective-permute-done.23.refs_1_
  83.6 3.7 %collective-permute-done.24.refs_2_ = bf16[40,2048]{1,0:T(8,128)(2,1)S(1)} collective-permute-done((bf16[40,2048]{1,0:T(8,128)(2,1)S(1)}, bf16[40,2048]{1,0:T(8,128)(2,1)S(1)}, u32[]{:S(2)}, u32[]{:S(2)}) %collective-permute-start.24) | collective-permute-done | bytes 163872 | tf_op jit(solution)/shard_map/ppermute | solution.py:542
  87.3 1.2 %combine.3 = bf16[128,2048]{1,0:T(8,128)(2,1)} custom-call(bf16[256,144]{1,0:T(8,128)(2,1)S(1)} %get-tuple-element.83.mix_ref, f32[128,2048]{1,0:T(8,128)S(1)} %combine.2.refs_0_, bf16[40,2048]{1,0:T(8,128)(2,1)S(1)} %collective-permute-done.23.refs_1_, bf16[40,2048]{1,0:T(8,128)(2,1)S(1)} %collective-permute-done.24.refs_2_, ...), custom_call_target="tpu_custom_call" | custom-call | tf_op jit(solution)/shard_map/combine/pallas_call | solution.py:462
  (32 shorter events, 0.1 us)
Async XLA Ops:
  2.0 10.5 %collective-permute-start = (bf16[1040,128]{1,0:T(8,128)(2,1)}, bf16[1040,128]{1,0:T(8,128)(2,1)S(1)}, u32[]{:S(2)}, u32[]{:S(2)}) collective-permute-start(bf16[1040,128]{1,0:T(8,128)(2,1)} %get-tuple-element.81.top_ref.refs_0_), channel_id=1, source_target_pairs={{0,4},{4,8},{8,12},{12,14},{14,10},{10,6},{6,2},{2,0},{1,5},{5,9},... | collective-permute-start | bytes 798728 | tf_op jit(solution)/shard_map/ppermute | solution.py:499
  5.1 9.5 %collective-permute-start.1 = (bf16[1040,128]{1,0:T(8,128)(2,1)}, bf16[1040,128]{1,0:T(8,128)(2,1)S(1)}, u32[]{:S(2)}, u32[]{:S(2)}) collective-permute-start(bf16[1040,128]{1,0:T(8,128)(2,1)} %get-tuple-element.82.bottom_ref.refs_1_), channel_id=1, source_target_pairs={{4,0},{8,4},{12,8},{14,12},{10,14},{6,10},{2,6},{0,2},{5,1},{9,5},... | collective-permute-start | bytes 798728 | tf_op jit(solution)/shard_map/ppermute | solution.py:499
  5.1 14.6 %collective-permute-start.2 = (bf16[1040,128]{1,0:T(8,128)(2,1)}, bf16[1040,128]{1,0:T(8,128)(2,1)S(1)}, u32[]{:S(2)}, u32[]{:S(2)}) collective-permute-start(bf16[1040,128]{1,0:T(8,128)(2,1)} %get-tuple-element.82.bottom_ref.refs_1_), channel_id=1, source_target_pairs={{0,4},{4,8},{8,12},{12,14},{14,10},{10,6},{6,2},{2,0},{1,5},{5,9},... | collective-permute-start | bytes 798728 | tf_op jit(solution)/shard_map/ppermute | solution.py:499
  7.1 13.2 %collective-permute-start.3 = (bf16[1040,128]{1,0:T(8,128)(2,1)}, bf16[1040,128]{1,0:T(8,128)(2,1)S(1)}, u32[]{:S(2)}, u32[]{:S(2)}) collective-permute-start(bf16[1040,128]{1,0:T(8,128)(2,1)} %get-tuple-element.81.top_ref.refs_0_), channel_id=1, source_target_pairs={{4,0},{8,4},{12,8},{14,12},{10,14},{6,10},{2,6},{0,2},{5,1},{9,5},... | collective-permute-start | bytes 798728 | tf_op jit(solution)/shard_map/ppermute | solution.py:499
  7.1 2.2 %copy-start.1 = (bf16[2048,1024]{1,0:T(8,128)(2,1)S(1)}, bf16[2048,1024]{1,0:T(8,128)(2,1)}, u32[]{:S(2)}) copy-start(bf16[2048,1024]{1,0:T(8,128)(2,1)} %refs_2_.6) | copy-start | bytes 12582916
  9.3 1.0 %copy-start.6 = (bf16[1040,128]{1,0:T(8,128)(2,1)S(1)}, bf16[1040,128]{1,0:T(8,128)(2,1)}, u32[]{:S(2)}) copy-start(bf16[1040,128]{1,0:T(8,128)(2,1)} %get-tuple-element.81.top_ref.refs_0_) | copy-start | bytes 798724
  10.3 1.0 %copy-start.8 = (bf16[1040,128]{1,0:T(8,128)(2,1)S(1)}, bf16[1040,128]{1,0:T(8,128)(2,1)}, u32[]{:S(2)}) copy-start(bf16[1040,128]{1,0:T(8,128)(2,1)} %get-tuple-element.82.bottom_ref.refs_1_) | copy-start | bytes 798724
  11.2 11.1 %copy-start.2 = (bf16[2048,1024]{1,0:T(8,128)(2,1)S(1)}, bf16[2048,1024]{1,0:T(8,128)(2,1)}, u32[]{:S(2)}) copy-start(bf16[2048,1024]{1,0:T(8,128)(2,1)} %refs_2_.6) | copy-start | bytes 12582916
  14.6 9.3 %collective-permute-start.4 = (bf16[1040,128]{1,0:T(8,128)(2,1)S(1)}, bf16[1040,128]{1,0:T(8,128)(2,1)S(1)}, u32[]{:S(2)}, u32[]{:S(2)}) collective-permute-start(bf16[1040,128]{1,0:T(8,128)(2,1)S(1)} %collective-permute-done.refs_0_), channel_id=1, source_target_pairs={{0,4},{4,8},{8,12},{12,14},{14,10},{10,6},{6,2},{2,0},{1,5},{5,9},... | collective-permute-start | bytes 798728 | tf_op jit(solution)/shard_map/ppermute | solution.py:499
  16.2 9.8 %collective-permute-start.5 = (bf16[1040,128]{1,0:T(8,128)(2,1)S(1)}, bf16[1040,128]{1,0:T(8,128)(2,1)S(1)}, u32[]{:S(2)}, u32[]{:S(2)}) collective-permute-start(bf16[1040,128]{1,0:T(8,128)(2,1)S(1)} %collective-permute-done.1.refs_3_), channel_id=1, source_target_pairs={{4,0},{8,4},{12,8},{14,12},{10,14},{6,10},{2,6},{0,2},{5,1},{9,5},... | collective-permute-start | bytes 798728 | tf_op jit(solution)/shard_map/ppermute | solution.py:499
  16.7 2.2 %copy-start.3 = (bf16[2048,1024]{1,0:T(8,128)(2,1)S(1)}, bf16[2048,1024]{1,0:T(8,128)(2,1)}, u32[]{:S(2)}) copy-start(bf16[2048,1024]{1,0:T(8,128)(2,1)} %refs_2_.7) | copy-start | bytes 12582916
  18.9 9.2 %copy-start.4 = (bf16[2048,1024]{1,0:T(8,128)(2,1)S(1)}, bf16[2048,1024]{1,0:T(8,128)(2,1)}, u32[]{:S(2)}) copy-start(bf16[2048,1024]{1,0:T(8,128)(2,1)} %refs_2_.7) | copy-start | bytes 12582916
  20.3 9.3 %collective-permute-start.6 = (bf16[1040,128]{1,0:T(8,128)(2,1)S(1)}, bf16[1040,128]{1,0:T(8,128)(2,1)S(1)}, u32[]{:S(2)}, u32[]{:S(2)}) collective-permute-start(bf16[1040,128]{1,0:T(8,128)(2,1)S(1)} %collective-permute-done.2.refs_1_), channel_id=1, source_target_pairs={{0,4},{4,8},{8,12},{12,14},{14,10},{10,6},{6,2},{2,0},{1,5},{5,9},... | collective-permute-start | bytes 798728 | tf_op jit(solution)/shard_map/ppermute | solution.py:499
  21.9 9.8 %collective-permute-start.7 = (bf16[1040,128]{1,0:T(8,128)(2,1)S(1)}, bf16[1040,128]{1,0:T(8,128)(2,1)S(1)}, u32[]{:S(2)}, u32[]{:S(2)}) collective-permute-start(bf16[1040,128]{1,0:T(8,128)(2,1)S(1)} %collective-permute-done.3.refs_2_), channel_id=1, source_target_pairs={{4,0},{8,4},{12,8},{14,12},{10,14},{6,10},{2,6},{0,2},{5,1},{9,5},... | collective-permute-start | bytes 798728 | tf_op jit(solution)/shard_map/ppermute | solution.py:499
  22.4 11.4 %copy-start.5 = (bf16[1,2048,1024]{2,1,0:T(8,128)(2,1)S(1)}, bf16[1,2048,1024]{2,1,0:T(8,128)(2,1)}, u32[]{:S(2)}) copy-start(bf16[1,2048,1024]{2,1,0:T(8,128)(2,1)} %param.14) | copy-start | bytes 12582916
  23.7 10.1 %copy-start = (bf16[1,1024,2048]{2,1,0:T(8,128)(2,1)S(1)}, bf16[1,1024,2048]{2,1,0:T(8,128)(2,1)}, u32[]{:S(2)}) copy-start(bf16[1,1024,2048]{2,1,0:T(8,128)(2,1)} %param.15) | copy-start | bytes 12582916
  26.1 9.8 %collective-permute-start.8 = (bf16[1040,128]{1,0:T(8,128)(2,1)S(1)}, bf16[1040,128]{1,0:T(8,128)(2,1)S(1)}, u32[]{:S(2)}, u32[]{:S(2)}) collective-permute-start(bf16[1040,128]{1,0:T(8,128)(2,1)S(1)} %collective-permute-done.4.refs_0_), channel_id=1, source_target_pairs={{0,4},{4,8},{8,12},{12,14},{14,10},{10,6},{6,2},{2,0},{1,5},{5,9},... | collective-permute-start | bytes 798728 | tf_op jit(solution)/shard_map/ppermute | solution.py:499
  27.6 9.8 %collective-permute-start.9 = (bf16[1040,128]{1,0:T(8,128)(2,1)S(1)}, bf16[1040,128]{1,0:T(8,128)(2,1)S(1)}, u32[]{:S(2)}, u32[]{:S(2)}) collective-permute-start(bf16[1040,128]{1,0:T(8,128)(2,1)S(1)} %collective-permute-done.5.refs_3_), channel_id=1, source_target_pairs={{4,0},{8,4},{12,8},{14,12},{10,14},{6,10},{2,6},{0,2},{5,1},{9,5},... | collective-permute-start | bytes 798728 | tf_op jit(solution)/shard_map/ppermute | solution.py:499
  28.1 18.9 %collective-permute-start.12 = (bf16[2,128,1024]{2,1,0:T(8,128)(2,1)S(1)}, bf16[2,128,1024]{2,1,0:T(8,128)(2,1)S(1)}, u32[]{:S(2)}, u32[]{:S(2)}) collective-permute-start(bf16[2,128,1024]{2,1,0:T(8,128)(2,1)S(1)} %get-tuple-element.88.refs_0_), channel_id=1, source_target_pairs={{0,1},{1,0},{2,3},{3,2},{4,5},{5,4},{6,7},{7,6},{8,9},{9,8},{10,11... | collective-permute-start | bytes 1572872 | tf_op jit(solution)/shard_map/ppermute | solution.py:502
  31.8 9.3 %collective-permute-start.10 = (bf16[1040,128]{1,0:T(8,128)(2,1)S(1)}, bf16[1040,128]{1,0:T(8,128)(2,1)S(1)}, u32[]{:S(2)}, u32[]{:S(2)}) collective-permute-start(bf16[1040,128]{1,0:T(8,128)(2,1)S(1)} %collective-permute-done.6.refs_1_), channel_id=1, source_target_pairs={{0,4},{4,8},{8,12},{12,14},{14,10},{10,6},{6,2},{2,0},{1,5},{5,9},... | collective-permute-start | bytes 798728 | tf_op jit(solution)/shard_map/ppermute | solution.py:499
  33.3 9.8 %collective-permute-start.11 = (bf16[1040,128]{1,0:T(8,128)(2,1)S(1)}, bf16[1040,128]{1,0:T(8,128)(2,1)S(1)}, u32[]{:S(2)}, u32[]{:S(2)}) collective-permute-start(bf16[1040,128]{1,0:T(8,128)(2,1)S(1)} %collective-permute-done.7.refs_2_), channel_id=1, source_target_pairs={{4,0},{8,4},{12,8},{14,12},{10,14},{6,10},{2,6},{0,2},{5,1},{9,5},... | collective-permute-start | bytes 798728 | tf_op jit(solution)/shard_map/ppermute | solution.py:499
  37.5 9.5 %collective-permute-start.13 = (bf16[1040,128]{1,0:T(8,128)(2,1)S(1)}, bf16[1040,128]{1,0:T(8,128)(2,1)S(1)}, u32[]{:S(2)}, u32[]{:S(2)}) collective-permute-start(bf16[1040,128]{1,0:T(8,128)(2,1)S(1)} %collective-permute-done.8.refs_0_), channel_id=1, source_target_pairs={{0,4},{4,8},{8,12},{12,14},{14,10},{10,6},{6,2},{2,0},{1,5},{5,9},... | collective-permute-start | bytes 798728 | tf_op jit(solution)/shard_map/ppermute | solution.py:499
  39.0 8.4 %collective-permute-start.14 = (bf16[1040,128]{1,0:T(8,128)(2,1)S(1)}, bf16[1040,128]{1,0:T(8,128)(2,1)S(1)}, u32[]{:S(2)}, u32[]{:S(2)}) collective-permute-start(bf16[1040,128]{1,0:T(8,128)(2,1)S(1)} %collective-permute-done.9.refs_3_), channel_id=1, source_target_pairs={{4,0},{8,4},{12,8},{14,12},{10,14},{6,10},{2,6},{0,2},{5,1},{9,5},... | collective-permute-start | bytes 798728 | tf_op jit(solution)/shard_map/ppermute | solution.py:499
  41.1 9.3 %collective-permute-start.15 = (bf16[2,256,1024]{2,1,0:T(8,128)(2,1)S(1)}, bf16[2,256,1024]{2,1,0:T(8,128)(2,1)S(1)}, u32[]{:S(2)}, u32[]{:S(2)}) collective-permute-start(bf16[2,256,1024]{2,1,0:T(8,128)(2,1)S(1)} %get-tuple-element.94.refs_1_), channel_id=1, source_target_pairs={{0,1},{1,0},{2,3},{3,2},{4,5},{5,4},{6,7},{7,6},{8,9},{9,8},{10,11... | collective-permute-start | bytes 3145736 | tf_op jit(solution)/shard_map/ppermute | solution.py:502
  43.2 7.2 %collective-permute-start.16 = (bf16[2,256,1024]{2,1,0:T(8,128)(2,1)S(1)}, bf16[2,256,1024]{2,1,0:T(8,128)(2,1)S(1)}, u32[]{:S(2)}, u32[]{:S(2)}) collective-permute-start(bf16[2,256,1024]{2,1,0:T(8,128)(2,1)S(1)} %get-tuple-element.107.refs_2_), channel_id=1, source_target_pairs={{0,1},{1,0},{2,3},{3,2},{4,5},{5,4},{6,7},{7,6},{8,9},{9,8},{10,11... | collective-permute-start | bytes 3145736 | tf_op jit(solution)/shard_map/ppermute | solution.py:502
  47.4 3.0 %collective-permute-start.17 = (bf16[2,256,1024]{2,1,0:T(8,128)(2,1)S(1)}, bf16[2,256,1024]{2,1,0:T(8,128)(2,1)S(1)}, u32[]{:S(2)}, u32[]{:S(2)}) collective-permute-start(bf16[2,256,1024]{2,1,0:T(8,128)(2,1)S(1)} %get-tuple-element.119.refs_3_), channel_id=1, source_target_pairs={{0,1},{1,0},{2,3},{3,2},{4,5},{5,4},{6,7},{7,6},{8,9},{9,8},{10,11... | collective-permute-start | bytes 3145736 | tf_op jit(solution)/shard_map/ppermute | solution.py:502
  49.1 2.0 %collective-permute-start.18 = (bf16[2,128,1024]{2,1,0:T(8,128)(2,1)S(1)}, bf16[2,128,1024]{2,1,0:T(8,128)(2,1)S(1)}, u32[]{:S(2)}, u32[]{:S(2)}) collective-permute-start(bf16[2,128,1024]{2,1,0:T(8,128)(2,1)S(1)} %get-tuple-element.124.refs_4_), channel_id=1, source_target_pairs={{0,1},{1,0},{2,3},{3,2},{4,5},{5,4},{6,7},{7,6},{8,9},{9,8},{10,11... | collective-permute-start | bytes 1572872 | tf_op jit(solution)/shard_map/ppermute | solution.py:502
  55.3 22.1 %collective-permute-start.19 = (bf16[40,2048]{1,0:T(8,128)(2,1)S(1)}, bf16[40,2048]{1,0:T(8,128)(2,1)S(1)}, u32[]{:S(2)}, u32[]{:S(2)}) collective-permute-start(bf16[40,2048]{1,0:T(8,128)(2,1)S(1)} %get-tuple-element.148), channel_id=1, source_target_pairs={{0,8},{2,10},{4,12},{6,14},{8,0},{10,2},{12,4},{14,6},{1,9},{3,11}... | collective-permute-start | bytes 491528 | tf_op jit(solution)/shard_map/ppermute | solution.py:542
  56.0 24.6 %collective-permute-start.20 = (bf16[40,2048]{1,0:T(8,128)(2,1)S(1)}, bf16[40,2048]{1,0:T(8,128)(2,1)S(1)}, u32[]{:S(2)}, u32[]{:S(2)}) collective-permute-start(bf16[40,2048]{1,0:T(8,128)(2,1)S(1)} %get-tuple-element.151), channel_id=1, source_target_pairs={{0,10},{2,8},{4,14},{6,12},{8,2},{10,0},{12,6},{14,4},{1,11},{3,9}... | collective-permute-start | bytes 491528 | tf_op jit(solution)/shard_map/ppermute | solution.py:542
  63.3 19.1 %copy-start.7 = (bf16[1040,128]{1,0:T(8,128)(2,1)S(1)}, bf16[1040,128]{1,0:T(8,128)(2,1)}, u32[]{:S(2)}) copy-start(bf16[1040,128]{1,0:T(8,128)(2,1)} %get-tuple-element.81.top_ref.refs_0_) | copy-start | bytes 798724
  63.3 19.1 %copy-start.9 = (bf16[1040,128]{1,0:T(8,128)(2,1)S(1)}, bf16[1040,128]{1,0:T(8,128)(2,1)}, u32[]{:S(2)}) copy-start(bf16[1040,128]{1,0:T(8,128)(2,1)} %get-tuple-element.82.bottom_ref.refs_1_) | copy-start | bytes 798724
  63.3 19.1 %copy-start.10 = (f32[2048,8]{0,1:T(8,128)S(1)}, f32[2048,8]{0,1:T(8,128)}, u32[]{:S(2)}) copy-start(f32[2048,8]{0,1:T(8,128)} %param.10) | copy-start | bytes 196612
  63.3 19.5 %collective-permute-start.21 = (bf16[40,2048]{1,0:T(8,128)(2,1)S(1)}, bf16[40,2048]{1,0:T(8,128)(2,1)S(1)}, u32[]{:S(2)}, u32[]{:S(2)}) collective-permute-start(bf16[40,2048]{1,0:T(8,128)(2,1)S(1)} %get-tuple-element.152), channel_id=1, source_target_pairs={{0,12},{2,14},{4,8},{6,10},{8,4},{10,6},{12,0},{14,2},{1,13},{3,15... | collective-permute-start | bytes 491528 | tf_op jit(solution)/shard_map/ppermute | solution.py:542
  63.4 19.4 %collective-permute-start.22 = (bf16[40,2048]{1,0:T(8,128)(2,1)S(1)}, bf16[40,2048]{1,0:T(8,128)(2,1)S(1)}, u32[]{:S(2)}, u32[]{:S(2)}) collective-permute-start(bf16[40,2048]{1,0:T(8,128)(2,1)S(1)} %get-tuple-element.153), channel_id=1, source_target_pairs={{0,14},{2,12},{4,10},{6,8},{8,6},{10,4},{12,2},{14,0},{1,15},{3,13... | collective-permute-start | bytes 491528 | tf_op jit(solution)/shard_map/ppermute | solution.py:542
  73.1 10.5 %collective-permute-start.23 = (bf16[40,2048]{1,0:T(8,128)(2,1)S(1)}, bf16[40,2048]{1,0:T(8,128)(2,1)S(1)}, u32[]{:S(2)}, u32[]{:S(2)}) collective-permute-start(bf16[40,2048]{1,0:T(8,128)(2,1)S(1)} %get-tuple-element.154), channel_id=1, source_target_pairs={{0,6},{2,4},{4,2},{6,0},{8,14},{10,12},{12,10},{14,8},{1,7},{3,5},... | collective-permute-start | bytes 491528 | tf_op jit(solution)/shard_map/ppermute | solution.py:542
  77.4 9.9 %collective-permute-start.24 = (bf16[40,2048]{1,0:T(8,128)(2,1)S(1)}, bf16[40,2048]{1,0:T(8,128)(2,1)S(1)}, u32[]{:S(2)}, u32[]{:S(2)}) collective-permute-start(bf16[40,2048]{1,0:T(8,128)(2,1)S(1)} %get-tuple-element.155), channel_id=1, source_target_pairs={{0,4},{2,6},{4,0},{6,2},{8,12},{10,14},{12,8},{14,10},{1,5},{3,7},... | collective-permute-start | bytes 491528 | tf_op jit(solution)/shard_map/ppermute | solution.py:542
  80.6 6.7 %collective-permute-start.25 = (bf16[40,2048]{1,0:T(8,128)(2,1)S(1)}, bf16[40,2048]{1,0:T(8,128)(2,1)S(1)}, u32[]{:S(2)}, u32[]{:S(2)}) collective-permute-start(bf16[40,2048]{1,0:T(8,128)(2,1)S(1)} %get-tuple-element.156), channel_id=1, source_target_pairs={{0,2},{2,0},{4,6},{6,4},{8,10},{10,8},{12,14},{14,12},{1,3},{3,1},... | collective-permute-start | bytes 491528 | tf_op jit(solution)/shard_map/ppermute | solution.py:542
